TPU v7x, 256 devices: a whole 4x4x8 slice. The times are simulated.
256 devices in a mesh: trow: 16 (over z, x_lo), tcol: 16 (over y, x_hi, core).
Axes of the slice: x: 4 (x_hi: 2, x_lo: 2; x = x_hi * 2 + x_lo), y: 4, z: 8, core: 2. Of those that a mesh axis runs over, the one named last changes fastest.
Arguments:
- latent: bfloat16 [128, 512, 1152], P('trow', 'tcol'), may hold values from -6 to 6
- control: bfloat16 [16, 64, 144, 1152], P('trow', 'tcol'), may hold values from -4 to 4
- valid: int32 [16, 64, 144], P('trow', 'tcol'), may hold values from 0 to 1, as said below
- radius: int32 [16], replicated, may hold values from 1 to 5
- modulation: float32 [2, 3, 1152], replicated, may hold values from -3 to 3
- w_qkv: bfloat16 [1152, 3456], replicated, as said below
- w_out: bfloat16 [1152, 1152], replicated, may hold values from -0.1875 to 0.1875
Outputs:
- blended: bfloat16 [128, 512, 1152], P('trow', 'tcol')
Inputs may be any that keep to these rules, and one draw needn't show every extreme that they name: `valid`: for each tile and each of its four sides a band width of 1 or 2 margin tokens is drawn; a token is 1 when its row and its column each lie in the core or in that side's band, and 0 otherwise; margin tokens outside the image are 0; core tokens are always 1. `w_qkv`: entries lie within -72 / sqrt(1152) and 72 / sqrt(1152).
All inputs are finite; a program needn't handle non-finite values.
Results may differ from a plain program's by a relative error of at most 0.009.
The roundings to bfloat16 on the way count: a program that leaves them out, or rounds other values in their place, can miss the bound.
Values may be sent and summed in bfloat16 or wider, within the bound.
No kernel may reach another device: no remote copies, remote signals or barrier semaphores. Data moves between devices by JAX's collectives and lax.ppermute only.
A program may use at most 192 MiB of HBM per device.

v0:
```python
import jax
import jax.numpy as jnp
from jax import lax
from jax.sharding import PartitionSpec as P

D = 1152
HEADS = 16
HEAD_DIM = 72
CORE = 8
MARGIN = 2
TILE_TOK = 144


GUIDE = 4.5


def from_behind(block, axis, distance):
    devices = range(lax.axis_size(axis))
    route = [(i - distance, i) for i in devices if i - distance in devices]
    return lax.ppermute(block, axis, route)


def padded(x, sides, width):
    for axis, dim in sides:
        size, length = (lax.axis_size(axis), x.shape[dim])
        up = [(i, (i + 1) % size) for i in range(size - 1)]
        down = [(j, i) for i, j in up]
        last = lax.slice_in_dim(x, length - width, length, axis=dim)
        first = lax.slice_in_dim(x, 0, width, axis=dim)
        before = lax.ppermute(last, axis, up)
        after = lax.ppermute(first, axis, down)
        x = jnp.concatenate([before, x, after], axis=dim)
    return x


def pad_front(array, before, after):
    widths = [(before, after)] + [(0, 0)] * (array.ndim - 1)
    return jnp.pad(array, widths)


def cut_tiles(grid, axis):
    moved = jnp.moveaxis(grid, axis, 0)
    count = (moved.shape[0] - 2 * MARGIN) // CORE
    rest = moved.shape[1:]
    head = moved[: CORE * count].reshape((count, CORE) + rest)
    tail = pad_front(moved[CORE:], 0, CORE - 2 * MARGIN).reshape((count, CORE) + rest)[
        :, : 2 * MARGIN
    ]
    tiles = jnp.concatenate([head, tail], axis=1)
    return jnp.moveaxis(tiles, (0, 1), (axis, axis + 1))


def place_tiles(tiles, axis):
    moved = jnp.moveaxis(tiles, (axis, axis + 1), (0, 1))
    count = moved.shape[0]
    rest = moved.shape[2:]
    head = pad_front(moved[:, :CORE].reshape((count * CORE,) + rest), 0, 2 * MARGIN)
    tail = jnp.moveaxis(pad_front(jnp.moveaxis(moved[:, CORE:], 1, 0), 0, CORE - 2 * MARGIN), 0, 1)
    tail = pad_front(tail.reshape((count * CORE,) + rest), CORE, 0)[: CORE * count + 2 * MARGIN]
    return jnp.moveaxis(head + tail, 0, axis)


def block_rows(tokens, control, valid, radius, modulation, w_qkv, w_out):
    side = CORE + 2 * MARGIN
    count = tokens.shape[0]
    index = jnp.arange(TILE_TOK, dtype=jnp.int32)
    row_pos = index // side
    col_pos = index % side
    dist = jnp.maximum(
        jnp.abs(row_pos[:, None] - row_pos[None, :]), jnp.abs(col_pos[:, None] - col_pos[None, :])
    )
    near = dist[None] <= radius[:, None, None]
    itself = index[:, None] == index[None, :]
    keyok = (valid[:, None, :] > 0) | itself[None]
    allowed = near[None] & keyok[:, None]
    xf = tokens.astype(jnp.float32)
    mean = jnp.mean(xf, axis=-1, keepdims=True)
    var = jnp.mean((xf - mean) ** 2, axis=-1, keepdims=True)
    normed = (xf - mean) * lax.rsqrt(var + 1e-06)
    hidden = (
        normed[None] * (1.0 + modulation[:, 1][:, None, None]) + modulation[:, 0][:, None, None]
    ).astype(jnp.bfloat16)
    qkv = jnp.einsum("bntd,de->bnte", hidden, w_qkv, preferred_element_type=jnp.float32).astype(
        jnp.bfloat16
    )
    query = qkv[..., :D].reshape(2, count, TILE_TOK, HEADS, HEAD_DIM)
    keys = qkv[..., D : 2 * D].reshape(2, count, TILE_TOK, HEADS, HEAD_DIM)
    values = qkv[..., 2 * D :].reshape(2, count, TILE_TOK, HEADS, HEAD_DIM)
    scores = jnp.einsum(
        "bnqhd,bnkhd->bnhqk", query, keys, preferred_element_type=jnp.float32
    ) / jnp.sqrt(jnp.float32(HEAD_DIM))
    scores = jnp.where(allowed[None], scores, jnp.float32(-1e30))
    top = jnp.max(scores, axis=-1, keepdims=True)
    expo = jnp.exp(scores - top)
    probs = (expo / jnp.sum(expo, axis=-1, keepdims=True)).astype(jnp.bfloat16)
    attn = jnp.einsum(
        "bnhqk,bnkhd->bnqhd", probs, values, preferred_element_type=jnp.float32
    ).astype(jnp.bfloat16)
    attn = attn.reshape(2, count, TILE_TOK, D)
    projected = jnp.einsum("bntd,de->bnte", attn, w_out, preferred_element_type=jnp.float32)
    return (
        xf[None] + modulation[:, 2][:, None, None] * projected + control.astype(jnp.float32)[None]
    )


def spread_margins(sums, counts):
    rows = sums.shape[0] - 2 * MARGIN
    north_sum, north_count = (
        from_behind(sums[rows + MARGIN :].astype(jnp.bfloat16), "trow", 1).astype(jnp.float32),
        from_behind(counts[rows + MARGIN :].astype(jnp.bfloat16), "trow", 1).astype(jnp.float32),
    )
    south_sum, south_count = (
        from_behind(sums[:MARGIN].astype(jnp.bfloat16), "trow", -1).astype(jnp.float32),
        from_behind(counts[:MARGIN].astype(jnp.bfloat16), "trow", -1).astype(jnp.float32),
    )
    mid_sum = (
        sums[MARGIN : MARGIN + rows].at[:MARGIN].add(north_sum).at[rows - MARGIN :].add(south_sum)
    )
    mid_count = (
        counts[MARGIN : MARGIN + rows]
        .at[:MARGIN]
        .add(north_count)
        .at[rows - MARGIN :]
        .add(south_count)
    )
    cols = sums.shape[1] - 2 * MARGIN
    west_sum, west_count = (
        from_behind(mid_sum[:, cols + MARGIN :].astype(jnp.bfloat16), "tcol", 1).astype(
            jnp.float32
        ),
        from_behind(mid_count[:, cols + MARGIN :].astype(jnp.bfloat16), "tcol", 1).astype(
            jnp.float32
        ),
    )
    east_sum, east_count = (
        from_behind(mid_sum[:, :MARGIN].astype(jnp.bfloat16), "tcol", -1).astype(jnp.float32),
        from_behind(mid_count[:, :MARGIN].astype(jnp.bfloat16), "tcol", -1).astype(jnp.float32),
    )
    core_sum = (
        mid_sum[:, MARGIN : MARGIN + cols]
        .at[:, :MARGIN]
        .add(west_sum)
        .at[:, cols - MARGIN :]
        .add(east_sum)
    )
    core_count = (
        mid_count[:, MARGIN : MARGIN + cols]
        .at[:, :MARGIN]
        .add(west_count)
        .at[:, cols - MARGIN :]
        .add(east_count)
    )
    return (core_sum, core_count)


def local(latent, control, valid, radius, modulation, w_qkv, w_out):
    side = CORE + 2 * MARGIN
    extended = padded(latent, (("trow", 0), ("tcol", 1)), MARGIN)
    tiles = cut_tiles(cut_tiles(extended, 0), 2)
    tile_r = tiles.shape[0]
    tile_c = tiles.shape[2]
    count = tile_r * tile_c
    tok = tiles.transpose(0, 2, 1, 3, 4).reshape(count, TILE_TOK, D)
    flat_valid = valid.reshape(count, TILE_TOK)
    branch_out = block_rows(
        tok, control.reshape(count, TILE_TOK, D), flat_valid, radius, modulation, w_qkv, w_out
    )
    weight = flat_valid.astype(jnp.float32)
    counts = place_tiles(
        place_tiles(weight.reshape(tile_r, tile_c, side, side).transpose(0, 2, 1, 3), 0), 1
    )
    guided = (branch_out[1] + GUIDE * (branch_out[0] - branch_out[1])) * weight[..., None]
    terms = guided.reshape(tile_r, tile_c, side, side, D).transpose(0, 2, 1, 3, 4)
    sums = place_tiles(place_tiles(terms, 0), 1)
    core_sum, core_count = spread_margins(sums, counts)
    blended = core_sum / core_count[..., None]
    return blended.astype(jnp.bfloat16)


def solution(mesh):
    placed = (
        P("trow", "tcol", None),
        P("trow", "tcol", None, None),
        P("trow", "tcol", None),
        P(),
        P(),
        P(),
        P(),
    )
    return jax.shard_map(
        local, mesh=mesh, in_specs=placed, out_specs=P("trow", "tcol", None), check_vma=False
    )
```

profile of v0, /device:TPU:103, one launch (start us, length us, event | category | flops | bytes accessed | tf_op | source)
XLA Modules:
  0.0 202.8 jit_solution(13352662634704397476)
XLA Ops:
  0.0 1.9 fusion.44
  1.9 5.0 %collective-permute-start = (bf16[2,32,1152]{2,1,0:T(8,128)(2,1)}, bf16[2,32,1152]{2,1,0:T(8,128)(2,1)}, u32[]{:S(2)}, u32[]{:S(2)}) collective-permute-start(bf16[2,32,1152]{2,1,0:T(8,128)(2,1)} %get-tuple-element.117), channel_id=1, source_target_pairs={{0,16},{16,32},{32,48},{48,64},{64,80},{80,96},{96,112},{112,128},... | collective-permute-start | bytes 442376 | tf_op jit(solution)/shard_map/ppermute | solution.py:30
  6.9 1.9 collective-permute-start.1
  10.6 5.5 %collective-permute-start.8 = (bf16[2,36]{0,1:T(8,128)(2,1)}, bf16[2,36]{0,1:T(8,128)(2,1)}, u32[]{:S(2)}, u32[]{:S(2)}) collective-permute-start(bf16[2,36]{0,1:T(8,128)(2,1)} %get-tuple-element.124), channel_id=1, source_target_pairs={{0,16},{16,32},{32,48},{48,64},{64,80},{80,96},{96,112},{112,128},... | collective-permute-start | bytes 440 | tf_op jit(solution)/shard_map/ppermute | solution.py:20
  16.1 1.9 collective-permute-start.9
  20.0 1.3 slice_bitcast_fusion.8
  21.4 3.0 %bitcast_convert_fusion = f32[4,144,1152]{2,1,0:T(8,128)} fusion(bf16[1,4,144,1152]{3,2,1,0:T(8,128)(2,1)} %param.24), kind=kLoop, calls=%fused_computation.43 | loop fusion | flops 663552 | bytes 3981312 | tf_op jit(solution)/shard_map/add | solution.py:102
  24.4 1.0 copy.97
  25.9 0.9 broadcast_or_fusion
  26.8 2.4 %broadcast_and_fusion = pred[4,16,144,144]{2,3,1,0:T(8,128)(4,1)} fusion(pred[4,144,144]{1,2,0:T(8,128)(4,1)S(1)} %broadcast_or_fusion, pred[16,144,144]{1,2,0:T(8,128)(4,1)S(1)} %broadcast_compare_fusion), kind=kLoop, calls=%fused_computation.17 | loop fusion | flops 1327104 | bytes 1741824 | tf_op jit(solution)/shard_map/and | solution.py:75
  29.9 1.4 slice_add_fusion.5
  31.3 0.8 scatter-add.34
  32.2 0.8 slice_add_fusion.4
  33.3 0.9 constant_dynamic-update-slice_fusion.2
  34.5 5.2 %collective-permute-start.2 = (bf16[12,2,1152]{2,1,0:T(2,128)(2,1)S(1)}, bf16[12,2,1152]{2,1,0:T(2,128)(2,1)S(1)}, u32[]{:S(2)}, u32[]{:S(2)}) collective-permute-start(bf16[12,2,1152]{2,1,0:T(2,128)(2,1)S(1)} %get-tuple-element.112), channel_id=1, source_target_pairs={{0,1},{1,2},{2,3},{3,4},{4,5},{5,6},{6,7},{7,8},{8,9},{9,10},{10,1... | collective-permute-start | bytes 165896 | tf_op jit(solution)/shard_map/ppermute | solution.py:30
  39.6 1.9 collective-permute-start.3
  42.7 6.0 %collective-permute-start.10 = (bf16[8,2]{0,1:T(2,128)(2,1)}, bf16[8,2]{0,1:T(2,128)(2,1)}, u32[]{:S(2)}, u32[]{:S(2)}) collective-permute-start(bf16[8,2]{0,1:T(2,128)(2,1)} %get-tuple-element.122), channel_id=1, source_target_pairs={{0,1},{1,2},{2,3},{3,4},{4,5},{5,6},{6,7},{7,8},{8,9},{9,10},{10,1... | collective-permute-start | bytes 104 | tf_op jit(solution)/shard_map/ppermute | solution.py:20
  48.7 1.9 collective-permute-start.11
  52.4 0.8 bitcast_reduce_fusion
  53.1 2.3 %maximum_convert_fusion = f32[4,12,1,12,1152]{4,0,1,3,2:T(4,128)} fusion(bf16[4,4,1,12,1152]{4,0,1,3,2:T(4,128)(2,1)S(1)} %copy.108, bf16[4,8,1,12,1152]{4,0,1,3,2:T(4,128)(2,1)S(1)} %copy.80), kind=kLoop, calls=%fused_computation.42 | loop fusion | flops 1327104 | bytes 3981312 | tf_op jit(solution)/shard_map/convert_element_type | solution.py:76
  55.5 1.5 fusion.19
  57.0 2.3 %subtract_multiply_fusion = f32[4,144,1152]{2,0,1:T(4,128)S(1)} fusion(f32[4,144]{0,1:T(8,128)S(1)} %reshape.506, f32[4,144]{0,1:T(8,128)S(1)} %reshape.507, f32[4,12,1,12,1152]{4,0,1,3,2:T(4,128)} %maximum_convert_fusion), kind=kLoop, calls=%fused_computation.31 | loop fusion | flops 1327104 | bytes 5313024 | tf_op jit(solution)/shard_map/mul | solution.py:79
  60.1 13.3 %fusion.8 = bf16[2,4,144,3456]{3,2,1,0:T(8,128)(2,1)S(1)} fusion(bf16[1152,3456]{1,0:T(8,128)(2,1)} %param.28, f32[2,1152]{1,0:T(2,128)S(1)} %copy-done.7, f32[2,1152]{1,0:T(2,128)S(1)} %copy-done.8, f32[4,144,1152]{2,1,0:T(8,128)S(1)} %copy.89), kind=kOutput, calls=%fused_computation.11 | convolution fusion | flops 9180905472 | bytes 18597888 | tf_op jit(solution)/shard_map/bntd,de->bnte/dot_general | solution.py:83
  73.4 3.4 %fusion.39 = (bf16[2,4,144,1152]{3,2,1,0:T(8,128)(2,1)}, bf16[2,4,144,1152]{3,2,1,0:T(8,128)(2,1)}, bf16[2,4,144,1152]{3,2,1,0:T(8,128)(2,1)}) fusion(bf16[2,4,144,3456]{3,2,1,0:T(8,128)(2,1)S(1)} %fusion.8), kind=kLoop, calls=%fused_computation.101 | loop fusion | bytes 15925248 | tf_op jit(solution)/shard_map/slice | solution.py:86
  76.8 10.6 %reshape.493 = bf16[2,4,144,16,72]{4,3,2,1,0:T(8,128)(2,1)} reshape(bf16[2,4,144,1152]{3,2,1,0:T(8,128)(2,1)} %get-tuple-element.105) | data formatting | bytes 5308416 | tf_op jit(solution)/shard_map/reshape | solution.py:86
  87.4 10.6 %reshape.494 = bf16[2,4,144,16,72]{4,3,2,1,0:T(8,128)(2,1)} reshape(bf16[2,4,144,1152]{3,2,1,0:T(8,128)(2,1)} %get-tuple-element.106) | data formatting | bytes 5308416 | tf_op jit(solution)/shard_map/reshape | solution.py:87
  98.1 6.0 %copy.107 = bf16[2,4,144,1152]{2,3,1,0:T(8,128)(2,1)} copy(bf16[2,4,144,1152]{3,2,1,0:T(8,128)(2,1)} %get-tuple-element.107) | data formatting | bytes 5308416 | tf_op jit(solution)/shard_map/reshape | solution.py:88
  104.1 3.4 %copy.81 = f32[4,144,1152]{2,1,0:T(8,128)} copy(f32[4,144,1152]{2,0,1:T(4,128)} %bitcast.99) | data formatting | bytes 5308416 | tf_op jit(solution)/shard_map/convert_element_type | solution.py:76
  107.5 13.0 %fusion.11 = f32[2,4,16,144,144]{3,4,2,1,0:T(8,128)} fusion(bf16[2,4,144,16,72]{4,3,2,1,0:T(8,128)(2,1)} %reshape.494, bf16[2,4,144,16,72]{4,3,2,1,0:T(8,128)(2,1)} %reshape.493), kind=kOutput, calls=%fused_computation.14 | convolution fusion | flops 382205952 | bytes 15925248 | tf_op jit(solution)/shard_map/bnqhd,bnkhd->bnhqk/dot_general | solution.py:89
  120.5 20.9 %fusion.47 = (f32[2,4,16,144]{3,2,1,0:T(8,128)}, f32[2,4,16,144,144]{3,4,2,1,0:T(8,128)}) fusion(f32[2,4,16,144,144]{3,4,2,1,0:T(8,128)} %fusion.11, pred[4,16,144,144]{2,3,1,0:T(8,128)(4,1)S(1)} %copy-done.3), kind=kOutput, calls=%fused_computation.109 | output fusion | flops 15925391 | bytes 22634496 | tf_op jit(solution)/shard_map/sub | solution.py:94
  141.4 11.7 %fusion.14 = bf16[2,4,16,72,144]{4,3,2,1,0:T(8,128)(2,1)} fusion(bf16[2,4,144,16,72]{2,4,3,1,0:T(8,128)(2,1)} %bitcast.104, f32[2,4,16,144,144]{3,4,2,1,0:T(8,128)} %get-tuple-element.126, f32[2,4,16,144]{3,2,1,0:T(8,128)} %get-tuple-element.125), kind=kOutput, calls=%fused_computation.19 | convolution fusion | flops 388841472 | bytes 15998976 | tf_op jit(solution)/shard_map/bnhqk,bnkhd->bnqhd/dot_general | solution.py:96
  153.1 7.3 %add_add_fusion = f32[2,4,144,1152]{3,2,1,0:T(8,128)S(1)} fusion(bf16[2,4,144,1152]{2,3,1,0:T(8,128)(2,1)} %bitcast.110, bf16[1152,1152]{1,0:T(8,128)(2,1)S(1)} %copy-done, f32[4,144,1152]{2,1,0:T(8,128)} %bitcast_convert_fusion, f32[2,1152]{1,0:T(2,128)S(1)} %copy-done.6, f32[4,144,1152]{2,1,0:T(8,128)} %copy.81), kind=kOutput, calls=%fused_computation.12 | convolution fusion | flops 3061628928 | bytes 15934464 | tf_op jit(solution)/shard_map/bntd,de->bnte/dot_general | solution.py:100
  160.7 1.0 copy.95
  161.7 1.0 copy.96
  162.8 0.9 multiply_bitcast_fusion
  164.6 1.4 copy-done.2
  166.5 1.3 slice-done
  168.2 5.2 %collective-permute-start.4 = (bf16[2,36,1152]{2,1,0:T(8,128)(2,1)S(1)}, bf16[2,36,1152]{2,1,0:T(8,128)(2,1)S(1)}, u32[]{:S(2)}, u32[]{:S(2)}) collective-permute-start(bf16[2,36,1152]{2,1,0:T(8,128)(2,1)S(1)} %get-tuple-element.111), channel_id=1, source_target_pairs={{0,16},{16,32},{32,48},{48,64},{64,80},{80,96},{96,112},{112,128},... | collective-permute-start | bytes 497672 | tf_op jit(solution)/shard_map/ppermute | solution.py:20
  173.4 1.2 constant_dynamic-update-slice_fusion.4
  174.7 1.9 collective-permute-start.5
  176.6 6.4 %collective-permute-done.5 = bf16[2,36,1152]{2,1,0:T(8,128)(2,1)S(1)} collective-permute-done((bf16[2,36,1152]{2,1,0:T(8,128)(2,1)S(1)}, bf16[2,36,1152]{2,1,0:T(8,128)(2,1)S(1)}, u32[]{:S(2)}, u32[]{:S(2)}) %collective-permute-start.5) | collective-permute-done | bytes 165920 | tf_op jit(solution)/shard_map/ppermute | solution.py:20
  183.1 1.1 copy-done.1
  184.4 8.1 %collective-permute-start.6 = (bf16[8,2,1152]{2,1,0:T(2,128)(2,1)S(1)}, bf16[8,2,1152]{2,1,0:T(2,128)(2,1)S(1)}, u32[]{:S(2)}, u32[]{:S(2)}) collective-permute-start(bf16[8,2,1152]{2,1,0:T(2,128)(2,1)S(1)} %get-tuple-element.115), channel_id=1, source_target_pairs={{0,1},{1,2},{2,3},{3,4},{4,5},{5,6},{6,7},{7,8},{8,9},{9,10},{10,1... | collective-permute-start | bytes 110600 | tf_op jit(solution)/shard_map/ppermute | solution.py:20
  192.6 1.5 slice.382
  194.1 1.9 collective-permute-start.7
  196.0 1.0 fusion.32
  197.0 4.7 %collective-permute-done.7 = bf16[8,2,1152]{2,1,0:T(2,128)(2,1)S(1)} collective-permute-done((bf16[8,2,1152]{2,1,0:T(2,128)(2,1)S(1)}, bf16[8,2,1152]{2,1,0:T(2,128)(2,1)S(1)}, u32[]{:S(2)}, u32[]{:S(2)}) %collective-permute-start.7) | collective-permute-done | bytes 36896 | tf_op jit(solution)/shard_map/ppermute | solution.py:20
  201.9 1.0 divide_convert_fusion.4
  (91 shorter events, 11.6 us)
Async XLA Ops:
  0.0 153.1 %copy-start = (bf16[1152,1152]{1,0:T(8,128)(2,1)S(1)}, bf16[1152,1152]{1,0:T(8,128)(2,1)}, u32[]{:S(2)}) copy-start(bf16[1152,1152]{1,0:T(8,128)(2,1)} %param.29) | copy-start | bytes 7962628
  0.0 25.5 %copy-start.9 = (s32[16]{0:T(128)S(1)}, s32[16]{0:T(128)}, u32[]{:S(2)}) copy-start(s32[16]{0:T(128)} %param.26) | copy-start | bytes 196
  1.9 31.4 %collective-permute-start = (bf16[2,32,1152]{2,1,0:T(8,128)(2,1)}, bf16[2,32,1152]{2,1,0:T(8,128)(2,1)}, u32[]{:S(2)}, u32[]{:S(2)}) collective-permute-start(bf16[2,32,1152]{2,1,0:T(8,128)(2,1)} %get-tuple-element.117), channel_id=1, source_target_pairs={{0,16},{16,32},{32,48},{48,64},{64,80},{80,96},{96,112},{112,128},... | collective-permute-start | bytes 442376 | tf_op jit(solution)/shard_map/ppermute | solution.py:30
  6.9 27.4 %collective-permute-start.1 = (bf16[2,32,1152]{2,1,0:T(8,128)(2,1)}, bf16[2,32,1152]{2,1,0:T(8,128)(2,1)S(1)}, u32[]{:S(2)}, u32[]{:S(2)}) collective-permute-start(bf16[2,32,1152]{2,1,0:T(8,128)(2,1)} %get-tuple-element.116), channel_id=1, source_target_pairs={{16,0},{32,16},{48,32},{64,48},{80,64},{96,80},{112,96},{128,112},... | collective-permute-start | bytes 442376 | tf_op jit(solution)/shard_map/ppermute | solution.py:31
  10.6 19.3 %collective-permute-start.8 = (bf16[2,36]{0,1:T(8,128)(2,1)}, bf16[2,36]{0,1:T(8,128)(2,1)}, u32[]{:S(2)}, u32[]{:S(2)}) collective-permute-start(bf16[2,36]{0,1:T(8,128)(2,1)} %get-tuple-element.124), channel_id=1, source_target_pairs={{0,16},{16,32},{32,48},{48,64},{64,80},{80,96},{96,112},{112,128},... | collective-permute-start | bytes 440 | tf_op jit(solution)/shard_map/ppermute | solution.py:20
  16.1 16.1 %collective-permute-start.9 = (bf16[2,36]{0,1:T(8,128)(2,1)S(1)}, bf16[2,36]{0,1:T(8,128)(2,1)}, u32[]{:S(2)}, u32[]{:S(2)}) collective-permute-start(bf16[2,36]{0,1:T(8,128)(2,1)S(1)} %get-tuple-element.123), channel_id=1, source_target_pairs={{16,0},{32,16},{48,32},{64,48},{80,64},{96,80},{112,96},{128,112},... | collective-permute-start | bytes 440 | tf_op jit(solution)/shard_map/ppermute | solution.py:20
  24.4 9.9 %copy-start.4 = (bf16[8,32,1152]{2,1,0:T(8,128)(2,1)S(1)}, bf16[8,32,1152]{2,1,0:T(8,128)(2,1)}, u32[]{:S(2)}) copy-start(bf16[8,32,1152]{2,1,0:T(8,128)(2,1)} %param.23) | copy-start | bytes 1769476
  34.5 16.2 %collective-permute-start.2 = (bf16[12,2,1152]{2,1,0:T(2,128)(2,1)S(1)}, bf16[12,2,1152]{2,1,0:T(2,128)(2,1)S(1)}, u32[]{:S(2)}, u32[]{:S(2)}) collective-permute-start(bf16[12,2,1152]{2,1,0:T(2,128)(2,1)S(1)} %get-tuple-element.112), channel_id=1, source_target_pairs={{0,1},{1,2},{2,3},{3,4},{4,5},{5,6},{6,7},{7,8},{8,9},{9,10},{10,1... | collective-permute-start | bytes 165896 | tf_op jit(solution)/shard_map/ppermute | solution.py:30
  39.6 11.0 %collective-permute-start.3 = (bf16[12,2,1152]{2,1,0:T(2,128)(2,1)S(1)}, bf16[12,2,1152]{2,1,0:T(2,128)(2,1)S(1)}, u32[]{:S(2)}, u32[]{:S(2)}) collective-permute-start(bf16[12,2,1152]{2,1,0:T(2,128)(2,1)S(1)} %get-tuple-element.113), channel_id=1, source_target_pairs={{1,0},{2,1},{3,2},{4,3},{5,4},{6,5},{7,6},{8,7},{9,8},{10,9},{11,1... | collective-permute-start | bytes 165896 | tf_op jit(solution)/shard_map/ppermute | solution.py:31
  42.7 130.7 %collective-permute-start.10 = (bf16[8,2]{0,1:T(2,128)(2,1)}, bf16[8,2]{0,1:T(2,128)(2,1)}, u32[]{:S(2)}, u32[]{:S(2)}) collective-permute-start(bf16[8,2]{0,1:T(2,128)(2,1)} %get-tuple-element.122), channel_id=1, source_target_pairs={{0,1},{1,2},{2,3},{3,4},{4,5},{5,6},{6,7},{7,8},{8,9},{9,10},{10,1... | collective-permute-start | bytes 104 | tf_op jit(solution)/shard_map/ppermute | solution.py:20
  48.7 143.8 %collective-permute-start.11 = (bf16[8,2]{0,1:T(2,128)(2,1)S(1)}, bf16[8,2]{0,1:T(2,128)(2,1)S(1)}, u32[]{:S(2)}, u32[]{:S(2)}) collective-permute-start(bf16[8,2]{0,1:T(2,128)(2,1)S(1)} %get-tuple-element.121), channel_id=1, source_target_pairs={{1,0},{2,1},{3,2},{4,3},{5,4},{6,5},{7,6},{8,7},{9,8},{10,9},{11,1... | collective-permute-start | bytes 104 | tf_op jit(solution)/shard_map/ppermute | solution.py:20
  59.3 0.7 copy-start.7
  59.3 0.7 copy-start.8
  107.5 13.0 %copy-start.3 = (pred[4,16,144,144]{2,3,1,0:T(8,128)(4,1)S(1)}, pred[4,16,144,144]{2,3,1,0:T(8,128)(4,1)}, u32[]{:S(2)}) copy-start(pred[4,16,144,144]{2,3,1,0:T(8,128)(4,1)} %broadcast_and_fusion) | copy-start | bytes 3981316
  141.4 11.7 %copy-start.6 = (f32[2,1152]{1,0:T(2,128)S(1)}, f32[2,1152]{1,0:T(2,128)}, u32[]{:S(2)}) copy-start(f32[2,1152]{1,0:T(2,128)} %get-tuple-element.118) | copy-start | bytes 27652
  164.5 1.5 copy-start.2
  166.3 1.5 slice-start
  167.9 5.5 %copy-start.5 = (f32[8,32]{0,1:T(8,128)S(1)}, f32[8,32]{0,1:T(8,128)}, u32[]{:S(2)}) copy-start(f32[8,32]{0,1:T(8,128)} %slice.396) | copy-start | bytes 3076
  168.2 8.4 %collective-permute-start.4 = (bf16[2,36,1152]{2,1,0:T(8,128)(2,1)S(1)}, bf16[2,36,1152]{2,1,0:T(8,128)(2,1)S(1)}, u32[]{:S(2)}, u32[]{:S(2)}) collective-permute-start(bf16[2,36,1152]{2,1,0:T(8,128)(2,1)S(1)} %get-tuple-element.111), channel_id=1, source_target_pairs={{0,16},{16,32},{32,48},{48,64},{64,80},{80,96},{96,112},{112,128},... | collective-permute-start | bytes 497672 | tf_op jit(solution)/shard_map/ppermute | solution.py:20
  174.7 8.4 %collective-permute-start.5 = (bf16[2,36,1152]{2,1,0:T(8,128)(2,1)S(1)}, bf16[2,36,1152]{2,1,0:T(8,128)(2,1)S(1)}, u32[]{:S(2)}, u32[]{:S(2)}) collective-permute-start(bf16[2,36,1152]{2,1,0:T(8,128)(2,1)S(1)} %get-tuple-element.110), channel_id=1, source_target_pairs={{16,0},{32,16},{48,32},{64,48},{80,64},{96,80},{112,96},{128,112},... | collective-permute-start | bytes 497672 | tf_op jit(solution)/shard_map/ppermute | solution.py:20
  183.1 1.1 copy-start.1
  184.4 11.6 %collective-permute-start.6 = (bf16[8,2,1152]{2,1,0:T(2,128)(2,1)S(1)}, bf16[8,2,1152]{2,1,0:T(2,128)(2,1)S(1)}, u32[]{:S(2)}, u32[]{:S(2)}) collective-permute-start(bf16[8,2,1152]{2,1,0:T(2,128)(2,1)S(1)} %get-tuple-element.115), channel_id=1, source_target_pairs={{0,1},{1,2},{2,3},{3,4},{4,5},{5,6},{6,7},{7,8},{8,9},{9,10},{10,1... | collective-permute-start | bytes 110600 | tf_op jit(solution)/shard_map/ppermute | solution.py:20
  194.1 7.7 %collective-permute-start.7 = (bf16[8,2,1152]{2,1,0:T(2,128)(2,1)S(1)}, bf16[8,2,1152]{2,1,0:T(2,128)(2,1)S(1)}, u32[]{:S(2)}, u32[]{:S(2)}) collective-permute-start(bf16[8,2,1152]{2,1,0:T(2,128)(2,1)S(1)} %get-tuple-element.114), channel_id=1, source_target_pairs={{1,0},{2,1},{3,2},{4,3},{5,4},{6,5},{7,6},{8,7},{9,8},{10,9},{11,1... | collective-permute-start | bytes 110600 | tf_op jit(solution)/shard_map/ppermute | solution.py:20
where the time goes:
time: 204 us; the launch traced here: 203 us
  local copies, waits for them, and re-layouts  52.8 us (26%)
  other arithmetic  46.5 us (23%)
  starting transfers between devices  46.4 us (23%)
  matrix products  45.3 us (22%)
  waiting for transfers between devices  11.1 us (5%)
    ppermute x8, starting transfers between devices, from_behind(): return lax.ppermute(block, axis, route)  32.4 us
    sub x1, other arithmetic, block_rows(): expo = jnp.exp(scores - top)  20.9 us
    dot_general x1, matrix products, block_rows(): jnp.einsum('bntd,de->bnte', hidden, w_qkv, preferred_element_type=jnp.flo...  13.3 us
    dot_general x1, matrix products, block_rows(): jnp.einsum('bnqhd,bnkhd->bnhqk', query, keys, preferred_element_type=jnp....  13 us
    dot_general x1, matrix products, block_rows(): jnp.einsum('bnhqk,bnkhd->bnqhd', probs, values, preferred_element_type=jn...  11.7 us
    ppermute x8, waiting for transfers between devices, from_behind(): return lax.ppermute(block, axis, route)  11.1 us
    reshape x1, local copies, waits for them, and re-layouts, block_rows(): query = qkv[..., :D].reshape(2, count, TILE_TOK, HEADS, HEAD_DIM)  10.6 us
    reshape x1, local copies, waits for them, and re-layouts, block_rows(): keys = qkv[..., D:2 * D].reshape(2, count, TILE_TOK, HEADS, HEAD_DIM)  10.6 us
  transfers between devices with their start and end apart: 12, of which 2 were waited for; matrix products, arithmetic and copies ran while one was open for 68% of the time, Pallas kernels for 0%

commit v1 on v0

v1 whole, which is shorter than its diff:
```python
import functools

import jax
import jax.numpy as jnp
import numpy as np
from jax import lax
from jax.experimental import pallas as pl
from jax.experimental.pallas import tpu as pltpu
from jax.sharding import PartitionSpec as P

D = 1152
HEADS = 16
HEAD_DIM = 72
CORE = 8
MARGIN = 2
SIDE = 12
TILE_TOK = 144
GUIDE = 4.5
REACH = 5
FAR = 99.0
BF = jnp.bfloat16
F32 = jnp.float32
EXP_SCALE = float(np.log2(np.e) / np.sqrt(72.0))
VMEM = 56 * 1024 * 1024

JR = np.array([j // 4 if j < 32 else (j - 40) // 4 if j < 40 else 8 + (j - 40) // 4 for j in range(48)])
JC = np.arange(48) % 4


def one_hot(rows, depth):
    hot = np.zeros((len(rows), depth), np.float32)
    for i, src in enumerate(rows):
        if src is not None and src >= 0:
            hot[i, src] = 1.0
    return hot


def source(row, col):
    if col < 0:
        return 384 + (row + 2) * REACH + col + REACH if col >= -REACH else None
    if col >= 32:
        return 480 + (row + 2) * REACH + col - 32 if col < 32 + REACH else None
    if row < 0:
        return 256 + (row + 2) * 32 + col
    if row >= 8:
        return 320 + (row - 8) * 32 + col
    return row * 32 + col


def kv_cols(block):
    return 4 * block - 2 + JC


def slots(block):
    cols = kv_cols(block)
    if block == 0:
        return [(0, [(-1, c) if c < 2 else (0, c - 2) for c in JC])]
    if block == 8:
        return [(3, [(3, 30 + c) if c < 2 else (4, 28 + c) for c in JC])]
    if block % 2:
        return [((block - 1) // 2, [((block - 1) // 2, c) for c in cols])]
    return [(block // 2 - 1, [(block // 2 - 1, c) for c in cols]), (block // 2, [(block // 2, c) for c in cols])]


def unit_queries(unit):
    out = []
    for block in range(2 * unit, 2 * unit + 3):
        pairs = dict(slots(block))[unit]
        out += [(int(tile), int(JR[j]), int(pairs[j][1])) for j in range(48)]
    return out


def window_keys(first, count):
    keys = [(int(JR[j]), int(kv_cols(b)[j])) for b in range(first, first + count) for j in range(48)] if False else []
    for b in range(first, first + count):
        cols = kv_cols(b)
        keys += [(int(JR[j]), int(cols[j])) for j in range(48)]
    return keys + [None] * (256 - len(keys))


def unit_queries(unit):
    out = []
    for block in range(2 * unit, 2 * unit + 3):
        pairs = dict(slots(block))[unit]
        out += [(int(pairs[j][0]), int(JR[j]), int(pairs[j][1])) for j in range(48)]
    return out


def tile_token(tile, row, col):
    r, c = row + 2, col - 8 * tile + 2
    return r * SIDE + c if 0 <= r < SIDE and 0 <= c < SIDE else None


def distances(queries, keys):
    dist = np.full((len(queries), 256), FAR, np.float32)
    for i, (tile, row, col) in enumerate(queries):
        for k, key in enumerate(keys):
            if key is not None and tile_token(tile, *key) is not None:
                if -REACH <= key[1] < 32 + REACH:
                    dist[i, k] = max(abs(row - key[0]), abs(col - key[1]))
    return dist


def key_map(tile, keys):
    return one_hot([None if key is None else tile_token(tile, *key) for key in keys], TILE_TOK).T


def query_map(unit, tile):
    return one_hot([tile_token(t, r, c) if t == tile else None for t, r, c in unit_queries(unit)], TILE_TOK)


@functools.cache
def tables():
    bf = lambda a: np.asarray(a, jnp.bfloat16)
    own = lambda b: [(int(JR[j]), int(kv_cols(b)[j])) for j in range(32)]
    rim = lambda b: [(int(JR[j]), int(kv_cols(b)[j])) for j in range(32, 48)]
    every = lambda b: [(int(JR[j]), int(kv_cols(b)[j])) for j in range(48)]
    t = {}
    t["own"] = bf(one_hot([source(*p) for b in range(1, 8) for p in own(b)], 256))
    t["rim"] = bf(one_hot([source(*p) - 256 for b in range(1, 8) for p in rim(b)], 128))
    dup = [(r, c) for _, r, c in unit_queries(0)[:48]] + [(r, c) for _, r, c in unit_queries(3)[96:]]
    edge = [p for b in (-1, 0, 8, 9) for p in every(b)] + dup
    t["edge"] = bf(one_hot([source(*p) for p in edge], 576))
    slot_pos = []
    for b in range(9):
        unit = min(b // 2, 3)
        slot_pos.append(unit_queries(unit)[(b - 2 * unit) * 48 : (b - 2 * unit + 1) * 48])
    t["x_core"] = bf(one_hot([source(r, c) for q in slot_pos for _, r, c in q[:32]], 256))
    t["x_rim"] = bf(one_hot([source(r, c) - 256 for q in slot_pos for _, r, c in q[32:]], 128))
    mid, west, east = window_keys(2, 5), window_keys(-1, 4), window_keys(6, 4)
    t["dist_mid"] = bf(distances(unit_queries(1) + unit_queries(2), mid))
    t["dist_side"] = bf(np.stack([distances(unit_queries(0), west), distances(unit_queries(3), east)]))
    t["key_mid"] = bf(np.stack([key_map(1, mid), key_map(2, mid)]))
    t["key_side"] = bf(np.stack([key_map(0, west), key_map(-1, west), key_map(3, east), key_map(4, east)]))
    t["query"] = bf(np.stack([query_map(u, u) for u in range(4)]))
    t["query_side"] = bf(np.stack([query_map(0, -1), query_map(3, 4)]))
    send = np.zeros((2, 64, 384), np.float32)
    ctl = np.zeros((2, 32, TILE_TOK), np.float32)
    for r in range(SIDE):
        for k in range(REACH):
            send[0, r * REACH + k, source(r - 2, k)] = 1.0
            send[1, r * REACH + k, source(r - 2, 32 - REACH + k)] = 1.0
        for k in range(2):
            ctl[0, r * 2 + k, r * SIDE + k] = 1.0
            ctl[1, r * 2 + k, r * SIDE + 10 + k] = 1.0
    t["send_own"], t["send_rim"] = bf(send[:, :, :256]), bf(send[:, :, 256:])
    t["send_ctl"] = bf(ctl)
    t["valid_pad"] = bf(np.eye(TILE_TOK, 256))
    put = np.zeros((2, 48, 32), np.float32)
    for j in range(48):
        if JC[j] < 2:
            put[0, j, (JR[j] + 2) * 2 + JC[j]] = 1.0
        else:
            put[1, j, (JR[j] + 2) * 2 + JC[j] - 2] = 1.0
    t["put_ctl"] = bf(put)
    back = np.zeros((256, 288), np.float32)
    for b in range(9):
        for j in range(32):
            if (b == 0 and JC[j] < 2) or (b == 8 and JC[j] >= 2):
                continue
            _, r, c = slot_pos[b][j]
            back[r * 32 + c, b * 32 + j] = 1.0
    assert (back.sum(1) == 1).all()
    t["back"] = bf(back)
    return t


def holders(block):
    out = []
    if block % 2 == 0 and block > 0:
        out.append((block // 2 - 1, 2))
    if block % 2 == 0 and block < 8:
        out.append((block // 2, 0))
    if block % 2:
        out.append(((block - 1) // 2, 1))
    return out


def dot(a, b):
    return jnp.dot(a, b, preferred_element_type=F32)


def dot_nt(a, b):
    return lax.dot_general(a, b, (((1,), (1,)), ((), ())), preferred_element_type=F32)


def hidden_rows(x, mod_ref):
    mean = jnp.mean(x, axis=-1, keepdims=True)
    centred = x - mean
    var = jnp.mean(centred * centred, axis=-1, keepdims=True)
    normed = centred * lax.rsqrt(var + 1e-6)
    return [(normed * (1.0 + mod_ref[g, 1:2, :]) + mod_ref[g, 0:1, :]).astype(BF) for g in (0, 1)]


def fill_bias(bias_ref, where, dist, row_a, row_b, second):
    usable = jnp.where(second, row_b, row_a) > 0.5
    usable = usable | (dist == 0.0)
    for r in range(5):
        bias_ref[where + (r,)] = jnp.where(usable & (dist <= r + 1.0), 0.0, -1e30)


def attend(q_ref, k_ref, v_ref, bias, radius_ref, weight, out_ref):
    lane = lax.broadcasted_iota(jnp.int32, (1, 256), 1)
    lane128 = lax.broadcasted_iota(jnp.int32, (1, 128), 1)
    tiles = {}
    for h in range(HEADS):
        lo = HEAD_DIM * h
        base = min(lo // 128, 7) * 128
        keep = ((lane >= lo - base) & (lane < lo + HEAD_DIM - base)).astype(F32).astype(BF)
        q = q_ref[:, base : base + 256] * keep
        s = dot_nt(q, k_ref[:, base : base + 256]) + bias(radius_ref[h] - 1)
        top = jnp.max(s, axis=-1, keepdims=True)
        e = jnp.exp2((s - top) * EXP_SCALE)
        total = jnp.sum(e, axis=-1, keepdims=True)
        o = dot(e.astype(BF), v_ref[:, base : base + 256])
        scale = weight / total
        for half in (0, 1):
            j = base // 128 + half
            start, end = max(lo - j * 128, 0), min(lo + HEAD_DIM - j * 128, 128)
            if start >= end:
                continue
            piece = o[:, half * 128 : half * 128 + 128] * scale
            if j in tiles:
                piece = jnp.where(lane128 >= start, piece, tiles[j])
            tiles[j] = piece
            if end == 128:
                out_ref[:, j * 128 : (j + 1) * 128] = tiles.pop(j).astype(BF)


def own_kernel(latent, control, valid, mod, w, own, send_own, send_ctl, valid_pad, qkv, msg, hid):
    step = pl.program_id(0)

    @pl.when(step == 0)
    def _():
        rows = hidden_rows(dot(own[...], latent[...]), mod)
        hid[:224] = rows[0]
        hid[224:] = rows[1]

    out = dot(hid[...], w[...]).astype(BF)
    qkv[0, 0] = out[:224]
    qkv[0, 1] = out[224:]

    @pl.when(step == 2)
    def _():
        rows = lax.broadcasted_iota(jnp.int32, (32, 1), 0)
        val = valid[...].astype(F32)
        for i, tile in ((0, 0), (1, 3)):
            msg[i, :64] = dot(send_own[i], latent[...]).astype(BF)
            hot = (send_ctl[i].astype(F32) * val[tile : tile + 1]).astype(BF)
            ctl = dot(hot, control[tile])
            row = dot(jnp.broadcast_to(val[tile : tile + 1], (8, TILE_TOK)).astype(BF), valid_pad[...])
            msg[i, 64:, 256:] = ctl[:, 256:].astype(BF)
            msg[i, 64:, :256] = jnp.where(rows == 31, row[0:1], ctl[:, :256]).astype(BF)


def pack_kernel(msg, above, below, send_rim, west, east):
    for i, out in ((0, west), (1, east)):
        rim = dot(send_rim[i, :, :64], above[...]) + dot(send_rim[i, :, 64:], below[...])
        out[:64] = (msg[i, :64].astype(F32) + rim).astype(BF)
        out[64:] = msg[i, 64:]


def middle_kernel(
    radius, above, below, valid, mod, w, qkv_own, rim, dist, key_map_ref, query, qkv, attn, hid, part, qw, kw, vw, bias
):
    step = pl.program_id(0)

    @pl.when(step == 0)
    def _():
        x = dot(rim[:, :64], above[...]) + dot(rim[:, 64:], below[...])
        rows = hidden_rows(x, mod)
        hid[:112] = rows[0]
        hid[112:] = rows[1]

    @pl.when(step < 3)
    def _():
        out = dot(hid[...], w[...]).astype(BF)
        qkv[0, 0] = out[:112]
        qkv[0, 1] = out[112:]
        part[step, 0] = out[:112]
        part[step, 1] = out[112:]

    @pl.when(step == 2)
    def _():
        val = valid[...].astype(F32).astype(BF)
        row_a = dot(val, key_map_ref[0])[1:2]
        row_b = dot(val, key_map_ref[1])[2:3]
        second = lax.broadcasted_iota(jnp.int32, (288, 1), 0) >= 144
        fill_bias(bias, (), dist[...].astype(F32), row_a, row_b, second)
        for g in (0, 1):
            for c, win in ((1, kw), (2, vw)):
                for i in range(5):
                    b = 2 + i
                    win[g, i * 48 : i * 48 + 32] = qkv_own[c, g, (b - 1) * 32 : b * 32]
                    win[g, i * 48 + 32 : i * 48 + 48] = part[c, g, (b - 1) * 16 : b * 16]
                win[g, 240:] = jnp.zeros((16, D), BF)
            for u in (0, 1):
                for i in range(3):
                    b = 2 + 2 * u + i
                    qw[g, u, i * 48 : i * 48 + 32] = qkv_own[0, g, (b - 1) * 32 : b * 32]
                    qw[g, u, i * 48 + 32 : i * 48 + 48] = part[0, g, (b - 1) * 16 : b * 16]

    @pl.when(step >= 3)
    def _():
        g = (step - 3) // 2
        u = (step - 3) % 2
        val = valid[pl.ds(u + 1, 1), :].astype(F32)
        weight = jnp.sum(query[0].astype(F32) * val, axis=1, keepdims=True)
        attend(
            qw.at[g, u], kw.at[g], vw.at[g], lambda r: bias[r, pl.ds(pl.multiple_of(u * 144, 16), 144), :], radius, weight, attn.at[0, 0]
        )


def unit_weights(unit, query, query_side, rows):
    hot = query[unit].astype(F32) * rows[unit]
    weight = jnp.sum(hot, axis=1, keepdims=True)
    if unit in (0, 3):
        i = unit // 3
        weight = weight + jnp.sum(query_side[i].astype(F32) * rows[4 + i], axis=1, keepdims=True)
    return hot, weight


def valid_rows(valid, west, east):
    val = valid[...].astype(F32)
    rows = [val[t : t + 1] for t in range(4)]
    for ref in (west, east):
        rows.append(ref[80:96, :256].astype(F32)[15:16, :TILE_TOK])
    return rows


def edge_kernel(
    radius, latent, above, below, west, east, valid, mod, w, qkv_own, qkv_rim, attn_mid, w_out, control,
    edge, dist, key_side, query, query_side, x_rim, put_ctl,
    up, down, core, count, hid, part, qw, kw, vw, bias, weights, attn,
):
    step = pl.program_id(0)

    @pl.when(step == 0)
    def _():
        x = (
            dot(edge[:, :256], latent[...])
            + dot(edge[:, 256:320], above[...])
            + dot(edge[:, 320:384], below[...])
            + dot(edge[:, 384:480], west[...])
            + dot(edge[:, 480:], east[...])
        )
        rows = hidden_rows(x, mod)
        hid[:192] = rows[0][:192]
        hid[192:384] = rows[1][:192]
        hid[384:480] = rows[0][192:]
        hid[480:] = rows[1][192:]

    @pl.when(step == 0)
    def _():
        out = dot(hid[384:], w[...]).astype(BF)
        for i in (0, 1):
            for g in (0, 1):
                at = g * 96 + i * 48
                qw[i, g, 96 * i : 96 * i + 48] = out[at : at + 48]

    @pl.when((step == 1) | (step == 2))
    def _():
        out = dot(hid[:384], w[...]).astype(BF)
        part[step - 1, 0] = out[:192]
        part[step - 1, 1] = out[192:]

    @pl.when(step == 2)
    def _():
        rows = valid_rows(valid, west, east)
        pair = lax.broadcasted_iota(jnp.int32, (144, 1), 0)
        for i, unit in ((0, 0), (1, 3)):
            eight = lambda r: jnp.broadcast_to(r, (8, TILE_TOK)).astype(BF)
            row_a = dot(eight(rows[unit]), key_side[2 * i])[0:1]
            row_b = dot(eight(rows[4 + i]), key_side[2 * i + 1])[0:1]
            second = (pair < 48) & (pair % 4 < 2) if i == 0 else (pair >= 96) & (pair % 4 >= 2)
            fill_bias(bias, (i,), dist[i].astype(F32), row_a, row_b, second)
            weights[i] = jnp.broadcast_to(unit_weights(unit, query, query_side, rows)[1], (144, 128))
            edges = ((0, 0), (1, 1)) if i == 0 else ((2, 2), (3, 3))
            inner = ((2, 1), (3, 2)) if i == 0 else ((0, 6), (1, 7))
            for g in (0, 1):
                for c, win in ((1, kw), (2, vw)):
                    for at, e in edges:
                        win[i, g, at * 48 : at * 48 + 48] = part[c - 1, g, e * 48 : e * 48 + 48]
                    for at, b in inner:
                        win[i, g, at * 48 : at * 48 + 32] = qkv_own[c, g, (b - 1) * 32 : b * 32]
                        win[i, g, at * 48 + 32 : at * 48 + 48] = qkv_rim[c, g, (b - 1) * 16 : b * 16]
                    win[i, g, 192:] = jnp.zeros((64, D), BF)
                for at, b in ((1, 1), (2, 2)) if i == 0 else ((0, 6), (1, 7)):
                    qw[i, g, at * 48 : at * 48 + 32] = qkv_own[0, g, (b - 1) * 32 : b * 32]
                    qw[i, g, at * 48 + 32 : at * 48 + 48] = qkv_rim[0, g, (b - 1) * 16 : b * 16]

    @pl.when((step >= 3) & (step < 7))
    def _():
        i = (step - 3) // 2
        g = (step - 3) % 2
        attend(qw.at[i, g], kw.at[i, g], vw.at[i, g], lambda r: bias[i, r], radius, weights[i][:, :1], attn.at[i, g])

    @pl.when(step == 7)
    def _():
        rows = valid_rows(valid, west, east)
        hots, wts = zip(*[unit_weights(u, query, query_side, rows) for u in range(4)])
        margin = [[], []]
        for g in (0, 1):
            for b in range(9):
                total = None
                for u, third in holders(b):
                    src = attn[u // 3, g] if u in (0, 3) else attn_mid[g, u - 1]
                    piece = src[third * 48 : third * 48 + 48].astype(F32)
                    total = piece if total is None else total + piece
                total = total.astype(BF)
                core[g, b * 32 : (b + 1) * 32] = total[:32]
                margin[g].append(total[32:])
        proj = dot(jnp.concatenate(margin[0] + margin[1], axis=0), w_out[...])
        sums = (GUIDE * mod[0, 2:3]) * proj[:144] + ((1.0 - GUIDE) * mod[1, 2:3]) * proj[144:]
        ctl = []
        for u in range(4):
            hot = jnp.concatenate([hots[u][i * 48 + 32 : i * 48 + 48] for i in range(3)], axis=0).astype(BF)
            ctl.append(dot(hot, control[u]))
        counts, extra = [], []
        for b in range(9):
            number = sum(wts[u][third * 48 : third * 48 + 48] for u, third in holders(b))
            count[b * 32 : (b + 1) * 32] = jnp.broadcast_to(number[:32], (32, 128))
            counts.append(number[32:])
            term = sum(ctl[u][third * 16 : third * 16 + 16] for u, third in holders(b))
            if b in (0, 8):
                term = term + dot(put_ctl[b // 8, 32:], (west if b == 0 else east)[64:])
            extra.append(term)
        number = jnp.concatenate(counts, axis=0)
        x = dot(x_rim[:, :64], above[...]) + dot(x_rim[:, 64:], below[...])
        sums = sums + number * x + jnp.concatenate(extra, axis=0)
        slot = lax.broadcasted_iota(jnp.int32, (72, D), 0)
        lane = lax.broadcasted_iota(jnp.int32, (72, D), 1)
        for at, out in ((0, up), (8, down)):
            pick = lambda a: jnp.concatenate([a[b * 16 + at : b * 16 + at + 8] for b in range(9)], axis=0)
            tail = jnp.sum(jnp.where(slot == lane, pick(number), 0.0), axis=0, keepdims=True)
            out[...] = jnp.concatenate([pick(sums), jnp.broadcast_to(tail, (8, D))], axis=0).astype(BF)


def core_kernel(core, w_out, mod, latent, control, valid, west, east, count, x_core, query, put_ctl, sums):
    val = valid[...].astype(F32)
    proj = dot(core[...].reshape(576, D), w_out[...])
    ctl = []
    for u in range(4):
        hot = (query[u].astype(F32) * val[u : u + 1]).astype(BF)
        hot = jnp.concatenate([hot[i * 48 : i * 48 + 32] for i in range(3)], axis=0)
        ctl.append(dot(hot, control[u]))
    x = dot(x_core[...], latent[...])
    gate0, gate1 = GUIDE * mod[0, 2:3], (1.0 - GUIDE) * mod[1, 2:3]
    for b in range(9):
        at = slice(b * 32, (b + 1) * 32)
        term = sum(ctl[u][third * 32 : third * 32 + 32] for u, third in holders(b))
        if b in (0, 8):
            term = term + dot(put_ctl[b // 8, :32], (west if b == 0 else east)[64:])
        term = term + gate0 * proj[at] + gate1 * proj[288 + b * 32 : 288 + (b + 1) * 32]
        sums[at] = term + count[at][:, :1] * x[at]


def final_kernel(sums, count, above, below, back, out):
    slot = lax.broadcasted_iota(jnp.int32, (72, 128), 0)
    lane = lax.broadcasted_iota(jnp.int32, (72, 128), 1)
    got = []
    for ref in (above, below):
        body = ref[...].astype(F32)
        number = jnp.sum(jnp.where(slot == lane, body[72:73, :128], 0.0), axis=1, keepdims=True)
        got.append((body[:72], number))
    blocks = []
    for b in range(9):
        total, number = sums[b * 32 : (b + 1) * 32], count[b * 32 : (b + 1) * 32]
        at = slice(b * 8, (b + 1) * 8)
        total = jnp.concatenate([total[:8] + got[0][0][at], total[8:24], total[24:] + got[1][0][at]], axis=0)
        number = jnp.concatenate([number[:8] + got[0][1][at], number[8:24], number[24:] + got[1][1][at]], axis=0)
        if b in (0, 8):
            shift = 2 if b == 0 else 30
            total = total + pltpu.roll(total, shift, 0)
            number = number + pltpu.roll(number, shift, 0)
        blocks.append((total / jnp.maximum(number[:, :1], 1.0)).astype(BF))
    out[...] = dot(back[...], jnp.concatenate(blocks, axis=0)).astype(BF)


def whole(shape):
    return pl.BlockSpec(shape, lambda *_: (0,) * len(shape))


def call(kernel, outs, args, specs=None, out_specs=None, grid=(1,), scratch=(), cost=(1e9, 4e6)):
    specs = specs or {}
    in_specs = [specs.get(i) or whole(a.shape) for i, a in enumerate(args)]
    out_specs = out_specs or [whole(o.shape) for o in outs]
    return pl.pallas_call(
        kernel,
        out_shape=outs,
        grid=grid,
        in_specs=in_specs,
        out_specs=out_specs,
        scratch_shapes=scratch,
        compiler_params=pltpu.CompilerParams(vmem_limit_bytes=VMEM, dimension_semantics=("arbitrary",) * len(grid)),
        cost_estimate=pl.CostEstimate(flops=int(cost[0]), bytes_accessed=int(cost[1]), transcendentals=0),
    )(*args)


def shape(*dims, dtype=BF):
    return jax.ShapeDtypeStruct(dims, dtype)


def local(latent, control, valid, radius, modulation, w_qkv, w_out):
    t = {k: jnp.asarray(v) for k, v in tables().items()}
    size_r, size_c = lax.axis_size("trow"), lax.axis_size("tcol")
    later_r = [(i, i + 1) for i in range(size_r - 1)]
    sooner_r = [(i + 1, i) for i in range(size_r - 1)]
    later_c = [(i, i + 1) for i in range(size_c - 1)]
    sooner_c = [(i + 1, i) for i in range(size_c - 1)]

    x = latent.reshape(256, D)
    control = control.reshape(4, TILE_TOK, D)
    valid = valid.reshape(4, TILE_TOK)
    above = lax.ppermute(x[192:], "trow", later_r)
    below = lax.ppermute(x[:64], "trow", sooner_r)
    smem = pl.BlockSpec(memory_space=pltpu.SMEM)
    chunk = pl.BlockSpec((D, D), lambda i: (0, jnp.minimum(i, 2)))

    qkv_own, msg = call(
        own_kernel,
        [shape(3, 2, 224, D), shape(2, 96, D)],
        [x, control, valid, modulation, w_qkv, t["own"], t["send_own"], t["send_ctl"], t["valid_pad"]],
        specs={4: chunk},
        out_specs=[pl.BlockSpec((1, 2, 224, D), lambda i: (i, 0, 0, 0)), whole((2, 96, D))],
        grid=(3,),
        scratch=[pltpu.VMEM((448, D), BF)],
        cost=(3.6e9, 12e6),
    )
    to_west, to_east = call(
        pack_kernel, [shape(96, D), shape(96, D)], [msg, above, below, t["send_rim"]], cost=(1e8, 1e6)
    )
    west = lax.ppermute(to_east, "tcol", later_c)
    east = lax.ppermute(to_west, "tcol", sooner_c)

    qkv_rim, attn_mid = call(
        middle_kernel,
        [shape(3, 2, 112, D), shape(2, 2, 144, D)],
        [radius, above, below, valid, modulation, w_qkv, qkv_own, t["rim"], t["dist_mid"], t["key_mid"], t["query"][1:2]],
        specs={0: smem, 5: chunk},
        out_specs=[
            pl.BlockSpec((1, 2, 112, D), lambda i: (jnp.minimum(i, 2), 0, 0, 0)),
            pl.BlockSpec((1, 1, 144, D), lambda i: (jnp.maximum(i - 3, 0) // 2, jnp.maximum(i - 3, 0) % 2, 0, 0)),
        ],
        grid=(7,),
        scratch=[
            pltpu.VMEM((224, D), BF),
            pltpu.VMEM((3, 2, 112, D), BF),
            pltpu.VMEM((2, 2, 144, D), BF),
            pltpu.VMEM((2, 256, D), BF),
            pltpu.VMEM((2, 256, D), BF),
            pltpu.VMEM((5, 288, 256), F32),
        ],
        cost=(8e9, 14e6),
    )
    up, down, core, count = call(
        edge_kernel,
        [shape(80, D), shape(80, D), shape(2, 288, D), shape(288, 128, dtype=F32)],
        [
            radius, x, above, below, west, east, valid, modulation, w_qkv, qkv_own, qkv_rim, attn_mid, w_out, control,
            t["edge"], t["dist_side"], t["key_side"], t["query"], t["query_side"], t["x_rim"], t["put_ctl"],
        ],
        specs={0: smem, 8: chunk},
        grid=(8,),
        scratch=[
            pltpu.VMEM((576, D), BF),
            pltpu.VMEM((2, 2, 192, D), BF),
            pltpu.VMEM((2, 2, 144, D), BF),
            pltpu.VMEM((2, 2, 256, D), BF),
            pltpu.VMEM((2, 2, 256, D), BF),
            pltpu.VMEM((2, 5, 144, 256), F32),
            pltpu.VMEM((2, 144, 128), F32),
            pltpu.VMEM((2, 2, 144, D), BF),
        ],
        cost=(1e10, 16e6),
    )
    got_below = lax.ppermute(up, "trow", sooner_r)
    got_above = lax.ppermute(down, "trow", later_r)
    (sums,) = call(
        core_kernel,
        [shape(288, D, dtype=F32)],
        [core, w_out, modulation, x, control, valid, west, east, count, t["x_core"], t["query"], t["put_ctl"]],
        cost=(2e9, 8e6),
    )
    (out,) = call(final_kernel, [shape(256, D)], [sums, count, got_above, got_below, t["back"]], cost=(2e8, 3e6))
    return out.reshape(CORE, 32, D)


def solution(mesh):
    placed = (
        P("trow", "tcol", None),
        P("trow", "tcol", None, None),
        P("trow", "tcol", None),
        P(),
        P(),
        P(),
        P(),
    )
    return jax.shard_map(
        local, mesh=mesh, in_specs=placed, out_specs=P("trow", "tcol", None), check_vma=False
    )
```

time: 204 us -> 112 us (0.55)
  the two profiles are of different devices: /device:TPU:103 before, /device:TPU:144 now
where the time goes in v1:
time: 112 us
  Pallas kernels  82.3 us (73%)
  starting transfers between devices  24 us (21%)
  local copies, waits for them, and re-layouts  5.16 us (5%)
    pallas_call x6, Pallas kernels, call(): pl.pallas_call(kernel, out_shape=outs, grid=grid, in_specs=in_specs, out_...  82.3 us
    ppermute x1, starting transfers between devices, local(): east = lax.ppermute(to_west, 'tcol', sooner_c)  6.23 us
    ppermute x1, starting transfers between devices, local(): got_below = lax.ppermute(up, 'trow', sooner_r)  6.03 us
    ppermute x1, starting transfers between devices, local(): below = lax.ppermute(x[:64], 'trow', sooner_r)  4.55 us
    unnamed x13, local copies, waits for them, and re-layouts  4.16 us
    ppermute x1, starting transfers between devices, local(): above = lax.ppermute(x[192:], 'trow', later_r)  3.4 us
  transfers between devices with their start and end apart: 6, of which 0 were waited for; matrix products, arithmetic and copies ran while one was open for 1% of the time, Pallas kernels for 39%

profile of v1, /device:TPU:144, one launch (start us, length us, event | category | flops | bytes accessed | tf_op | source)
XLA Modules:
  0.0 111.7 jit_solution(4237911638098134333)
XLA Ops:
  0.0 1.0 fusion
  1.0 3.4 %collective-permute-start = (bf16[64,1152]{1,0:T(8,128)(2,1)S(1)}, bf16[64,1152]{1,0:T(8,128)(2,1)S(1)}, u32[]{:S(2)}, u32[]{:S(2)}) collective-permute-start(bf16[64,1152]{1,0:T(8,128)(2,1)S(1)} %bitcast.13), channel_id=1, source_target_pairs={{0,16},{16,32},{32,48},{48,64},{64,80},{80,96},{96,112},{112,128},... | collective-permute-start | bytes 442376 | tf_op jit(solution)/shard_map/ppermute | solution.py:515
  4.4 4.6 %collective-permute-start.1 = (bf16[64,1152]{1,0:T(8,128)(2,1)S(1)}, bf16[64,1152]{1,0:T(8,128)(2,1)S(1)}, u32[]{:S(2)}, u32[]{:S(2)}) collective-permute-start(bf16[64,1152]{1,0:T(8,128)(2,1)S(1)} %bitcast.12), channel_id=1, source_target_pairs={{16,0},{32,16},{48,32},{64,48},{80,64},{96,80},{112,96},{128,112},... | collective-permute-start | bytes 442376 | tf_op jit(solution)/shard_map/ppermute | solution.py:516
  9.0 1.4 %copy.25.mod = f32[2,3,1152]{2,1,0:T(4,128)} copy(f32[2,3,1152]{2,0,1:T(2,128)} %param.28) | data formatting | bytes 55296 | tf_op args[4]
  10.3 10.0 %shard_map.226 = (bf16[3,2,224,1152]{3,2,1,0:T(8,128)(2,1)}, bf16[2,96,1152]{2,1,0:T(8,128)(2,1)}) custom-call(bf16[256,1152]{1,0:T(8,128)(2,1)} %bitcast.6, bf16[4,144,1152]{2,1,0:T(8,128)(2,1)} %bitcast.9, s32[4,144]{1,0:T(4,128)} %bitcast.14, f32[2,3,1152]{2,1,0:T(4,128)} %copy.25.mod, bf16[1152,3456]{1,0:T(8,128)(2,1)} %w.5, ...), custom_call_target="tpu_custom_call" | custom-call | flops 3600000000 | bytes 12000000 | tf_op jit(solution)/shard_map/pallas_call | solution.py:488
  20.4 0.0 collective-permute-done.above
  20.4 0.0 copy-start.4
  20.4 0.0 collective-permute-done.1.below
  20.4 0.0 copy-start.5
  20.4 0.6 copy-done.4
  21.0 0.1 copy-done.5
  21.1 2.2 %shard_map.227 = (bf16[96,1152]{1,0:T(8,128)(2,1)}, bf16[96,1152]{1,0:T(8,128)(2,1)}) custom-call(bf16[2,96,1152]{2,1,0:T(8,128)(2,1)} %get-tuple-element.15.msg, bf16[64,1152]{1,0:T(8,128)(2,1)} %copy-done.4, bf16[64,1152]{1,0:T(8,128)(2,1)} %copy-done.5, bf16[2,64,128]{2,1,0:T(8,128)(2,1)} %constant.46.clone.send_rim), custom_call_target="tpu_custom_call" | custom-call | flops 100000000 | bytes 1000000 | tf_op jit(solution)/shard_map/pallas_call | solution.py:488
  23.3 1.9 %collective-permute-start.2 = (bf16[96,1152]{1,0:T(8,128)(2,1)}, bf16[96,1152]{1,0:T(8,128)(2,1)S(1)}, u32[]{:S(2)}, u32[]{:S(2)}) collective-permute-start(bf16[96,1152]{1,0:T(8,128)(2,1)} %get-tuple-element.16), channel_id=1, source_target_pairs={{0,1},{1,2},{2,3},{3,4},{4,5},{5,6},{6,7},{7,8},{8,9},{9,10},{10,1... | collective-permute-start | bytes 663560 | tf_op jit(solution)/shard_map/ppermute | solution.py:533
  25.2 6.2 %collective-permute-start.3 = (bf16[96,1152]{1,0:T(8,128)(2,1)}, bf16[96,1152]{1,0:T(8,128)(2,1)S(1)}, u32[]{:S(2)}, u32[]{:S(2)}) collective-permute-start(bf16[96,1152]{1,0:T(8,128)(2,1)} %get-tuple-element.17), channel_id=1, source_target_pairs={{1,0},{2,1},{3,2},{4,3},{5,4},{6,5},{7,6},{8,7},{9,8},{10,9},{11,1... | collective-permute-start | bytes 663560 | tf_op jit(solution)/shard_map/ppermute | solution.py:534
  31.5 26.6 %shard_map.228 = (bf16[3,2,112,1152]{3,2,1,0:T(8,128)(2,1)}, bf16[2,2,144,1152]{3,2,1,0:T(8,128)(2,1)}) custom-call(s32[16]{0:T(128)} %radius.3, bf16[64,1152]{1,0:T(8,128)(2,1)} %copy-done.4, bf16[64,1152]{1,0:T(8,128)(2,1)} %copy-done.5, s32[4,144]{1,0:T(4,128)} %bitcast.15, f32[2,3,1152]{2,1,0:T(4,128)} %copy.25.mod, bf16[1152,3456]{1,0:T(8,128)(2,1)} %w.5, ...), custom_call_target="tpu_custom_call" | custom-call | flops 8000000000 | bytes 14000000 | tf_op jit(solution)/shard_map/pallas_call | solution.py:488
  58.1 0.0 collective-permute-done.2.west
  58.1 0.0 copy-start
  58.1 0.0 collective-permute-done.3.east
  58.1 0.0 copy-start.1
  58.1 0.7 copy-done
  58.8 0.1 copy-done.1
  58.9 33.9 %shard_map.229 = (bf16[80,1152]{1,0:T(8,128)(2,1)}, bf16[80,1152]{1,0:T(8,128)(2,1)}, bf16[2,288,1152]{2,1,0:T(8,128)(2,1)}, f32[288,128]{1,0:T(8,128)}) custom-call(s32[16]{0:T(128)} %radius.3, bf16[256,1152]{1,0:T(8,128)(2,1)} %bitcast.7, bf16[64,1152]{1,0:T(8,128)(2,1)} %copy-done.4, bf16[64,1152]{1,0:T(8,128)(2,1)} %copy-done.5, ...), custom_call_target="tpu_custom_call" | custom-call | flops 10000000000 | bytes 16000000 | tf_op jit(solution)/shard_map/pallas_call | solution.py:488
  92.8 1.9 %collective-permute-start.4 = (bf16[80,1152]{1,0:T(8,128)(2,1)}, bf16[80,1152]{1,0:T(8,128)(2,1)S(1)}, u32[]{:S(2)}, u32[]{:S(2)}) collective-permute-start(bf16[80,1152]{1,0:T(8,128)(2,1)} %get-tuple-element.23), channel_id=1, source_target_pairs={{0,16},{16,32},{32,48},{48,64},{64,80},{80,96},{96,112},{112,128},... | collective-permute-start | bytes 552968 | tf_op jit(solution)/shard_map/ppermute | solution.py:578
  94.7 6.0 %collective-permute-start.5 = (bf16[80,1152]{1,0:T(8,128)(2,1)}, bf16[80,1152]{1,0:T(8,128)(2,1)S(1)}, u32[]{:S(2)}, u32[]{:S(2)}) collective-permute-start(bf16[80,1152]{1,0:T(8,128)(2,1)} %get-tuple-element.24), channel_id=1, source_target_pairs={{16,0},{32,16},{48,32},{64,48},{80,64},{96,80},{112,96},{128,112},... | collective-permute-start | bytes 552968 | tf_op jit(solution)/shard_map/ppermute | solution.py:577
  100.7 6.6 %shard_map.230.sums = f32[288,1152]{1,0:T(8,128)} custom-call(bf16[2,288,1152]{2,1,0:T(8,128)(2,1)} %get-tuple-element.21.core, bf16[1152,1152]{1,0:T(8,128)(2,1)} %w_out.3, f32[2,3,1152]{2,1,0:T(4,128)} %copy.25.mod, bf16[256,1152]{1,0:T(8,128)(2,1)} %bitcast.8, bf16[4,144,1152]{2,1,0:T(8,128)(2,1)} %bitcast.11, s32[4,144]{1,0:T(4,128)} %bitcast.17, ...), custom_call_target="tpu_custom_call" | custom-call | flops 2000000000 | bytes 8000000 | tf_op jit(solution)/shard_map/pallas_call | solution.py:488
  107.3 0.0 collective-permute-done.4.above
  107.3 0.0 copy-start.2
  107.3 0.0 collective-permute-done.5.below
  107.3 0.7 copy-done.2
  108.0 0.0 copy-start.3
  108.0 0.7 copy-done.3
  108.7 3.0 %shard_map.231 = bf16[256,1152]{1,0:T(8,128)(2,1)} custom-call(f32[288,1152]{1,0:T(8,128)} %shard_map.230.sums, f32[288,128]{1,0:T(8,128)} %get-tuple-element.22.count, bf16[80,1152]{1,0:T(8,128)(2,1)} %copy-done.2, bf16[80,1152]{1,0:T(8,128)(2,1)} %copy-done.3, bf16[256,288]{1,0:T(8,128)(2,1)} %constant.50.clone.back), custom_call_target="tpu_custom_call" | custom-call | flops 200000000 | bytes 3000000 | tf_op jit(solution)/shard_map/pallas_call | solution.py:488
Async XLA Ops:
  1.0 19.4 %collective-permute-start = (bf16[64,1152]{1,0:T(8,128)(2,1)S(1)}, bf16[64,1152]{1,0:T(8,128)(2,1)S(1)}, u32[]{:S(2)}, u32[]{:S(2)}) collective-permute-start(bf16[64,1152]{1,0:T(8,128)(2,1)S(1)} %bitcast.13), channel_id=1, source_target_pairs={{0,16},{16,32},{32,48},{48,64},{64,80},{80,96},{96,112},{112,128},... | collective-permute-start | bytes 442376 | tf_op jit(solution)/shard_map/ppermute | solution.py:515
  4.4 16.0 %collective-permute-start.1 = (bf16[64,1152]{1,0:T(8,128)(2,1)S(1)}, bf16[64,1152]{1,0:T(8,128)(2,1)S(1)}, u32[]{:S(2)}, u32[]{:S(2)}) collective-permute-start(bf16[64,1152]{1,0:T(8,128)(2,1)S(1)} %bitcast.12), channel_id=1, source_target_pairs={{16,0},{32,16},{48,32},{64,48},{80,64},{96,80},{112,96},{128,112},... | collective-permute-start | bytes 442376 | tf_op jit(solution)/shard_map/ppermute | solution.py:516
  20.4 0.7 copy-start.4
  20.4 0.7 copy-start.5
  23.3 34.8 %collective-permute-start.2 = (bf16[96,1152]{1,0:T(8,128)(2,1)}, bf16[96,1152]{1,0:T(8,128)(2,1)S(1)}, u32[]{:S(2)}, u32[]{:S(2)}) collective-permute-start(bf16[96,1152]{1,0:T(8,128)(2,1)} %get-tuple-element.16), channel_id=1, source_target_pairs={{0,1},{1,2},{2,3},{3,4},{4,5},{5,6},{6,7},{7,8},{8,9},{9,10},{10,1... | collective-permute-start | bytes 663560 | tf_op jit(solution)/shard_map/ppermute | solution.py:533
  25.2 32.9 %collective-permute-start.3 = (bf16[96,1152]{1,0:T(8,128)(2,1)}, bf16[96,1152]{1,0:T(8,128)(2,1)S(1)}, u32[]{:S(2)}, u32[]{:S(2)}) collective-permute-start(bf16[96,1152]{1,0:T(8,128)(2,1)} %get-tuple-element.17), channel_id=1, source_target_pairs={{1,0},{2,1},{3,2},{4,3},{5,4},{6,5},{7,6},{8,7},{9,8},{10,9},{11,1... | collective-permute-start | bytes 663560 | tf_op jit(solution)/shard_map/ppermute | solution.py:534
  58.1 0.7 copy-start
  58.1 0.7 copy-start.1
  92.8 14.6 %collective-permute-start.4 = (bf16[80,1152]{1,0:T(8,128)(2,1)}, bf16[80,1152]{1,0:T(8,128)(2,1)S(1)}, u32[]{:S(2)}, u32[]{:S(2)}) collective-permute-start(bf16[80,1152]{1,0:T(8,128)(2,1)} %get-tuple-element.23), channel_id=1, source_target_pairs={{0,16},{16,32},{32,48},{48,64},{64,80},{80,96},{96,112},{112,128},... | collective-permute-start | bytes 552968 | tf_op jit(solution)/shard_map/ppermute | solution.py:578
  94.7 12.6 %collective-permute-start.5 = (bf16[80,1152]{1,0:T(8,128)(2,1)}, bf16[80,1152]{1,0:T(8,128)(2,1)S(1)}, u32[]{:S(2)}, u32[]{:S(2)}) collective-permute-start(bf16[80,1152]{1,0:T(8,128)(2,1)} %get-tuple-element.24), channel_id=1, source_target_pairs={{16,0},{32,16},{48,32},{64,48},{80,64},{96,80},{112,96},{128,112},... | collective-permute-start | bytes 552968 | tf_op jit(solution)/shard_map/ppermute | solution.py:577
  107.3 0.7 copy-start.2
  108.0 0.7 copy-start.3

commit v2 on v0

v2 whole, which is shorter than its diff:
```python
import functools

import jax
import jax.numpy as jnp
import numpy as np
from jax import lax
from jax.experimental import pallas as pl
from jax.experimental.pallas import tpu as pltpu
from jax.sharding import PartitionSpec as P

D = 1152
HEADS = 16
HEAD_DIM = 72
CORE = 8
MARGIN = 2
SIDE = 12
TILE_TOK = 144
GUIDE = 4.5
REACH = 5
FAR = 99.0
BF = jnp.bfloat16
F32 = jnp.float32
EXP_SCALE = float(np.log2(np.e) / np.sqrt(72.0))
VMEM = 28 * 1024 * 1024

JR = np.array([j // 4 if j < 32 else (j - 40) // 4 if j < 40 else 8 + (j - 40) // 4 for j in range(48)])
JC = np.arange(48) % 4
FIRST = (-1, 1, 3, 4, 6)
CUTS = (0, 126, 252, 324, 450, 576)
KEYS = 192


def one_hot(rows, depth):
    hot = np.zeros((len(rows), depth), np.float32)
    for i, src in enumerate(rows):
        if src is not None:
            hot[i, src] = 1.0
    return hot


def source(row, col):
    if col < 0:
        return 384 + (row + 2) * REACH + col + REACH if col >= -REACH else None
    if col >= 32:
        return 480 + (row + 2) * REACH + col - 32 if col < 32 + REACH else None
    return natural(row, col)


def natural(row, col):
    if row < 0:
        return 256 + (row + 2) * 32 + col
    if row >= 8:
        return 320 + (row - 8) * 32 + col
    return row * 32 + col


def block_tokens(block):
    return [(int(r), int(4 * block - 2 + c)) for r, c in zip(JR, JC)]


def unit_queries(unit):
    entries = [(-1, 0), (-1, 1)]
    for t in range(4):
        entries += [(t, c) for c in range(max(8 * t - 2, 0), min(8 * t + 10, 32))]
    entries += [(4, 30), (4, 31)]
    flat = [(t, r, c) for t, c in entries for r in range(-2, 10)][CUTS[unit] : CUTS[unit + 1]]
    return flat + [None] * (128 - len(flat))


def unit_keys(unit):
    return [p for b in range(FIRST[unit], FIRST[unit] + 4) for p in block_tokens(b)]


def tile_token(tile, row, col):
    r, c = row + 2, col - 8 * tile + 2
    return r * SIDE + c if 0 <= r < SIDE and 0 <= c < SIDE else None


def distances(unit):
    dist = np.full((KEYS, 128), FAR, np.float32)
    for i, query in enumerate(unit_queries(unit)):
        for k, key in enumerate(unit_keys(unit)):
            if query is not None and -REACH <= key[1] < 32 + REACH and tile_token(query[0], *key) is not None:
                dist[k, i] = max(abs(query[1] - key[0]), abs(query[2] - key[1]))
    return dist


@functools.cache
def tables():
    bf = lambda a: np.asarray(a, jnp.bfloat16)
    t = {}
    t["own"] = bf(one_hot([source(*p) for b in range(1, 8) for p in block_tokens(b)[:32]], 256))
    rim = one_hot([source(*p) for b in range(1, 8) for p in block_tokens(b)[32:]], 384)
    queries = [[None if q is None else source(*q[1:]) for q in unit_queries(u)] for u in range(5)]
    middle = np.concatenate([rim, one_hot(queries[1] + queries[2] + queries[3], 384)])
    t["middle"] = bf(middle)
    edge = one_hot([source(*p) for b in (-1, 0, 8, 9) for p in block_tokens(b)], 576)
    t["edge"] = bf(np.concatenate([edge, one_hot(queries[0] + queries[4], 576)]))
    t["dist"] = bf(np.stack([distances(u) for u in range(5)]))
    t["key"] = bf(
        np.stack([[one_hot([tile_token(u + k, *p) for p in unit_keys(u)], TILE_TOK) for k in (-1, 0)] for u in range(5)])
    )
    slot = np.zeros((5, 2, TILE_TOK, 128), np.float32)
    comb = np.zeros((5, 384, 128), np.float32)
    second = np.zeros((5, 1, 128), np.float32)
    for u in range(5):
        for i, q in enumerate(unit_queries(u)):
            if q is not None:
                which = q[0] - u + 1
                assert which in (0, 1)
                slot[u, which, tile_token(*q), i] = 1.0
                second[u, 0, i] = which
                comb[u, natural(*q[1:]), i] = 1.0
    t["slot"], t["second"] = bf(slot), second
    t["comb_core"], t["comb_rim"] = bf(comb[:, :256]), bf(comb[:, 256:])
    send = np.zeros((2, 64, 384), np.float32)
    send_ctl = np.zeros((2, 32, TILE_TOK), np.float32)
    put = np.zeros((2, 384, 32), np.float32)
    for r in range(SIDE):
        for k in range(REACH):
            send[0, r * REACH + k, source(r - 2, k)] = 1.0
            send[1, r * REACH + k, source(r - 2, 32 - REACH + k)] = 1.0
        for k in range(2):
            send_ctl[0, r * 2 + k, r * SIDE + k] = 1.0
            send_ctl[1, r * 2 + k, r * SIDE + 10 + k] = 1.0
            put[0, natural(r - 2, k), r * 2 + k] = 1.0
            put[1, natural(r - 2, 30 + k), r * 2 + k] = 1.0
    t["send_own"], t["send_rim"], t["send_ctl"] = bf(send[:, :, :256]), bf(send[:, :, 256:]), bf(send_ctl)
    t["put_core"], t["put_rim"] = bf(put[:, :256]), bf(put[:, 256:])
    t["valid_pad"] = bf(np.eye(TILE_TOK, 256))
    ctl = np.zeros((4, 384, TILE_TOK), np.float32)
    for tile in range(4):
        for r in range(-2, 10):
            for c in range(max(8 * tile - 2, 0), min(8 * tile + 10, 32)):
                ctl[tile, natural(r, c), tile_token(tile, r, c)] = 1.0
    t["ctl_core"], t["ctl_rim"] = bf(ctl[:, :256]), bf(ctl[:, 256:])
    return t


def dot(a, b):
    return jnp.dot(a, b, preferred_element_type=F32)


def dot_nt(a, b):
    return lax.dot_general(a, b, (((1,), (1,)), ((), ())), preferred_element_type=F32)


def hidden_rows(x, mod_ref):
    mean = jnp.mean(x, axis=-1, keepdims=True)
    centred = x - mean
    var = jnp.mean(centred * centred, axis=-1, keepdims=True)
    normed = centred * lax.rsqrt(var + 1e-6)
    return [(normed * (1.0 + mod_ref[g, 1:2, :]) + mod_ref[g, 0:1, :]).astype(BF) for g in (0, 1)]


def eight(row):
    return jnp.broadcast_to(row, (8, row.shape[1])).astype(BF)


def fill_bias(bias_ref, unit, dist, key_a, key_b, second, valid_a, valid_b):
    usable_a, usable_b = dot_nt(key_a, eight(valid_a))[:, :1], dot_nt(key_b, eight(valid_b))[:, :1]
    dist = dist.astype(F32)
    usable = (jnp.where(second > 0.5, usable_b, usable_a) > 0.5) | (dist == 0.0)
    dist = jnp.where(usable, dist, FAR)
    for r in range(5):
        bias_ref[unit, r] = jnp.where(dist <= r + 1.0, 0.0, -1e30)


def attend(q_ref, keys, values, bias, radius_ref, out_ref):
    lane = lax.broadcasted_iota(jnp.int32, (1, 256), 1)
    scores, probs = [], []
    for p in range(8):
        lanes = slice(128 * p, 128 * p + 256)
        q = q_ref[:, lanes]
        both = [
            q * ((lane >= 16 * p + at) & (lane < 16 * p + at + HEAD_DIM)).astype(F32).astype(BF) for at in (0, HEAD_DIM)
        ]
        scores.append(dot_nt(keys(lanes), jnp.concatenate(both, axis=0)))
    for p in range(8):
        exps, scales = [], []
        for i in (0, 1):
            s = scores[p][:, 128 * i : 128 * i + 128] + bias(radius_ref[2 * p + i] - 1)
            top = jnp.max(s, axis=0, keepdims=True)
            e = jnp.exp2((s - top) * EXP_SCALE)
            scales.append(1.0 / jnp.sum(e, axis=0, keepdims=True))
            exps.append(e)
        probs.append((jnp.concatenate(exps, axis=1).astype(BF), scales))
    for p in range(8):
        v = values(slice(128 * p, 128 * p + 256)).T[16 * p : 16 * p + 144]
        e, scales = probs[p]
        o = dot(v, e)
        o = jnp.concatenate([o[:72, :128] * scales[0], o[72:, 128:] * scales[1]], axis=0)
        out_ref[144 * p : 144 * p + 144, :] = o.astype(BF)


def inner_window(own, rim, c, g, first, count):
    def get(lanes):
        parts = []
        for i in range(count):
            parts += [own[c, g, first + i, :, lanes], rim[c, g, first + i, :, lanes]]
        return parts

    return get


def own_kernel(latent, control, valid, mod, w, own, send_own, send_ctl, valid_pad, kv, msg, hid):
    rows = hidden_rows(dot(own[...], latent[...]), mod)
    hid[:224] = rows[0]
    hid[224:] = rows[1]
    for c in (0, 1):
        out = dot(hid[...], w[:, (c + 1) * D : (c + 2) * D])
        kv[c] = out.astype(BF).reshape(2, 7, 32, D)
    rows = lax.broadcasted_iota(jnp.int32, (32, 1), 0)
    val = valid[...].astype(F32)
    for i, tile in ((0, 0), (1, 3)):
        msg[i, :64] = dot(send_own[i], latent[...]).astype(BF)
        hot = (send_ctl[i].astype(F32) * val[tile : tile + 1]).astype(BF)
        ctl = dot(hot, control[tile])
        row = dot(eight(val[tile : tile + 1]), valid_pad[...])
        msg[i, 64:, 256:] = ctl[:, 256:].astype(BF)
        msg[i, 64:, :256] = jnp.where(rows == 31, row[0:1], ctl[:, :256]).astype(BF)


def pack_kernel(msg, above, below, send_rim, west, east):
    for i, out in ((0, west), (1, east)):
        rim = dot(send_rim[i, :, :64], above[...]) + dot(send_rim[i, :, 64:], below[...])
        out[:64] = (msg[i, :64].astype(F32) + rim).astype(BF)
        out[64:] = msg[i, 64:]


def middle_kernel(radius, latent, above, below, valid, mod, w, kv_own, middle, dist, key, second, kv_rim, attn, hid, qs, bias):
    x = dot(middle[:, :256], latent[...]) + dot(middle[:, 256:320], above[...]) + dot(middle[:, 320:], below[...])
    rows = hidden_rows(x, mod)
    for g in (0, 1):
        hid[g * 112 : (g + 1) * 112] = rows[g][:112]
        hid[224 + g * 384 : 224 + (g + 1) * 384] = rows[g][112:]
    qs[...] = dot(hid[224:], w[:, :D]).astype(BF).reshape(2, 3, 128, D)
    for c in (0, 1):
        kv_rim[c] = dot(hid[:224], w[:, (c + 1) * D : (c + 2) * D]).astype(BF).reshape(2, 7, 16, D)
    val = valid[...].astype(F32)
    for u in range(3):
        fill_bias(bias, u, dist[u], key[u, 0], key[u, 1], second[u], val[u : u + 1], val[u + 1 : u + 2])

    @pl.loop(0, 6)
    def _(i):
        u, g = i // 2, i % 2
        first = u + jnp.minimum(u, 1)
        keys = inner_window(kv_own, kv_rim, 0, g, first, 4)
        values = inner_window(kv_own, kv_rim, 1, g, first, 4)
        attend(
            qs.at[g, u],
            lambda lanes: jnp.concatenate(keys(lanes), axis=0),
            lambda lanes: jnp.concatenate(values(lanes), axis=0),
            lambda r: bias[u, r],
            radius,
            attn.at[u, g],
        )


def valid_rows(valid, west, east):
    val = valid[...].astype(F32)
    side = [ref[80:96, :256].astype(F32)[15:16, :TILE_TOK] for ref in (west, east)]
    return [side[0]] + [val[t : t + 1] for t in range(4)] + [side[1]]


def gather(unit, slot, comb, rows):
    weight = dot(eight(rows[unit]), slot[unit, 0]) + dot(eight(rows[unit + 1]), slot[unit, 1])
    return comb[unit].astype(F32) * weight[:1]


def block_sums(attn_of, rows, x, w_out, mod, control, west, east, slot, comb, ctl, put):
    weights = [gather(u, slot, comb, rows) for u in range(5)]
    number = sum(jnp.sum(w, axis=1, keepdims=True) for w in weights)
    n = number.shape[0]
    attn = [sum(dot_nt(weights[u].astype(BF), attn_of(u, g)) for u in range(5)).astype(BF) for g in (0, 1)]
    proj = dot(jnp.concatenate(attn, axis=0), w_out[...])
    sums = (GUIDE * mod[0, 2:3]) * proj[:n] + ((1.0 - GUIDE) * mod[1, 2:3]) * proj[n:] + number * x
    for tile in range(4):
        sums = sums + dot((ctl[tile].astype(F32) * rows[tile + 1]).astype(BF), control[tile])
    return sums + dot(put[0], west[64:]) + dot(put[1], east[64:]), number


def edge_kernel(
    radius, latent, above, below, west, east, valid, mod, w, kv_own, kv_rim, attn_mid, w_out, control,
    edge, dist, key, second, slot, comb, ctl, put,
    up, down, attn, hid, qs, kv, bias,
):
    x = (
        dot(edge[:, :256], latent[...])
        + dot(edge[:, 256:320], above[...])
        + dot(edge[:, 320:384], below[...])
        + dot(edge[:, 384:480], west[...])
        + dot(edge[:, 480:], east[...])
    )
    normed = hidden_rows(x, mod)
    for g in (0, 1):
        hid[g * 192 : (g + 1) * 192] = normed[g][:192]
        hid[384 + g * 256 : 384 + (g + 1) * 256] = normed[g][192:]
    qs[...] = dot(hid[384:], w[:, :D]).astype(BF).reshape(2, 2, 128, D)
    for c in (0, 1):
        kv[c] = dot(hid[:384], w[:, (c + 1) * D : (c + 2) * D]).astype(BF).reshape(2, 4, 48, D)
    rows = valid_rows(valid, west, east)
    for i, u in ((0, 0), (1, 4)):
        fill_bias(bias, i, dist[i], key[i, 0], key[i, 1], second[i], rows[u], rows[u + 1])

    for i in (0, 1):

        @pl.loop(0, 2)
        def _(g):
            def window(c):
                inner = inner_window(kv_own, kv_rim, c, g, 5 * i, 2)

                def get(lanes):
                    outer = [kv[c, g, 2 * i, :, lanes], kv[c, g, 2 * i + 1, :, lanes]]
                    parts = inner(lanes) + outer if i else outer + inner(lanes)
                    return jnp.concatenate(parts, axis=0)

                return get

            attend(qs.at[g, i], window(0), window(1), lambda r: bias[i, r], radius, attn.at[i, g])

    attn_of = lambda u, g: attn[u // 4, g] if u in (0, 4) else attn_mid[u - 1, g]
    x = jnp.concatenate([above[...], below[...]], axis=0).astype(F32)
    sums, number = block_sums(attn_of, rows, x, w_out, mod, control, west, east, slot, comb, ctl, put)
    row = lax.broadcasted_iota(jnp.int32, (64, 128), 0)
    lane = lax.broadcasted_iota(jnp.int32, (64, 128), 1)
    for at, out in ((0, up), (64, down)):
        out[:64] = sums[at : at + 64].astype(BF)
        tail = jnp.sum(jnp.where(row == lane, number[at : at + 64], 0.0), axis=0, keepdims=True)
        out[64:, :128] = jnp.broadcast_to(tail, (16, 128)).astype(BF)
        out[64:, 128:] = jnp.zeros((16, D - 128), BF)


def core_kernel(
    attn_mid, attn_edge, latent, west, east, valid, mod, w_out, control, slot, comb, ctl, put, out, rest, count, done, sem
):
    rows = valid_rows(valid, west, east)
    attn_of = lambda u, g: attn_edge[u // 4, g] if u in (0, 4) else attn_mid[u - 1, g]
    sums, number = block_sums(
        attn_of, rows, latent[...].astype(F32), w_out, mod, control, west, east, slot, comb, ctl, put
    )
    done[...] = (sums[64:192] / number[64:192]).astype(BF)
    copy = pltpu.make_async_copy(done, out.at[pl.ds(64, 128)], sem)
    copy.start()
    rest[0] = sums[:64]
    rest[1] = sums[192:]
    count[0] = jnp.broadcast_to(number[:64], (64, 128))
    count[1] = jnp.broadcast_to(number[192:], (64, 128))
    copy.wait()


def final_kernel(rest, count, above, below, whole_out, out, done, sem):
    del whole_out
    row = lax.broadcasted_iota(jnp.int32, (64, 128), 0)
    lane = lax.broadcasted_iota(jnp.int32, (64, 128), 1)
    copies = []
    for i, ref in ((0, above), (1, below)):
        tail = ref[64:80, :128].astype(F32)[:1]
        number = jnp.sum(jnp.where(row == lane, tail, 0.0), axis=1, keepdims=True) + count[i][:, :1]
        done[i] = ((rest[i] + ref[:64].astype(F32)) / number).astype(BF)
        copies.append(pltpu.make_async_copy(done.at[i], out.at[pl.ds(192 * i, 64)], sem.at[i]))
        copies[i].start()
    for copy in copies:
        copy.wait()


def call(kernel, outs, args, specs=None, out_specs=None, scratch=(), cost=(1e9, 4e6), aliases=None, limit=VMEM):
    specs = specs or {}
    out_specs = out_specs or {}
    vmem = pl.BlockSpec(memory_space=pltpu.VMEM)
    return pl.pallas_call(
        kernel,
        out_shape=outs,
        in_specs=[specs.get(i, vmem) for i in range(len(args))],
        out_specs=[out_specs.get(i, vmem) for i in range(len(outs))],
        scratch_shapes=scratch,
        input_output_aliases=aliases or {},
        compiler_params=pltpu.CompilerParams(vmem_limit_bytes=limit),
        cost_estimate=pl.CostEstimate(flops=int(cost[0]), bytes_accessed=int(cost[1]), transcendentals=0),
    )(*[jnp.asarray(a) for a in args])


def shape(*dims, dtype=BF):
    return jax.ShapeDtypeStruct(dims, dtype)


def local(latent, control, valid, radius, modulation, w_qkv, w_out):
    t = tables()
    size_r, size_c = lax.axis_size("trow"), lax.axis_size("tcol")
    later_r = [(i, i + 1) for i in range(size_r - 1)]
    sooner_r = [(i + 1, i) for i in range(size_r - 1)]
    later_c = [(i, i + 1) for i in range(size_c - 1)]
    sooner_c = [(i + 1, i) for i in range(size_c - 1)]

    x = latent.reshape(256, D)
    control = control.reshape(4, TILE_TOK, D)
    valid = valid.reshape(4, TILE_TOK)
    above = lax.ppermute(x[192:], "trow", later_r)
    below = lax.ppermute(x[:64], "trow", sooner_r)
    smem = pl.BlockSpec(memory_space=pltpu.SMEM)
    hbm = pl.BlockSpec(memory_space=pl.ANY)

    kv_own, msg = call(
        own_kernel,
        [shape(2, 2, 7, 32, D), shape(2, 96, D)],
        [x, control, valid, modulation, w_qkv, t["own"], t["send_own"], t["send_ctl"], t["valid_pad"]],
        scratch=[pltpu.VMEM((448, D), BF)],
        cost=(3.6e9, 12e6),
    )
    to_west, to_east = call(
        pack_kernel, [shape(96, D), shape(96, D)], [msg, above, below, t["send_rim"]], cost=(1e8, 1e6)
    )
    west = lax.ppermute(to_east, "tcol", later_c)
    east = lax.ppermute(to_west, "tcol", sooner_c)

    mid = slice(1, 4)
    kv_rim, attn_mid = call(
        middle_kernel,
        [shape(2, 2, 7, 16, D), shape(3, 2, D, 128)],
        [
            radius, x, above, below, valid, modulation, w_qkv, kv_own,
            t["middle"], t["dist"][mid], t["key"][mid], t["second"][mid],
        ],
        specs={0: smem},
        scratch=[
            pltpu.VMEM((992, D), BF),
            pltpu.VMEM((2, 3, 128, D), BF),
            pltpu.VMEM((3, 5, KEYS, 128), F32),
        ],
        cost=(8e9, 14e6),
    )
    ends = slice(0, 5, 4)
    up, down, attn_edge = call(
        edge_kernel,
        [shape(80, D), shape(80, D), shape(2, 2, D, 128)],
        [
            radius, x, above, below, west, east, valid, modulation, w_qkv, kv_own, kv_rim, attn_mid, w_out, control,
            t["edge"], t["dist"][ends], t["key"][ends], t["second"][ends], t["slot"], t["comb_rim"], t["ctl_rim"], t["put_rim"],
        ],
        specs={0: smem},
        scratch=[
            pltpu.VMEM((896, D), BF),
            pltpu.VMEM((2, 2, 128, D), BF),
            pltpu.VMEM((2, 2, 4, 48, D), BF),
            pltpu.VMEM((2, 5, KEYS, 128), F32),
        ],
        cost=(1e10, 16e6),
    )
    got_below = lax.ppermute(up, "trow", sooner_r)
    got_above = lax.ppermute(down, "trow", later_r)
    out, rest, count = call(
        core_kernel,
        [shape(256, D), shape(2, 64, D, dtype=F32), shape(2, 64, 128, dtype=F32)],
        [
            attn_mid, attn_edge, x, west, east, valid, modulation, w_out, control,
            t["slot"], t["comb_core"], t["ctl_core"], t["put_core"],
        ],
        out_specs={0: hbm},
        scratch=[pltpu.VMEM((128, D), BF), pltpu.SemaphoreType.DMA],
        cost=(3e9, 8e6),
    )
    (out,) = call(
        final_kernel,
        [shape(256, D)],
        [rest, count, got_above, got_below, out],
        specs={4: hbm},
        out_specs={0: hbm},
        scratch=[pltpu.VMEM((2, 64, D), BF), pltpu.SemaphoreType.DMA((2,))],
        aliases={4: 0},
        cost=(2e8, 3e6),
    )
    return out.reshape(CORE, 32, D)


def solution(mesh):
    placed = (
        P("trow", "tcol", None),
        P("trow", "tcol", None, None),
        P("trow", "tcol", None),
        P(),
        P(),
        P(),
        P(),
    )
    return jax.shard_map(
        local, mesh=mesh, in_specs=placed, out_specs=P("trow", "tcol", None), check_vma=False
    )
```

time: 204 us -> 75.1 us (0.37)
  the two profiles are of different devices: /device:TPU:103 before, /device:TPU:106 now
where the time goes in v2:
time: 75.1 us; the launch traced here: 74.5 us
  Pallas kernels  37.3 us (50%)
  starting transfers between devices  23.1 us (31%)
  local copies, waits for them, and re-layouts  11.6 us (15%)
  waiting for transfers between devices  1.92 us (3%)
    pallas_call x6, Pallas kernels, call(): pl.pallas_call(kernel, out_shape=outs, in_specs=[specs.get(i, vmem) for i...  37.3 us
    unnamed x59, local copies, waits for them, and re-layouts  10.6 us
    ppermute x1, starting transfers between devices, local(): east = lax.ppermute(to_west, 'tcol', sooner_c)  6.05 us
    ppermute x1, starting transfers between devices, local(): got_above = lax.ppermute(down, 'trow', later_r)  6.02 us
    ppermute x1, starting transfers between devices, local(): above = lax.ppermute(x[192:], 'trow', later_r)  5.01 us
    ppermute x1, starting transfers between devices, local(): got_below = lax.ppermute(up, 'trow', sooner_r)  2.14 us
    ppermute x1, starting transfers between devices, local(): below = lax.ppermute(x[:64], 'trow', sooner_r)  1.92 us
    ppermute x1, starting transfers between devices, local(): west = lax.ppermute(to_east, 'tcol', later_c)  1.92 us
  transfers between devices with their start and end apart: 6, of which 1 were waited for; matrix products, arithmetic and copies ran while one was open for 1% of the time, Pallas kernels for 30%

profile of v2, /device:TPU:106, one launch (start us, length us, event | category | flops | bytes accessed | tf_op | source)
XLA Modules:
  0.0 74.5 jit_solution(7766996124926860553)
XLA Ops:
  0.0 1.0 %fusion = (bf16[2,32,1152]{2,1,0:T(8,128)(2,1)S(1)}, bf16[2,32,1152]{2,1,0:T(8,128)(2,1)S(1)}) fusion(bf16[8,32,1152]{2,1,0:T(8,128)(2,1)} %param.27), kind=kLoop, calls=%fused_computation | loop fusion | bytes 589824 | tf_op jit(solution)/shard_map/slice | solution.py:399
  1.0 5.0 %collective-permute-start = (bf16[64,1152]{1,0:T(8,128)(2,1)S(1)}, bf16[64,1152]{1,0:T(8,128)(2,1)S(1)}, u32[]{:S(2)}, u32[]{:S(2)}) collective-permute-start(bf16[64,1152]{1,0:T(8,128)(2,1)S(1)} %bitcast.18), channel_id=1, source_target_pairs={{0,16},{16,32},{32,48},{48,64},{64,80},{80,96},{96,112},{112,128},... | collective-permute-start | bytes 442376 | tf_op jit(solution)/shard_map/ppermute | solution.py:398
  6.0 1.9 %collective-permute-start.1 = (bf16[64,1152]{1,0:T(8,128)(2,1)S(1)}, bf16[64,1152]{1,0:T(8,128)(2,1)S(1)}, u32[]{:S(2)}, u32[]{:S(2)}) collective-permute-start(bf16[64,1152]{1,0:T(8,128)(2,1)S(1)} %bitcast.17), channel_id=1, source_target_pairs={{16,0},{32,16},{48,32},{64,48},{80,64},{96,80},{112,96},{128,112},... | collective-permute-start | bytes 442376 | tf_op jit(solution)/shard_map/ppermute | solution.py:399
  8.0 0.8 %copy.30.mod = f32[2,3,1152]{2,1,0:T(4,128)S(1)} copy(f32[2,3,1152]{2,0,1:T(2,128)} %param.31) | data formatting | bytes 55296 | tf_op args[4]
  8.7 0.0 copy-start
  8.7 1.1 %copy-done = bf16[8,32,1152]{2,1,0:T(8,128)(2,1)S(1)} copy-done((bf16[8,32,1152]{2,1,0:T(8,128)(2,1)S(1)}, bf16[8,32,1152]{2,1,0:T(8,128)(2,1)}, u32[]{:S(2)}) %copy-start) | copy-done | bytes 589848
  9.8 3.3 %copy-done.3 = bf16[1152,3456]{1,0:T(8,128)(2,1)S(1)} copy-done((bf16[1152,3456]{1,0:T(8,128)(2,1)S(1)}, bf16[1152,3456]{1,0:T(8,128)(2,1)}, u32[]{:S(2)}) %copy-start.3) | copy-done | bytes 7962648
  13.0 1.3 %copy-done.6 = bf16[1,4,144,1152]{3,2,1,0:T(8,128)(2,1)S(1)} copy-done((bf16[1,4,144,1152]{3,2,1,0:T(8,128)(2,1)S(1)}, bf16[1,4,144,1152]{3,2,1,0:T(8,128)(2,1)}, u32[]{:S(2)}) %copy-start.6) | copy-done | bytes 1327128
  14.4 0.7 copy-done.8
  15.1 0.9 %copy-done.21 = bf16[224,256]{1,0:T(8,128)(2,1)S(1)} copy-done((bf16[224,256]{1,0:T(8,128)(2,1)S(1)}, bf16[224,256]{1,0:T(8,128)(2,1)}, u32[]{:S(2)}) %copy-start.21) | copy-done | bytes 114712
  16.0 0.9 %copy-done.23 = bf16[144,256]{1,0:T(8,128)(2,1)S(1)} copy-done((bf16[144,256]{1,0:T(8,128)(2,1)S(1)}, bf16[144,256]{1,0:T(8,128)(2,1)}, u32[]{:S(2)}) %copy-start.23) | copy-done | bytes 73752
  16.8 0.8 %copy-done.25 = bf16[2,64,256]{2,1,0:T(8,128)(2,1)S(1)} copy-done((bf16[2,64,256]{2,1,0:T(8,128)(2,1)S(1)}, bf16[2,64,256]{2,1,0:T(8,128)(2,1)}, u32[]{:S(2)}) %copy-start.25) | copy-done | bytes 65560
  17.7 0.8 %copy-done.26 = bf16[2,32,144]{2,1,0:T(8,128)(2,1)S(1)} copy-done((bf16[2,32,144]{2,1,0:T(8,128)(2,1)S(1)}, bf16[2,32,144]{2,1,0:T(8,128)(2,1)}, u32[]{:S(2)}) %copy-start.26) | copy-done | bytes 18456
  18.4 0.0 copy-start.10
  18.5 0.0 copy-start.14
  18.5 0.0 copy-start.19
  18.5 0.0 copy-start.27
  18.5 4.0 %shard_map.253 = (bf16[2,2,7,32,1152]{4,3,2,1,0:T(8,128)(2,1)S(1)}, bf16[2,96,1152]{2,1,0:T(8,128)(2,1)S(1)}) custom-call(bf16[256,1152]{1,0:T(8,128)(2,1)S(1)} %bitcast.6, bf16[4,144,1152]{2,1,0:T(8,128)(2,1)S(1)} %bitcast.10, s32[4,144]{1,0:T(4,128)S(1)} %bitcast.13, f32[2,3,1152]{2,1,0:T(4,128)S(1)} %copy.30.mod, bf16[1152,3456]{1,0:T(8,128)(2,1)S(1)} %copy-done.3, ...), custom_call_target="tpu_custom_call" | custom-call | flops 3600000000 | bytes 12000000 | tf_op jit(solution)/shard_map/pallas_call | solution.py:371
  22.5 0.0 collective-permute-done.above
  22.5 0.0 collective-permute-done.1.below
  22.5 0.4 shard_map.255
  22.9 1.9 %collective-permute-start.2 = (bf16[96,1152]{1,0:T(8,128)(2,1)S(1)}, bf16[96,1152]{1,0:T(8,128)(2,1)S(1)}, u32[]{:S(2)}, u32[]{:S(2)}) collective-permute-start(bf16[96,1152]{1,0:T(8,128)(2,1)S(1)} %get-tuple-element.20), channel_id=1, source_target_pairs={{0,1},{1,2},{2,3},{3,4},{4,5},{5,6},{6,7},{7,8},{8,9},{9,10},{10,1... | collective-permute-start | bytes 663560 | tf_op jit(solution)/shard_map/ppermute | solution.py:413
  24.8 6.0 %collective-permute-start.3 = (bf16[96,1152]{1,0:T(8,128)(2,1)S(1)}, bf16[96,1152]{1,0:T(8,128)(2,1)S(1)}, u32[]{:S(2)}, u32[]{:S(2)}) collective-permute-start(bf16[96,1152]{1,0:T(8,128)(2,1)S(1)} %get-tuple-element.21), channel_id=1, source_target_pairs={{1,0},{2,1},{3,2},{4,3},{5,4},{6,5},{7,6},{8,7},{9,8},{10,9},{11,1... | collective-permute-start | bytes 663560 | tf_op jit(solution)/shard_map/ppermute | solution.py:414
  30.9 0.0 copy-start.5
  30.9 0.0 copy-start.7
  30.9 0.0 copy-start.11
  31.0 0.0 copy-start.13
  31.0 0.0 copy-start.15
  31.0 0.0 copy-start.17
  31.0 0.0 copy-start.18
  31.0 0.0 copy-start.22
  31.0 0.0 copy-start.24
  31.0 0.0 copy-start.28
  31.1 13.0 %shard_map.254 = (bf16[2,2,7,16,1152]{4,3,2,1,0:T(8,128)(2,1)S(1)}, bf16[3,2,1152,128]{3,2,1,0:T(8,128)(2,1)S(1)}) custom-call(s32[16]{0:T(128)S(1)} %copy-done.9, bf16[256,1152]{1,0:T(8,128)(2,1)S(1)} %bitcast.7, bf16[64,1152]{1,0:T(8,128)(2,1)S(1)} %collective-permute-done.above, bf16[64,1152]{1,0:T(8,128)(2,1)S(1)} %collective-permute-done.1.below, ...), custom_call_target="tpu_custom_call" | custom-call | flops 8000000000 | bytes 14000000 | tf_op jit(solution)/shard_map/pallas_call | solution.py:371
  44.1 0.0 collective-permute-done.2.west
  44.1 0.0 collective-permute-done.3.east
  44.1 0.0 copy-done.5
  44.1 0.0 copy-done.7
  44.2 0.0 copy-start.12
  44.2 0.0 copy-start.16
  44.2 0.0 copy-start.20
  44.2 13.6 %shard_map.256 = (bf16[80,1152]{1,0:T(8,128)(2,1)S(1)}, bf16[80,1152]{1,0:T(8,128)(2,1)S(1)}, bf16[2,2,1152,128]{3,2,1,0:T(8,128)(2,1)S(1)}) custom-call(s32[16]{0:T(128)S(1)} %copy-done.9, bf16[256,1152]{1,0:T(8,128)(2,1)S(1)} %bitcast.8, bf16[64,1152]{1,0:T(8,128)(2,1)S(1)} %collective-permute-done.above, ...), custom_call_target="tpu_custom_call" | custom-call | flops 10000000000 | bytes 16000000 | tf_op jit(solution)/shard_map/pallas_call | solution.py:371
  57.8 6.0 %collective-permute-start.4 = (bf16[80,1152]{1,0:T(8,128)(2,1)S(1)}, bf16[80,1152]{1,0:T(8,128)(2,1)S(1)}, u32[]{:S(2)}, u32[]{:S(2)}) collective-permute-start(bf16[80,1152]{1,0:T(8,128)(2,1)S(1)} %get-tuple-element.26), channel_id=1, source_target_pairs={{0,16},{16,32},{32,48},{48,64},{64,80},{80,96},{96,112},{112,128},... | collective-permute-start | bytes 552968 | tf_op jit(solution)/shard_map/ppermute | solution.py:450
  63.8 2.1 %collective-permute-start.5 = (bf16[80,1152]{1,0:T(8,128)(2,1)S(1)}, bf16[80,1152]{1,0:T(8,128)(2,1)S(1)}, u32[]{:S(2)}, u32[]{:S(2)}) collective-permute-start(bf16[80,1152]{1,0:T(8,128)(2,1)S(1)} %get-tuple-element.27), channel_id=1, source_target_pairs={{16,0},{32,16},{48,32},{64,48},{80,64},{96,80},{112,96},{128,112},... | collective-permute-start | bytes 552968 | tf_op jit(solution)/shard_map/ppermute | solution.py:449
  66.0 5.4 %shard_map.257 = (bf16[256,1152]{1,0:T(8,128)(2,1)}, f32[2,64,1152]{2,1,0:T(8,128)S(1)}, f32[2,64,128]{2,1,0:T(8,128)S(1)}) custom-call(bf16[3,2,1152,128]{3,2,1,0:T(8,128)(2,1)S(1)} %get-tuple-element.18.attn_mid, bf16[2,2,1152,128]{3,2,1,0:T(8,128)(2,1)S(1)} %get-tuple-element.23.attn_edge, bf16[256,1152]{1,0:T(8,128)(2,1)S(1)} %bitcast.9, ...), custom_call_target="tpu_custom_call" | custom-call | flops 3000000000 | bytes 8000000 | tf_op jit(solution)/shard_map/pallas_call | solution.py:371
  71.5 0.0 collective-permute-done.4.above
  71.5 1.9 %collective-permute-done.5.below = bf16[80,1152]{1,0:T(8,128)(2,1)S(1)} collective-permute-done((bf16[80,1152]{1,0:T(8,128)(2,1)S(1)}, bf16[80,1152]{1,0:T(8,128)(2,1)S(1)}, u32[]{:S(2)}, u32[]{:S(2)}) %collective-permute-start.5) | collective-permute-done | bytes 184352 | tf_op jit(solution)/shard_map/ppermute | solution.py:449
  73.4 0.9 %shard_map.258 = bf16[256,1152]{1,0:T(8,128)(2,1)} custom-call(f32[2,64,1152]{2,1,0:T(8,128)S(1)} %get-tuple-element.24.rest, f32[2,64,128]{2,1,0:T(8,128)S(1)} %get-tuple-element.25.count, bf16[80,1152]{1,0:T(8,128)(2,1)S(1)} %collective-permute-done.4.above, bf16[80,1152]{1,0:T(8,128)(2,1)S(1)} %collective-permute-done.5.below, ...), custom_call_target="tpu_custom_call", output_to_operand_aliasing={{}: (4, {})} | custom-call | flops 200000000 | bytes 3000000 | tf_op jit(solution)/shard_map/pallas_call | solution.py:371
  (30 shorter events, 0.1 us)
Async XLA Ops:
  1.0 21.5 %collective-permute-start = (bf16[64,1152]{1,0:T(8,128)(2,1)S(1)}, bf16[64,1152]{1,0:T(8,128)(2,1)S(1)}, u32[]{:S(2)}, u32[]{:S(2)}) collective-permute-start(bf16[64,1152]{1,0:T(8,128)(2,1)S(1)} %bitcast.18), channel_id=1, source_target_pairs={{0,16},{16,32},{32,48},{48,64},{64,80},{80,96},{96,112},{112,128},... | collective-permute-start | bytes 442376 | tf_op jit(solution)/shard_map/ppermute | solution.py:398
  6.0 16.5 %collective-permute-start.1 = (bf16[64,1152]{1,0:T(8,128)(2,1)S(1)}, bf16[64,1152]{1,0:T(8,128)(2,1)S(1)}, u32[]{:S(2)}, u32[]{:S(2)}) collective-permute-start(bf16[64,1152]{1,0:T(8,128)(2,1)S(1)} %bitcast.17), channel_id=1, source_target_pairs={{16,0},{32,16},{48,32},{64,48},{80,64},{96,80},{112,96},{128,112},... | collective-permute-start | bytes 442376 | tf_op jit(solution)/shard_map/ppermute | solution.py:399
  8.7 1.1 %copy-start = (bf16[8,32,1152]{2,1,0:T(8,128)(2,1)S(1)}, bf16[8,32,1152]{2,1,0:T(8,128)(2,1)}, u32[]{:S(2)}) copy-start(bf16[8,32,1152]{2,1,0:T(8,128)(2,1)} %param.27) | copy-start | bytes 1769476
  9.8 3.3 %copy-start.3 = (bf16[1152,3456]{1,0:T(8,128)(2,1)S(1)}, bf16[1152,3456]{1,0:T(8,128)(2,1)}, u32[]{:S(2)}) copy-start(bf16[1152,3456]{1,0:T(8,128)(2,1)} %w.5) | copy-start | bytes 23887876
  13.0 1.3 %copy-start.6 = (bf16[1,4,144,1152]{3,2,1,0:T(8,128)(2,1)S(1)}, bf16[1,4,144,1152]{3,2,1,0:T(8,128)(2,1)}, u32[]{:S(2)}) copy-start(bf16[1,4,144,1152]{3,2,1,0:T(8,128)(2,1)} %param.28) | copy-start | bytes 3981316
  14.4 0.7 copy-start.8
  15.1 0.9 %copy-start.21 = (bf16[224,256]{1,0:T(8,128)(2,1)S(1)}, bf16[224,256]{1,0:T(8,128)(2,1)}, u32[]{:S(2)}) copy-start(bf16[224,256]{1,0:T(8,128)(2,1)} %constant.40.clone.own) | copy-start | bytes 344068
  16.0 0.9 %copy-start.23 = (bf16[144,256]{1,0:T(8,128)(2,1)S(1)}, bf16[144,256]{1,0:T(8,128)(2,1)}, u32[]{:S(2)}) copy-start(bf16[144,256]{1,0:T(8,128)(2,1)} %constant.43.clone.valid_pad) | copy-start | bytes 221188
  16.8 0.8 %copy-start.25 = (bf16[2,64,256]{2,1,0:T(8,128)(2,1)S(1)}, bf16[2,64,256]{2,1,0:T(8,128)(2,1)}, u32[]{:S(2)}) copy-start(bf16[2,64,256]{2,1,0:T(8,128)(2,1)} %constant.41.clone.send_own) | copy-start | bytes 196612
  17.7 0.8 %copy-start.26 = (bf16[2,32,144]{2,1,0:T(8,128)(2,1)S(1)}, bf16[2,32,144]{2,1,0:T(8,128)(2,1)}, u32[]{:S(2)}) copy-start(bf16[2,32,144]{2,1,0:T(8,128)(2,1)} %constant.42.clone.send_ctl) | copy-start | bytes 55300
  18.4 4.1 %copy-start.2 = (bf16[2,64,128]{2,1,0:T(8,128)(2,1)S(1)}, bf16[2,64,128]{2,1,0:T(8,128)(2,1)}, u32[]{:S(2)}) copy-start(bf16[2,64,128]{2,1,0:T(8,128)(2,1)} %constant.44.clone.send_rim) | copy-start | bytes 98308
  18.4 12.4 %copy-start.1 = (bf16[8,32,1152]{2,1,0:T(8,128)(2,1)S(1)}, bf16[8,32,1152]{2,1,0:T(8,128)(2,1)}, u32[]{:S(2)}) copy-start(bf16[8,32,1152]{2,1,0:T(8,128)(2,1)} %param.27) | copy-start | bytes 1769476
  18.4 12.4 %copy-start.4 = (bf16[1152,3456]{1,0:T(8,128)(2,1)S(1)}, bf16[1152,3456]{1,0:T(8,128)(2,1)}, u32[]{:S(2)}) copy-start(bf16[1152,3456]{1,0:T(8,128)(2,1)} %w.5) | copy-start | bytes 23887876
  18.4 12.4 %copy-start.9 = (s32[16]{0:T(128)S(1)}, s32[16]{0:T(128)}, u32[]{:S(2)}) copy-start(s32[16]{0:T(128)} %radius.3) | copy-start | bytes 196
  18.4 12.4 %copy-start.10 = (bf16[3,2,192,144]{3,2,1,0:T(8,128)(2,1)S(1)}, bf16[3,2,192,144]{3,2,1,0:T(8,128)(2,1)}, u32[]{:S(2)}) copy-start(bf16[3,2,192,144]{3,2,1,0:T(8,128)(2,1)} %constant.47.clone.key) | copy-start | bytes 995332
  18.5 12.4 %copy-start.14 = (bf16[496,384]{1,0:T(8,128)(2,1)S(1)}, bf16[496,384]{1,0:T(8,128)(2,1)}, u32[]{:S(2)}) copy-start(bf16[496,384]{1,0:T(8,128)(2,1)} %constant.45.clone.middle) | copy-start | bytes 1142788
  18.5 12.4 %copy-start.19 = (bf16[3,192,128]{2,1,0:T(8,128)(2,1)S(1)}, bf16[3,192,128]{2,1,0:T(8,128)(2,1)}, u32[]{:S(2)}) copy-start(bf16[3,192,128]{2,1,0:T(8,128)(2,1)} %constant.46.clone.dist) | copy-start | bytes 442372
  18.5 12.4 %copy-start.27 = (f32[3,1,128]{2,1,0:T(1,128)S(1)}, f32[3,1,128]{2,1,0:T(1,128)}, u32[]{:S(2)}) copy-start(f32[3,1,128]{2,1,0:T(1,128)} %constant.48.clone.second) | copy-start | bytes 4612
  22.9 21.2 %collective-permute-start.2 = (bf16[96,1152]{1,0:T(8,128)(2,1)S(1)}, bf16[96,1152]{1,0:T(8,128)(2,1)S(1)}, u32[]{:S(2)}, u32[]{:S(2)}) collective-permute-start(bf16[96,1152]{1,0:T(8,128)(2,1)S(1)} %get-tuple-element.20), channel_id=1, source_target_pairs={{0,1},{1,2},{2,3},{3,4},{4,5},{5,6},{6,7},{7,8},{8,9},{9,10},{10,1... | collective-permute-start | bytes 663560 | tf_op jit(solution)/shard_map/ppermute | solution.py:413
  24.8 19.3 %collective-permute-start.3 = (bf16[96,1152]{1,0:T(8,128)(2,1)S(1)}, bf16[96,1152]{1,0:T(8,128)(2,1)S(1)}, u32[]{:S(2)}, u32[]{:S(2)}) collective-permute-start(bf16[96,1152]{1,0:T(8,128)(2,1)S(1)} %get-tuple-element.21), channel_id=1, source_target_pairs={{1,0},{2,1},{3,2},{4,3},{5,4},{6,5},{7,6},{8,7},{9,8},{10,9},{11,1... | collective-permute-start | bytes 663560 | tf_op jit(solution)/shard_map/ppermute | solution.py:414
  30.9 13.2 %copy-start.5 = (bf16[1152,1152]{1,0:T(8,128)(2,1)S(1)}, bf16[1152,1152]{1,0:T(8,128)(2,1)}, u32[]{:S(2)}) copy-start(bf16[1152,1152]{1,0:T(8,128)(2,1)} %w_out.3) | copy-start | bytes 7962628
  30.9 13.2 %copy-start.7 = (bf16[1,4,144,1152]{3,2,1,0:T(8,128)(2,1)S(1)}, bf16[1,4,144,1152]{3,2,1,0:T(8,128)(2,1)}, u32[]{:S(2)}) copy-start(bf16[1,4,144,1152]{3,2,1,0:T(8,128)(2,1)} %param.28) | copy-start | bytes 3981316
  30.9 13.2 %copy-start.11 = (bf16[448,576]{1,0:T(8,128)(2,1)S(1)}, bf16[448,576]{1,0:T(8,128)(2,1)}, u32[]{:S(2)}) copy-start(bf16[448,576]{1,0:T(8,128)(2,1)} %constant.49.clone.edge) | copy-start | bytes 1548292
  31.0 13.2 %copy-start.13 = (bf16[2,2,192,144]{3,2,1,0:T(8,128)(2,1)S(1)}, bf16[2,2,192,144]{3,2,1,0:T(8,128)(2,1)}, u32[]{:S(2)}) copy-start(bf16[2,2,192,144]{3,2,1,0:T(8,128)(2,1)} %constant.51.clone.key) | copy-start | bytes 663556
  31.0 13.2 %copy-start.15 = (bf16[5,2,144,128]{3,2,1,0:T(8,128)(2,1)S(1)}, bf16[5,2,144,128]{3,2,1,0:T(8,128)(2,1)}, u32[]{:S(2)}) copy-start(bf16[5,2,144,128]{3,2,1,0:T(8,128)(2,1)} %constant.53.clone.slot) | copy-start | bytes 1105924
  31.0 13.2 %copy-start.17 = (bf16[4,128,144]{2,1,0:T(8,128)(2,1)S(1)}, bf16[4,128,144]{2,1,0:T(8,128)(2,1)}, u32[]{:S(2)}) copy-start(bf16[4,128,144]{2,1,0:T(8,128)(2,1)} %constant.55.clone.ctl) | copy-start | bytes 442372
  31.0 13.2 %copy-start.18 = (bf16[5,128,128]{2,1,0:T(8,128)(2,1)S(1)}, bf16[5,128,128]{2,1,0:T(8,128)(2,1)}, u32[]{:S(2)}) copy-start(bf16[5,128,128]{2,1,0:T(8,128)(2,1)} %constant.54.clone.comb) | copy-start | bytes 491524
  31.0 13.2 %copy-start.22 = (bf16[2,192,128]{2,1,0:T(8,128)(2,1)S(1)}, bf16[2,192,128]{2,1,0:T(8,128)(2,1)}, u32[]{:S(2)}) copy-start(bf16[2,192,128]{2,1,0:T(8,128)(2,1)} %constant.50.clone.dist) | copy-start | bytes 294916
  31.0 13.1 %copy-start.24 = (bf16[2,128,32]{2,1,0:T(8,128)(2,1)S(1)}, bf16[2,128,32]{2,1,0:T(8,128)(2,1)}, u32[]{:S(2)}) copy-start(bf16[2,128,32]{2,1,0:T(8,128)(2,1)} %constant.56.clone.put) | copy-start | bytes 49156
  31.0 13.1 %copy-start.28 = (f32[2,1,128]{2,1,0:T(1,128)S(1)}, f32[2,1,128]{2,1,0:T(1,128)}, u32[]{:S(2)}) copy-start(f32[2,1,128]{2,1,0:T(1,128)} %constant.52.clone.second) | copy-start | bytes 3076
  44.2 21.8 %copy-start.12 = (bf16[4,256,144]{2,1,0:T(8,128)(2,1)S(1)}, bf16[4,256,144]{2,1,0:T(8,128)(2,1)}, u32[]{:S(2)}) copy-start(bf16[4,256,144]{2,1,0:T(8,128)(2,1)} %constant.58.clone.ctl) | copy-start | bytes 884740
  44.2 21.8 %copy-start.16 = (bf16[5,256,128]{2,1,0:T(8,128)(2,1)S(1)}, bf16[5,256,128]{2,1,0:T(8,128)(2,1)}, u32[]{:S(2)}) copy-start(bf16[5,256,128]{2,1,0:T(8,128)(2,1)} %constant.57.clone.comb) | copy-start | bytes 983044
  44.2 21.8 %copy-start.20 = (bf16[2,256,32]{2,1,0:T(8,128)(2,1)S(1)}, bf16[2,256,32]{2,1,0:T(8,128)(2,1)}, u32[]{:S(2)}) copy-start(bf16[2,256,32]{2,1,0:T(8,128)(2,1)} %constant.59.clone.put) | copy-start | bytes 98308
  57.8 13.7 %collective-permute-start.4 = (bf16[80,1152]{1,0:T(8,128)(2,1)S(1)}, bf16[80,1152]{1,0:T(8,128)(2,1)S(1)}, u32[]{:S(2)}, u32[]{:S(2)}) collective-permute-start(bf16[80,1152]{1,0:T(8,128)(2,1)S(1)} %get-tuple-element.26), channel_id=1, source_target_pairs={{0,16},{16,32},{32,48},{48,64},{64,80},{80,96},{96,112},{112,128},... | collective-permute-start | bytes 552968 | tf_op jit(solution)/shard_map/ppermute | solution.py:450
  63.8 9.5 %collective-permute-start.5 = (bf16[80,1152]{1,0:T(8,128)(2,1)S(1)}, bf16[80,1152]{1,0:T(8,128)(2,1)S(1)}, u32[]{:S(2)}, u32[]{:S(2)}) collective-permute-start(bf16[80,1152]{1,0:T(8,128)(2,1)S(1)} %get-tuple-element.27), channel_id=1, source_target_pairs={{16,0},{32,16},{48,32},{64,48},{80,64},{96,80},{112,96},{128,112},... | collective-permute-start | bytes 552968 | tf_op jit(solution)/shard_map/ppermute | solution.py:449

commit v3 on v2

--- a/solution.py
+++ b/solution.py
@@ -150,7 +150,7 @@
     centred = x - mean
     var = jnp.mean(centred * centred, axis=-1, keepdims=True)
     normed = centred * lax.rsqrt(var + 1e-6)
-    return [(normed * (1.0 + mod_ref[g, 1:2, :]) + mod_ref[g, 0:1, :]).astype(BF) for g in (0, 1)]
+    return [(normed * (1.0 + mod_ref[1, g : g + 1, :]) + mod_ref[0, g : g + 1, :]).astype(BF) for g in (0, 1)]
 
 
 def eight(row):
@@ -203,20 +203,45 @@
     return get
 
 
-def own_kernel(latent, control, valid, mod, w, own, send_own, send_ctl, valid_pad, kv, msg, hid):
+def own_kernel(
+    latent_h, control_h, valid_h, mod_h, w_h, own_h, send_own_h, send_ctl_h, valid_pad_h,
+    kv, msg, w, latent, control, valid, mod, own, send_own, send_ctl, valid_pad, hid, sem,
+):
+    pairs = [
+        (latent_h, latent),
+        (own_h, own),
+        (mod_h, mod),
+        (w_h.at[:, pl.ds(D, D)], w.at[:, pl.ds(D, D)]),
+        (w_h.at[:, pl.ds(2 * D, D)], w.at[:, pl.ds(2 * D, D)]),
+        (control_h.at[pl.ds(0, 1)], control.at[pl.ds(0, 1)]),
+        (control_h.at[pl.ds(3, 1)], control.at[pl.ds(1, 1)]),
+        (valid_h, valid),
+        (send_own_h, send_own),
+        (send_ctl_h, send_ctl),
+        (valid_pad_h, valid_pad),
+        (w_h.at[:, pl.ds(0, D)], w.at[:, pl.ds(0, D)]),
+    ]
+    copies = [pltpu.make_async_copy(src, dst, sem.at[i]) for i, (src, dst) in enumerate(pairs)]
+    for copy in copies:
+        copy.start()
+    for copy in copies[:3]:
+        copy.wait()
     rows = hidden_rows(dot(own[...], latent[...]), mod)
     hid[:224] = rows[0]
     hid[224:] = rows[1]
     for c in (0, 1):
+        copies[3 + c].wait()
         out = dot(hid[...], w[:, (c + 1) * D : (c + 2) * D])
         kv[c] = out.astype(BF).reshape(2, 7, 32, D)
+    for copy in copies[5:]:
+        copy.wait()
     rows = lax.broadcasted_iota(jnp.int32, (32, 1), 0)
     val = valid[...].astype(F32)
-    for i, tile in ((0, 0), (1, 3)):
+    for i, tile, rim in ((0, 0, 2 * SIDE + 1), (1, 3, 2 * SIDE + 10)):
         msg[i, :64] = dot(send_own[i], latent[...]).astype(BF)
-        hot = (send_ctl[i].astype(F32) * val[tile : tile + 1]).astype(BF)
-        ctl = dot(hot, control[tile])
-        row = dot(eight(val[tile : tile + 1]), valid_pad[...])
+        own_row = val[tile : tile + 1]
+        ctl = dot((send_ctl[i].astype(F32) * own_row).astype(BF), control[i])
+        row = dot(eight(own_row * own_row[:, rim : rim + 1]), valid_pad[...])
         msg[i, 64:, 256:] = ctl[:, 256:].astype(BF)
         msg[i, 64:, :256] = jnp.where(rows == 31, row[0:1], ctl[:, :256]).astype(BF)
 
@@ -274,7 +299,7 @@
     n = number.shape[0]
     attn = [sum(dot_nt(weights[u].astype(BF), attn_of(u, g)) for u in range(5)).astype(BF) for g in (0, 1)]
     proj = dot(jnp.concatenate(attn, axis=0), w_out[...])
-    sums = (GUIDE * mod[0, 2:3]) * proj[:n] + ((1.0 - GUIDE) * mod[1, 2:3]) * proj[n:] + number * x
+    sums = (GUIDE * mod[2, 0:1]) * proj[:n] + ((1.0 - GUIDE) * mod[2, 1:2]) * proj[n:] + number * x
     for tile in range(4):
         sums = sums + dot((ctl[tile].astype(F32) * rows[tile + 1]).astype(BF), control[tile])
     return sums + dot(put[0], west[64:]) + dot(put[1], east[64:]), number
@@ -387,10 +412,10 @@
 def local(latent, control, valid, radius, modulation, w_qkv, w_out):
     t = tables()
     size_r, size_c = lax.axis_size("trow"), lax.axis_size("tcol")
-    later_r = [(i, i + 1) for i in range(size_r - 1)]
-    sooner_r = [(i + 1, i) for i in range(size_r - 1)]
-    later_c = [(i, i + 1) for i in range(size_c - 1)]
-    sooner_c = [(i + 1, i) for i in range(size_c - 1)]
+    later_r = [(i, (i + 1) % size_r) for i in range(size_r)]
+    sooner_r = [((i + 1) % size_r, i) for i in range(size_r)]
+    later_c = [(i, (i + 1) % size_c) for i in range(size_c)]
+    sooner_c = [((i + 1) % size_c, i) for i in range(size_c)]
 
     x = latent.reshape(256, D)
     control = control.reshape(4, TILE_TOK, D)
@@ -400,11 +425,18 @@
     smem = pl.BlockSpec(memory_space=pltpu.SMEM)
     hbm = pl.BlockSpec(memory_space=pl.ANY)
 
-    kv_own, msg = call(
+    mod = modulation.transpose(1, 0, 2)
+    far = lambda a: pltpu.with_memory_space_constraint(jnp.asarray(a), pltpu.MemorySpace.HBM)
+    first = [x, control, valid, mod, w_qkv, t["own"], t["send_own"], t["send_ctl"], t["valid_pad"]]
+    staged = [(256, D, BF), (2, TILE_TOK, D, BF), (4, TILE_TOK, jnp.int32), (3, 2, D, F32)]
+    staged += [t[k].shape + (BF,) for k in ("own", "send_own", "send_ctl", "valid_pad")]
+    kv_own, msg, w = call(
         own_kernel,
-        [shape(2, 2, 7, 32, D), shape(2, 96, D)],
-        [x, control, valid, modulation, w_qkv, t["own"], t["send_own"], t["send_ctl"], t["valid_pad"]],
-        scratch=[pltpu.VMEM((448, D), BF)],
+        [shape(2, 2, 7, 32, D), shape(2, 96, D), shape(D, 3 * D)],
+        [far(a) for a in first],
+        specs={i: hbm for i in range(len(first))},
+        scratch=[pltpu.VMEM(s[:-1], s[-1]) for s in staged]
+        + [pltpu.VMEM((448, D), BF), pltpu.SemaphoreType.DMA((12,))],
         cost=(3.6e9, 12e6),
     )
     to_west, to_east = call(
@@ -418,7 +450,7 @@
         middle_kernel,
         [shape(2, 2, 7, 16, D), shape(3, 2, D, 128)],
         [
-            radius, x, above, below, valid, modulation, w_qkv, kv_own,
+            radius, x, above, below, valid, mod, w, kv_own,
             t["middle"], t["dist"][mid], t["key"][mid], t["second"][mid],
         ],
         specs={0: smem},
@@ -434,7 +466,7 @@
         edge_kernel,
         [shape(80, D), shape(80, D), shape(2, 2, D, 128)],
         [
-            radius, x, above, below, west, east, valid, modulation, w_qkv, kv_own, kv_rim, attn_mid, w_out, control,
+            radius, x, above, below, west, east, valid, mod, w, kv_own, kv_rim, attn_mid, w_out, control,
             t["edge"], t["dist"][ends], t["key"][ends], t["second"][ends], t["slot"], t["comb_rim"], t["ctl_rim"], t["put_rim"],
         ],
         specs={0: smem},
@@ -452,7 +484,7 @@
         core_kernel,
         [shape(256, D), shape(2, 64, D, dtype=F32), shape(2, 64, 128, dtype=F32)],
         [
-            attn_mid, attn_edge, x, west, east, valid, modulation, w_out, control,
+            attn_mid, attn_edge, x, west, east, valid, mod, w_out, control,
             t["slot"], t["comb_core"], t["ctl_core"], t["put_core"],
         ],
         out_specs={0: hbm},

time: 75.1 us -> 56.9 us (0.76)
  the two profiles are of different devices: /device:TPU:106 before, /device:TPU:8 now
where the time goes in v3:
time: 56.9 us; the launch traced here: 56.8 us
  Pallas kernels  39.7 us (70%)
  starting transfers between devices  15.4 us (27%)
  local copies, waits for them, and re-layouts  1.14 us (2%)
    pallas_call x6, Pallas kernels, call(): pl.pallas_call(kernel, out_shape=outs, in_specs=[specs.get(i, vmem) for i...  39.7 us
    ppermute x1, starting transfers between devices, local(): below = lax.ppermute(x[:64], 'trow', sooner_r)  5.38 us
    ppermute x1, starting transfers between devices, local(): east = lax.ppermute(to_west, 'tcol', sooner_c)  4.14 us
    ppermute x1, starting transfers between devices, local(): got_below = lax.ppermute(up, 'trow', sooner_r)  4.12 us
    ppermute x1, starting transfers between devices, local(): above = lax.ppermute(x[192:], 'trow', later_r)  1.57 us
  transfers between devices with their start and end apart: 6, of which 0 were waited for; matrix products, arithmetic and copies ran while one was open for 0% of the time, Pallas kernels for 44%

profile of v3, /device:TPU:8, one launch (start us, length us, event | category | flops | bytes accessed | tf_op | source)
XLA Modules:
  0.0 56.8 jit_solution(1909752123918078459)
XLA Ops:
  0.0 1.0 %fusion = (bf16[2,32,1152]{2,1,0:T(8,128)(2,1)S(1)}, bf16[2,32,1152]{2,1,0:T(8,128)(2,1)S(1)}) fusion(bf16[8,32,1152]{2,1,0:T(8,128)(2,1)} %param.27), kind=kLoop, calls=%fused_computation | loop fusion | bytes 589824 | tf_op jit(solution)/shard_map/slice | solution.py:424
  1.0 1.6 %collective-permute-start = (bf16[64,1152]{1,0:T(8,128)(2,1)S(1)}, bf16[64,1152]{1,0:T(8,128)(2,1)S(1)}, u32[]{:S(2)}, u32[]{:S(2)}) collective-permute-start(bf16[64,1152]{1,0:T(8,128)(2,1)S(1)} %bitcast.23), channel_id=1, source_target_pairs={{0,16},{16,32},{32,48},{48,64},{64,80},{80,96},{96,112},{112,128},... | collective-permute-start | bytes 442376 | tf_op jit(solution)/shard_map/ppermute | solution.py:423
  2.6 5.4 %collective-permute-start.1 = (bf16[64,1152]{1,0:T(8,128)(2,1)S(1)}, bf16[64,1152]{1,0:T(8,128)(2,1)S(1)}, u32[]{:S(2)}, u32[]{:S(2)}) collective-permute-start(bf16[64,1152]{1,0:T(8,128)(2,1)S(1)} %bitcast.22), channel_id=1, source_target_pairs={{16,0},{32,16},{48,32},{64,48},{80,64},{96,80},{112,96},{128,112},... | collective-permute-start | bytes 442376 | tf_op jit(solution)/shard_map/ppermute | solution.py:424
  8.0 0.0 copy-start.6
  8.0 0.0 copy-start.7
  8.0 0.0 copy-start.11
  8.0 0.0 copy-start.16
  8.0 0.0 copy-start.20
  8.0 6.3 %shard_map.253 = (bf16[2,2,7,32,1152]{4,3,2,1,0:T(8,128)(2,1)S(1)}, bf16[2,96,1152]{2,1,0:T(8,128)(2,1)S(1)}, bf16[1152,3456]{1,0:T(8,128)(2,1)S(1)}) custom-call(bf16[256,1152]{1,0:T(8,128)(2,1)} %bitcast.7, bf16[4,144,1152]{2,1,0:T(8,128)(2,1)} %bitcast.11, s32[4,144]{1,0:T(4,128)} %bitcast.18, f32[3,2,1152]{2,1,0:T(2,128)} %bitcast.14, ...), custom_call_target="tpu_custom_call" | custom-call | flops 3600000000 | bytes 12000000 | tf_op jit(solution)/shard_map/pallas_call | solution.py:396
  14.4 0.0 collective-permute-done.above
  14.4 0.0 collective-permute-done.1.below
  14.4 0.0 copy-done.1
  14.4 0.4 shard_map.255
  14.8 0.1 collective-permute-start.2
  14.9 4.1 %collective-permute-start.3 = (bf16[96,1152]{1,0:T(8,128)(2,1)S(1)}, bf16[96,1152]{1,0:T(8,128)(2,1)S(1)}, u32[]{:S(2)}, u32[]{:S(2)}) collective-permute-start(bf16[96,1152]{1,0:T(8,128)(2,1)S(1)} %get-tuple-element.23), channel_id=1, source_target_pairs={{1,0},{2,1},{3,2},{4,3},{5,4},{6,5},{7,6},{8,7},{9,8},{10,9},{11,1... | collective-permute-start | bytes 663560 | tf_op jit(solution)/shard_map/ppermute | solution.py:446
  19.0 0.0 copy-done
  19.0 0.0 copy-done.4
  19.0 0.0 copy-done.5
  19.0 0.0 copy-done.6
  19.0 0.0 copy-done.7
  19.0 0.0 copy-done.11
  19.0 0.0 copy-done.16
  19.1 0.0 copy-done.20
  19.1 0.0 copy-start.2
  19.1 0.0 copy-start.3
  19.1 0.0 copy-start.8
  19.1 0.0 copy-start.10
  19.1 0.0 copy-start.12
  19.1 0.0 copy-start.14
  19.1 0.0 copy-start.15
  19.2 0.0 copy-start.18
  19.2 0.0 copy-start.19
  19.2 0.0 copy-start.21
  19.2 13.0 %shard_map.254 = (bf16[2,2,7,16,1152]{4,3,2,1,0:T(8,128)(2,1)S(1)}, bf16[3,2,1152,128]{3,2,1,0:T(8,128)(2,1)S(1)}) custom-call(s32[16]{0:T(128)S(1)} %copy-done.6, bf16[256,1152]{1,0:T(8,128)(2,1)S(1)} %bitcast.8, bf16[64,1152]{1,0:T(8,128)(2,1)S(1)} %collective-permute-done.above, bf16[64,1152]{1,0:T(8,128)(2,1)S(1)} %collective-permute-done.1.below, ...), custom_call_target="tpu_custom_call" | custom-call | flops 8000000000 | bytes 14000000 | tf_op jit(solution)/shard_map/pallas_call | solution.py:396
  32.2 0.0 collective-permute-done.2.west
  32.2 0.0 collective-permute-done.3.east
  32.2 0.0 copy-done.2
  32.2 0.0 copy-done.3
  32.3 0.0 copy-start.9
  32.3 0.0 copy-start.13
  32.3 0.0 copy-start.17
  32.4 13.6 %shard_map.256 = (bf16[80,1152]{1,0:T(8,128)(2,1)S(1)}, bf16[80,1152]{1,0:T(8,128)(2,1)S(1)}, bf16[2,2,1152,128]{3,2,1,0:T(8,128)(2,1)S(1)}) custom-call(s32[16]{0:T(128)S(1)} %copy-done.6, bf16[256,1152]{1,0:T(8,128)(2,1)S(1)} %bitcast.9, bf16[64,1152]{1,0:T(8,128)(2,1)S(1)} %collective-permute-done.above, ...), custom_call_target="tpu_custom_call" | custom-call | flops 10000000000 | bytes 16000000 | tf_op jit(solution)/shard_map/pallas_call | solution.py:396
  45.9 0.1 collective-permute-start.4
  46.0 4.1 %collective-permute-start.5 = (bf16[80,1152]{1,0:T(8,128)(2,1)S(1)}, bf16[80,1152]{1,0:T(8,128)(2,1)S(1)}, u32[]{:S(2)}, u32[]{:S(2)}) collective-permute-start(bf16[80,1152]{1,0:T(8,128)(2,1)S(1)} %get-tuple-element.29), channel_id=1, source_target_pairs={{16,0},{32,16},{48,32},{64,48},{80,64},{96,80},{112,96},{128,112},... | collective-permute-start | bytes 552968 | tf_op jit(solution)/shard_map/ppermute | solution.py:481
  50.2 5.5 %shard_map.257 = (bf16[256,1152]{1,0:T(8,128)(2,1)}, f32[2,64,1152]{2,1,0:T(8,128)S(1)}, f32[2,64,128]{2,1,0:T(8,128)S(1)}) custom-call(bf16[3,2,1152,128]{3,2,1,0:T(8,128)(2,1)S(1)} %get-tuple-element.20.attn_mid, bf16[2,2,1152,128]{3,2,1,0:T(8,128)(2,1)S(1)} %get-tuple-element.25.attn_edge, bf16[256,1152]{1,0:T(8,128)(2,1)S(1)} %bitcast.10, ...), custom_call_target="tpu_custom_call" | custom-call | flops 3000000000 | bytes 8000000 | tf_op jit(solution)/shard_map/pallas_call | solution.py:396
  55.6 0.0 collective-permute-done.4.above
  55.6 0.0 collective-permute-done.5.below
  55.7 0.9 %shard_map.258 = bf16[256,1152]{1,0:T(8,128)(2,1)} custom-call(f32[2,64,1152]{2,1,0:T(8,128)S(1)} %get-tuple-element.26.rest, f32[2,64,128]{2,1,0:T(8,128)S(1)} %get-tuple-element.27.count, bf16[80,1152]{1,0:T(8,128)(2,1)S(1)} %collective-permute-done.4.above, bf16[80,1152]{1,0:T(8,128)(2,1)S(1)} %collective-permute-done.5.below, ...), custom_call_target="tpu_custom_call", output_to_operand_aliasing={{}: (4, {})} | custom-call | flops 200000000 | bytes 3000000 | tf_op jit(solution)/shard_map/pallas_call | solution.py:396
  (15 shorter events, 0.0 us)
Async XLA Ops:
  1.0 13.4 %collective-permute-start = (bf16[64,1152]{1,0:T(8,128)(2,1)S(1)}, bf16[64,1152]{1,0:T(8,128)(2,1)S(1)}, u32[]{:S(2)}, u32[]{:S(2)}) collective-permute-start(bf16[64,1152]{1,0:T(8,128)(2,1)S(1)} %bitcast.23), channel_id=1, source_target_pairs={{0,16},{16,32},{32,48},{48,64},{64,80},{80,96},{96,112},{112,128},... | collective-permute-start | bytes 442376 | tf_op jit(solution)/shard_map/ppermute | solution.py:423
  2.6 11.8 %collective-permute-start.1 = (bf16[64,1152]{1,0:T(8,128)(2,1)S(1)}, bf16[64,1152]{1,0:T(8,128)(2,1)S(1)}, u32[]{:S(2)}, u32[]{:S(2)}) collective-permute-start(bf16[64,1152]{1,0:T(8,128)(2,1)S(1)} %bitcast.22), channel_id=1, source_target_pairs={{16,0},{32,16},{48,32},{64,48},{80,64},{96,80},{112,96},{128,112},... | collective-permute-start | bytes 442376 | tf_op jit(solution)/shard_map/ppermute | solution.py:424
  8.0 6.4 %copy-start.1 = (bf16[2,64,128]{2,1,0:T(8,128)(2,1)S(1)}, bf16[2,64,128]{2,1,0:T(8,128)(2,1)}, u32[]{:S(2)}) copy-start(bf16[2,64,128]{2,1,0:T(8,128)(2,1)} %constant.44.clone.send_rim) | copy-start | bytes 98308
  8.0 11.1 %copy-start = (bf16[8,32,1152]{2,1,0:T(8,128)(2,1)S(1)}, bf16[8,32,1152]{2,1,0:T(8,128)(2,1)}, u32[]{:S(2)}) copy-start(bf16[8,32,1152]{2,1,0:T(8,128)(2,1)} %param.27) | copy-start | bytes 1769476
  8.0 11.1 %copy-start.4 = (f32[2,3,1152]{2,0,1:T(2,128)S(1)}, f32[2,3,1152]{2,0,1:T(2,128)}, u32[]{:S(2)}) copy-start(f32[2,3,1152]{2,0,1:T(2,128)} %param.31) | copy-start | bytes 82948
  8.0 11.1 %copy-start.5 = (s32[1,4,144]{2,1,0:T(4,128)S(1)}, s32[1,4,144]{2,1,0:T(4,128)}, u32[]{:S(2)}) copy-start(s32[1,4,144]{2,1,0:T(4,128)} %param.29) | copy-start | bytes 6916
  8.0 11.1 %copy-start.6 = (s32[16]{0:T(128)S(1)}, s32[16]{0:T(128)}, u32[]{:S(2)}) copy-start(s32[16]{0:T(128)} %radius.3) | copy-start | bytes 196
  8.0 11.0 %copy-start.7 = (bf16[3,2,192,144]{3,2,1,0:T(8,128)(2,1)S(1)}, bf16[3,2,192,144]{3,2,1,0:T(8,128)(2,1)}, u32[]{:S(2)}) copy-start(bf16[3,2,192,144]{3,2,1,0:T(8,128)(2,1)} %constant.47.clone.key) | copy-start | bytes 995332
  8.0 11.0 %copy-start.11 = (bf16[496,384]{1,0:T(8,128)(2,1)S(1)}, bf16[496,384]{1,0:T(8,128)(2,1)}, u32[]{:S(2)}) copy-start(bf16[496,384]{1,0:T(8,128)(2,1)} %constant.45.clone.middle) | copy-start | bytes 1142788
  8.0 11.0 %copy-start.16 = (bf16[3,192,128]{2,1,0:T(8,128)(2,1)S(1)}, bf16[3,192,128]{2,1,0:T(8,128)(2,1)}, u32[]{:S(2)}) copy-start(bf16[3,192,128]{2,1,0:T(8,128)(2,1)} %constant.46.clone.dist) | copy-start | bytes 442372
  8.0 11.0 %copy-start.20 = (f32[3,1,128]{2,1,0:T(1,128)S(1)}, f32[3,1,128]{2,1,0:T(1,128)}, u32[]{:S(2)}) copy-start(f32[3,1,128]{2,1,0:T(1,128)} %constant.48.clone.second) | copy-start | bytes 4612
  14.8 17.4 %collective-permute-start.2 = (bf16[96,1152]{1,0:T(8,128)(2,1)S(1)}, bf16[96,1152]{1,0:T(8,128)(2,1)S(1)}, u32[]{:S(2)}, u32[]{:S(2)}) collective-permute-start(bf16[96,1152]{1,0:T(8,128)(2,1)S(1)} %get-tuple-element.22), channel_id=1, source_target_pairs={{0,1},{1,2},{2,3},{3,4},{4,5},{5,6},{6,7},{7,8},{8,9},{9,10},{10,1... | collective-permute-start | bytes 663560 | tf_op jit(solution)/shard_map/ppermute | solution.py:445
  14.9 17.3 %collective-permute-start.3 = (bf16[96,1152]{1,0:T(8,128)(2,1)S(1)}, bf16[96,1152]{1,0:T(8,128)(2,1)S(1)}, u32[]{:S(2)}, u32[]{:S(2)}) collective-permute-start(bf16[96,1152]{1,0:T(8,128)(2,1)S(1)} %get-tuple-element.23), channel_id=1, source_target_pairs={{1,0},{2,1},{3,2},{4,3},{5,4},{6,5},{7,6},{8,7},{9,8},{10,9},{11,1... | collective-permute-start | bytes 663560 | tf_op jit(solution)/shard_map/ppermute | solution.py:446
  19.1 13.2 %copy-start.2 = (bf16[1152,1152]{1,0:T(8,128)(2,1)S(1)}, bf16[1152,1152]{1,0:T(8,128)(2,1)}, u32[]{:S(2)}) copy-start(bf16[1152,1152]{1,0:T(8,128)(2,1)} %w_out.3) | copy-start | bytes 7962628
  19.1 13.2 %copy-start.3 = (bf16[1,4,144,1152]{3,2,1,0:T(8,128)(2,1)S(1)}, bf16[1,4,144,1152]{3,2,1,0:T(8,128)(2,1)}, u32[]{:S(2)}) copy-start(bf16[1,4,144,1152]{3,2,1,0:T(8,128)(2,1)} %param.28) | copy-start | bytes 3981316
  19.1 13.2 %copy-start.8 = (bf16[448,576]{1,0:T(8,128)(2,1)S(1)}, bf16[448,576]{1,0:T(8,128)(2,1)}, u32[]{:S(2)}) copy-start(bf16[448,576]{1,0:T(8,128)(2,1)} %constant.49.clone.edge) | copy-start | bytes 1548292
  19.1 13.1 %copy-start.10 = (bf16[2,2,192,144]{3,2,1,0:T(8,128)(2,1)S(1)}, bf16[2,2,192,144]{3,2,1,0:T(8,128)(2,1)}, u32[]{:S(2)}) copy-start(bf16[2,2,192,144]{3,2,1,0:T(8,128)(2,1)} %constant.51.clone.key) | copy-start | bytes 663556
  19.1 13.1 %copy-start.12 = (bf16[5,2,144,128]{3,2,1,0:T(8,128)(2,1)S(1)}, bf16[5,2,144,128]{3,2,1,0:T(8,128)(2,1)}, u32[]{:S(2)}) copy-start(bf16[5,2,144,128]{3,2,1,0:T(8,128)(2,1)} %constant.53.clone.slot) | copy-start | bytes 1105924
  19.1 13.1 %copy-start.14 = (bf16[4,128,144]{2,1,0:T(8,128)(2,1)S(1)}, bf16[4,128,144]{2,1,0:T(8,128)(2,1)}, u32[]{:S(2)}) copy-start(bf16[4,128,144]{2,1,0:T(8,128)(2,1)} %constant.55.clone.ctl) | copy-start | bytes 442372
  19.1 13.1 %copy-start.15 = (bf16[5,128,128]{2,1,0:T(8,128)(2,1)S(1)}, bf16[5,128,128]{2,1,0:T(8,128)(2,1)}, u32[]{:S(2)}) copy-start(bf16[5,128,128]{2,1,0:T(8,128)(2,1)} %constant.54.clone.comb) | copy-start | bytes 491524
  19.2 13.1 %copy-start.18 = (bf16[2,192,128]{2,1,0:T(8,128)(2,1)S(1)}, bf16[2,192,128]{2,1,0:T(8,128)(2,1)}, u32[]{:S(2)}) copy-start(bf16[2,192,128]{2,1,0:T(8,128)(2,1)} %constant.50.clone.dist) | copy-start | bytes 294916
  19.2 13.1 %copy-start.19 = (bf16[2,128,32]{2,1,0:T(8,128)(2,1)S(1)}, bf16[2,128,32]{2,1,0:T(8,128)(2,1)}, u32[]{:S(2)}) copy-start(bf16[2,128,32]{2,1,0:T(8,128)(2,1)} %constant.56.clone.put) | copy-start | bytes 49156
  19.2 13.1 %copy-start.21 = (f32[2,1,128]{2,1,0:T(1,128)S(1)}, f32[2,1,128]{2,1,0:T(1,128)}, u32[]{:S(2)}) copy-start(f32[2,1,128]{2,1,0:T(1,128)} %constant.52.clone.second) | copy-start | bytes 3076
  32.3 17.8 %copy-start.9 = (bf16[4,256,144]{2,1,0:T(8,128)(2,1)S(1)}, bf16[4,256,144]{2,1,0:T(8,128)(2,1)}, u32[]{:S(2)}) copy-start(bf16[4,256,144]{2,1,0:T(8,128)(2,1)} %constant.58.clone.ctl) | copy-start | bytes 884740
  32.3 17.8 %copy-start.13 = (bf16[5,256,128]{2,1,0:T(8,128)(2,1)S(1)}, bf16[5,256,128]{2,1,0:T(8,128)(2,1)}, u32[]{:S(2)}) copy-start(bf16[5,256,128]{2,1,0:T(8,128)(2,1)} %constant.57.clone.comb) | copy-start | bytes 983044
  32.3 17.8 %copy-start.17 = (bf16[2,256,32]{2,1,0:T(8,128)(2,1)S(1)}, bf16[2,256,32]{2,1,0:T(8,128)(2,1)}, u32[]{:S(2)}) copy-start(bf16[2,256,32]{2,1,0:T(8,128)(2,1)} %constant.59.clone.put) | copy-start | bytes 98308
  45.9 9.7 %collective-permute-start.4 = (bf16[80,1152]{1,0:T(8,128)(2,1)S(1)}, bf16[80,1152]{1,0:T(8,128)(2,1)S(1)}, u32[]{:S(2)}, u32[]{:S(2)}) collective-permute-start(bf16[80,1152]{1,0:T(8,128)(2,1)S(1)} %get-tuple-element.28), channel_id=1, source_target_pairs={{0,16},{16,32},{32,48},{48,64},{64,80},{80,96},{96,112},{112,128},... | collective-permute-start | bytes 552968 | tf_op jit(solution)/shard_map/ppermute | solution.py:482
  46.0 9.6 %collective-permute-start.5 = (bf16[80,1152]{1,0:T(8,128)(2,1)S(1)}, bf16[80,1152]{1,0:T(8,128)(2,1)S(1)}, u32[]{:S(2)}, u32[]{:S(2)}) collective-permute-start(bf16[80,1152]{1,0:T(8,128)(2,1)S(1)} %get-tuple-element.29), channel_id=1, source_target_pairs={{16,0},{32,16},{48,32},{64,48},{80,64},{96,80},{112,96},{128,112},... | collective-permute-start | bytes 552968 | tf_op jit(solution)/shard_map/ppermute | solution.py:481

commit v4 on v3

--- a/solution.py
+++ b/solution.py
@@ -28,6 +28,7 @@
 FIRST = (-1, 1, 3, 4, 6)
 CUTS = (0, 126, 252, 324, 450, 576)
 KEYS = 192
+GROUP = 4
 
 
 def one_hot(rows, depth):
@@ -166,35 +167,47 @@
         bias_ref[unit, r] = jnp.where(dist <= r + 1.0, 0.0, -1e30)
 
 
-def attend(q_ref, keys, values, bias, radius_ref, out_ref):
+def attend(queries, keys, values, bias, radius_ref, put):
     lane = lax.broadcasted_iota(jnp.int32, (1, 256), 1)
-    scores, probs = [], []
-    for p in range(8):
+
+    def score(g, p):
         lanes = slice(128 * p, 128 * p + 256)
-        q = q_ref[:, lanes]
+        q = queries(g, lanes)
         both = [
             q * ((lane >= 16 * p + at) & (lane < 16 * p + at + HEAD_DIM)).astype(F32).astype(BF) for at in (0, HEAD_DIM)
         ]
-        scores.append(dot_nt(keys(lanes), jnp.concatenate(both, axis=0)))
-    for p in range(8):
+        return dot_nt(keys(g, lanes), jnp.concatenate(both, axis=0))
+
+    def soften(p, scores):
         exps, scales = [], []
         for i in (0, 1):
-            s = scores[p][:, 128 * i : 128 * i + 128] + bias(radius_ref[2 * p + i] - 1)
+            s = scores[:, 128 * i : 128 * i + 128] + bias(radius_ref[2 * p + i] - 1)
             top = jnp.max(s, axis=0, keepdims=True)
             e = jnp.exp2((s - top) * EXP_SCALE)
             scales.append(1.0 / jnp.sum(e, axis=0, keepdims=True))
             exps.append(e)
-        probs.append((jnp.concatenate(exps, axis=1).astype(BF), scales))
-    for p in range(8):
-        v = values(slice(128 * p, 128 * p + 256)).T[16 * p : 16 * p + 144]
-        e, scales = probs[p]
+        return jnp.concatenate(exps, axis=1).astype(BF), scales
+
+    def collect(g, p, e, scales):
+        v = values(g, slice(128 * p, 128 * p + 256)).T[16 * p : 16 * p + 144]
         o = dot(v, e)
         o = jnp.concatenate([o[:72, :128] * scales[0], o[72:, 128:] * scales[1]], axis=0)
-        out_ref[144 * p : 144 * p + 144, :] = o.astype(BF)
-
-
-def inner_window(own, rim, c, g, first, count):
-    def get(lanes):
+        put(g, slice(144 * p, 144 * p + 144), o.astype(BF))
+
+    items = [(g, p) for g in (0, 1) for p in range(8)]
+    scores = {k: score(*items[k]) for k in range(GROUP)}
+    probs = {}
+    for k in range(len(items) + GROUP):
+        if k + GROUP < len(items):
+            scores[k + GROUP] = score(*items[k + GROUP])
+        if k < len(items):
+            probs[k] = soften(items[k][1], scores.pop(k))
+        if k >= GROUP:
+            collect(*items[k - GROUP], *probs.pop(k - GROUP))
+
+
+def inner_window(own, rim, c, first, count):
+    def get(g, lanes):
         parts = []
         for i in range(count):
             parts += [own[c, g, first + i, :, lanes], rim[c, g, first + i, :, lanes]]
@@ -253,9 +266,13 @@
         out[64:] = msg[i, 64:]
 
 
-def middle_kernel(radius, latent, above, below, valid, mod, w, kv_own, middle, dist, key, second, kv_rim, attn, hid, qs, bias):
-    x = dot(middle[:, :256], latent[...]) + dot(middle[:, 256:320], above[...]) + dot(middle[:, 320:], below[...])
-    rows = hidden_rows(x, mod)
+def middle_kernel(
+    radius, latent, above, below, valid, mod, w, kv_own, middle, dist, key, second, kv_rim, attn, near, hid, qs, bias
+):
+    near[:256] = latent[...]
+    near[256:320] = above[...]
+    near[320:] = below[...]
+    rows = hidden_rows(dot(middle[...], near[...]), mod)
     for g in (0, 1):
         hid[g * 112 : (g + 1) * 112] = rows[g][:112]
         hid[224 + g * 384 : 224 + (g + 1) * 384] = rows[g][112:]
@@ -266,19 +283,22 @@
     for u in range(3):
         fill_bias(bias, u, dist[u], key[u, 0], key[u, 1], second[u], val[u : u + 1], val[u + 1 : u + 2])
 
-    @pl.loop(0, 6)
-    def _(i):
-        u, g = i // 2, i % 2
+    @pl.loop(0, 3)
+    def _(u):
         first = u + jnp.minimum(u, 1)
-        keys = inner_window(kv_own, kv_rim, 0, g, first, 4)
-        values = inner_window(kv_own, kv_rim, 1, g, first, 4)
+        keys = inner_window(kv_own, kv_rim, 0, first, 4)
+        values = inner_window(kv_own, kv_rim, 1, first, 4)
+
+        def put(g, rows, o):
+            attn[g, rows, pl.ds(pl.multiple_of(u * 128, 128), 128)] = o
+
         attend(
-            qs.at[g, u],
-            lambda lanes: jnp.concatenate(keys(lanes), axis=0),
-            lambda lanes: jnp.concatenate(values(lanes), axis=0),
+            lambda g, lanes: qs[g, u, :, lanes],
+            lambda g, lanes: jnp.concatenate(keys(g, lanes), axis=0),
+            lambda g, lanes: jnp.concatenate(values(g, lanes), axis=0),
             lambda r: bias[u, r],
             radius,
-            attn.at[u, g],
+            put,
         )
 
 
@@ -293,11 +313,13 @@
     return comb[unit].astype(F32) * weight[:1]
 
 
-def block_sums(attn_of, rows, x, w_out, mod, control, west, east, slot, comb, ctl, put):
+def block_sums(attn_mid, attn_edge, rows, x, w_out, mod, control, west, east, slot, comb, ctl, put):
     weights = [gather(u, slot, comb, rows) for u in range(5)]
     number = sum(jnp.sum(w, axis=1, keepdims=True) for w in weights)
     n = number.shape[0]
-    attn = [sum(dot_nt(weights[u].astype(BF), attn_of(u, g)) for u in range(5)).astype(BF) for g in (0, 1)]
+    inner = jnp.concatenate(weights[1:4], axis=1).astype(BF)
+    outer = jnp.concatenate([weights[0], weights[4]], axis=1).astype(BF)
+    attn = [(dot_nt(inner, attn_mid[g]) + dot_nt(outer, attn_edge[g])).astype(BF) for g in (0, 1)]
     proj = dot(jnp.concatenate(attn, axis=0), w_out[...])
     sums = (GUIDE * mod[2, 0:1]) * proj[:n] + ((1.0 - GUIDE) * mod[2, 1:2]) * proj[n:] + number * x
     for tile in range(4):
@@ -307,16 +329,14 @@
 
 def edge_kernel(
     radius, latent, above, below, west, east, valid, mod, w, kv_own, kv_rim, attn_mid, w_out, control,
-    edge, dist, key, second, slot, comb, ctl, put,
-    up, down, attn, hid, qs, kv, bias,
+    edge, dist, key, second, slot, comb, ctl, put_ctl,
+    up, down, attn, near, hid, qs, kv, bias,
 ):
-    x = (
-        dot(edge[:, :256], latent[...])
-        + dot(edge[:, 256:320], above[...])
-        + dot(edge[:, 320:384], below[...])
-        + dot(edge[:, 384:480], west[...])
-        + dot(edge[:, 480:], east[...])
-    )
+    at = 0
+    for ref in (latent, above, below, west, east):
+        near[at : at + ref.shape[0]] = ref[...]
+        at += ref.shape[0]
+    x = dot(edge[...], near[...])
     normed = hidden_rows(x, mod)
     for g in (0, 1):
         hid[g * 192 : (g + 1) * 192] = normed[g][:192]
@@ -330,23 +350,23 @@
 
     for i in (0, 1):
 
-        @pl.loop(0, 2)
-        def _(g):
-            def window(c):
-                inner = inner_window(kv_own, kv_rim, c, g, 5 * i, 2)
-
-                def get(lanes):
-                    outer = [kv[c, g, 2 * i, :, lanes], kv[c, g, 2 * i + 1, :, lanes]]
-                    parts = inner(lanes) + outer if i else outer + inner(lanes)
-                    return jnp.concatenate(parts, axis=0)
-
-                return get
-
-            attend(qs.at[g, i], window(0), window(1), lambda r: bias[i, r], radius, attn.at[i, g])
-
-    attn_of = lambda u, g: attn[u // 4, g] if u in (0, 4) else attn_mid[u - 1, g]
+        def window(c):
+            inner = inner_window(kv_own, kv_rim, c, 5 * i, 2)
+
+            def get(g, lanes):
+                outer = [kv[c, g, 2 * i, :, lanes], kv[c, g, 2 * i + 1, :, lanes]]
+                parts = inner(g, lanes) + outer if i else outer + inner(g, lanes)
+                return jnp.concatenate(parts, axis=0)
+
+            return get
+
+        def put(g, rows, o):
+            attn[g, rows, 128 * i : 128 * i + 128] = o
+
+        attend(lambda g, lanes: qs[g, i, :, lanes], window(0), window(1), lambda r: bias[i, r], radius, put)
+
     x = jnp.concatenate([above[...], below[...]], axis=0).astype(F32)
-    sums, number = block_sums(attn_of, rows, x, w_out, mod, control, west, east, slot, comb, ctl, put)
+    sums, number = block_sums(attn_mid, attn, rows, x, w_out, mod, control, west, east, slot, comb, ctl, put_ctl)
     row = lax.broadcasted_iota(jnp.int32, (64, 128), 0)
     lane = lax.broadcasted_iota(jnp.int32, (64, 128), 1)
     for at, out in ((0, up), (64, down)):
@@ -360,9 +380,8 @@
     attn_mid, attn_edge, latent, west, east, valid, mod, w_out, control, slot, comb, ctl, put, out, rest, count, done, sem
 ):
     rows = valid_rows(valid, west, east)
-    attn_of = lambda u, g: attn_edge[u // 4, g] if u in (0, 4) else attn_mid[u - 1, g]
     sums, number = block_sums(
-        attn_of, rows, latent[...].astype(F32), w_out, mod, control, west, east, slot, comb, ctl, put
+        attn_mid, attn_edge, rows, latent[...].astype(F32), w_out, mod, control, west, east, slot, comb, ctl, put
     )
     done[...] = (sums[64:192] / number[64:192]).astype(BF)
     copy = pltpu.make_async_copy(done, out.at[pl.ds(64, 128)], sem)
@@ -448,13 +467,14 @@
     mid = slice(1, 4)
     kv_rim, attn_mid = call(
         middle_kernel,
-        [shape(2, 2, 7, 16, D), shape(3, 2, D, 128)],
+        [shape(2, 2, 7, 16, D), shape(2, D, 384)],
         [
             radius, x, above, below, valid, mod, w, kv_own,
             t["middle"], t["dist"][mid], t["key"][mid], t["second"][mid],
         ],
         specs={0: smem},
         scratch=[
+            pltpu.VMEM((384, D), BF),
             pltpu.VMEM((992, D), BF),
             pltpu.VMEM((2, 3, 128, D), BF),
             pltpu.VMEM((3, 5, KEYS, 128), F32),
@@ -464,13 +484,14 @@
     ends = slice(0, 5, 4)
     up, down, attn_edge = call(
         edge_kernel,
-        [shape(80, D), shape(80, D), shape(2, 2, D, 128)],
+        [shape(80, D), shape(80, D), shape(2, D, 256)],
         [
             radius, x, above, below, west, east, valid, mod, w, kv_own, kv_rim, attn_mid, w_out, control,
             t["edge"], t["dist"][ends], t["key"][ends], t["second"][ends], t["slot"], t["comb_rim"], t["ctl_rim"], t["put_rim"],
         ],
         specs={0: smem},
         scratch=[
+            pltpu.VMEM((576, D), BF),
             pltpu.VMEM((896, D), BF),
             pltpu.VMEM((2, 2, 128, D), BF),
             pltpu.VMEM((2, 2, 4, 48, D), BF),

time: 56.9 us -> 52.7 us (0.926)
  Pallas kernels: 39.7 us -> 35 us
    pallas_call x6, Pallas kernels: 39.7 us -> 35 us  [call(): pl.pallas_call(kernel, out_shape=outs, in_specs=[specs.get(i, vmem) for i...]
  transfers between devices with their start and end apart: 6 -> 6, of which waited for: 0 -> 1; matrix products, arithmetic and copies ran while one was open for 0% -> 0% of each run, Pallas kernels for 44% -> 43%
where the time goes in v4:
time: 52.7 us; the launch traced here: 52.6 us
  Pallas kernels  35 us (66%)
  starting transfers between devices  15.4 us (29%)
  local copies, waits for them, and re-layouts  1.14 us (2%)
  between operations  0.55 us (1%)
  waiting for transfers between devices  0.54 us (1%)
    pallas_call x6, Pallas kernels, call(): pl.pallas_call(kernel, out_shape=outs, in_specs=[specs.get(i, vmem) for i...  35 us
    ppermute x1, starting transfers between devices, local(): below = lax.ppermute(x[:64], 'trow', sooner_r)  5.38 us
    ppermute x1, starting transfers between devices, local(): east = lax.ppermute(to_west, 'tcol', sooner_c)  4.14 us
    ppermute x1, starting transfers between devices, local(): got_below = lax.ppermute(up, 'trow', sooner_r)  4.12 us
    ppermute x1, starting transfers between devices, local(): above = lax.ppermute(x[192:], 'trow', later_r)  1.57 us
  transfers between devices with their start and end apart: 6, of which 1 were waited for; matrix products, arithmetic and copies ran while one was open for 0% of the time, Pallas kernels for 43%

profile of v4, /device:TPU:8, one launch (start us, length us, event | category | flops | bytes accessed | tf_op | source)
XLA Modules:
  0.0 52.6 jit_solution(3066991646901283698)
XLA Ops:
  0.0 1.0 %fusion = (bf16[2,32,1152]{2,1,0:T(8,128)(2,1)S(1)}, bf16[2,32,1152]{2,1,0:T(8,128)(2,1)S(1)}) fusion(bf16[8,32,1152]{2,1,0:T(8,128)(2,1)} %param.27), kind=kLoop, calls=%fused_computation | loop fusion | bytes 589824 | tf_op jit(solution)/shard_map/slice | solution.py:443
  1.0 1.6 %collective-permute-start = (bf16[64,1152]{1,0:T(8,128)(2,1)S(1)}, bf16[64,1152]{1,0:T(8,128)(2,1)S(1)}, u32[]{:S(2)}, u32[]{:S(2)}) collective-permute-start(bf16[64,1152]{1,0:T(8,128)(2,1)S(1)} %bitcast.23), channel_id=1, source_target_pairs={{0,16},{16,32},{32,48},{48,64},{64,80},{80,96},{96,112},{112,128},... | collective-permute-start | bytes 442376 | tf_op jit(solution)/shard_map/ppermute | solution.py:442
  2.6 5.4 %collective-permute-start.1 = (bf16[64,1152]{1,0:T(8,128)(2,1)S(1)}, bf16[64,1152]{1,0:T(8,128)(2,1)S(1)}, u32[]{:S(2)}, u32[]{:S(2)}) collective-permute-start(bf16[64,1152]{1,0:T(8,128)(2,1)S(1)} %bitcast.22), channel_id=1, source_target_pairs={{16,0},{32,16},{48,32},{64,48},{80,64},{96,80},{112,96},{128,112},... | collective-permute-start | bytes 442376 | tf_op jit(solution)/shard_map/ppermute | solution.py:443
  8.0 0.0 copy-start.6
  8.0 0.0 copy-start.7
  8.0 0.0 copy-start.11
  8.0 0.0 copy-start.16
  8.0 0.0 copy-start.20
  8.0 6.3 %shard_map.253 = (bf16[2,2,7,32,1152]{4,3,2,1,0:T(8,128)(2,1)S(1)}, bf16[2,96,1152]{2,1,0:T(8,128)(2,1)S(1)}, bf16[1152,3456]{1,0:T(8,128)(2,1)S(1)}) custom-call(bf16[256,1152]{1,0:T(8,128)(2,1)} %bitcast.7, bf16[4,144,1152]{2,1,0:T(8,128)(2,1)} %bitcast.11, s32[4,144]{1,0:T(4,128)} %bitcast.18, f32[3,2,1152]{2,1,0:T(2,128)} %bitcast.14, ...), custom_call_target="tpu_custom_call" | custom-call | flops 3600000000 | bytes 12000000 | tf_op jit(solution)/shard_map/pallas_call | solution.py:415
  14.4 0.0 collective-permute-done.above
  14.4 0.0 collective-permute-done.1.below
  14.4 0.0 copy-done.1
  14.4 0.4 shard_map.255
  14.8 0.1 collective-permute-start.2
  14.9 4.1 %collective-permute-start.3 = (bf16[96,1152]{1,0:T(8,128)(2,1)S(1)}, bf16[96,1152]{1,0:T(8,128)(2,1)S(1)}, u32[]{:S(2)}, u32[]{:S(2)}) collective-permute-start(bf16[96,1152]{1,0:T(8,128)(2,1)S(1)} %get-tuple-element.23), channel_id=1, source_target_pairs={{1,0},{2,1},{3,2},{4,3},{5,4},{6,5},{7,6},{8,7},{9,8},{10,9},{11,1... | collective-permute-start | bytes 663560 | tf_op jit(solution)/shard_map/ppermute | solution.py:465
  19.0 0.0 copy-done
  19.0 0.0 copy-done.4
  19.0 0.0 copy-done.5
  19.0 0.0 copy-done.6
  19.0 0.0 copy-done.7
  19.0 0.0 copy-done.11
  19.0 0.0 copy-done.16
  19.1 0.0 copy-done.20
  19.1 0.0 copy-start.2
  19.1 0.0 copy-start.3
  19.1 0.0 copy-start.8
  19.1 0.0 copy-start.10
  19.1 0.0 copy-start.12
  19.1 0.0 copy-start.14
  19.1 0.0 copy-start.15
  19.2 0.0 copy-start.18
  19.2 0.0 copy-start.19
  19.2 0.0 copy-start.21
  19.2 11.2 %shard_map.254 = (bf16[2,2,7,16,1152]{4,3,2,1,0:T(8,128)(2,1)S(1)}, bf16[2,1152,384]{2,1,0:T(8,128)(2,1)S(1)}) custom-call(s32[16]{0:T(128)S(1)} %copy-done.6, bf16[256,1152]{1,0:T(8,128)(2,1)S(1)} %bitcast.8, bf16[64,1152]{1,0:T(8,128)(2,1)S(1)} %collective-permute-done.above, bf16[64,1152]{1,0:T(8,128)(2,1)S(1)} %collective-permute-done.1.below, ...), custom_call_target="tpu_custom_call" | custom-call | flops 8000000000 | bytes 14000000 | tf_op jit(solution)/shard_map/pallas_call | solution.py:415
  30.4 0.0 collective-permute-done.2.west
  30.4 0.0 collective-permute-done.3.east
  30.4 0.0 copy-done.2
  30.5 0.0 copy-start.9
  30.5 0.0 copy-start.13
  30.6 0.0 copy-start.17
  30.6 11.3 %shard_map.256 = (bf16[80,1152]{1,0:T(8,128)(2,1)S(1)}, bf16[80,1152]{1,0:T(8,128)(2,1)S(1)}, bf16[2,1152,256]{2,1,0:T(8,128)(2,1)S(1)}) custom-call(s32[16]{0:T(128)S(1)} %copy-done.6, bf16[256,1152]{1,0:T(8,128)(2,1)S(1)} %bitcast.9, bf16[64,1152]{1,0:T(8,128)(2,1)S(1)} %collective-permute-done.above, bf16[64,1152]{1,0:T(8,128)(2,1)S(1)} %collective-permute-done.1.below, ...), custom_call_target="tpu_custom_call" | custom-call | flops 10000000000 | bytes 16000000 | tf_op jit(solution)/shard_map/pallas_call | solution.py:415
  41.8 0.1 collective-permute-start.4
  41.9 4.1 %collective-permute-start.5 = (bf16[80,1152]{1,0:T(8,128)(2,1)S(1)}, bf16[80,1152]{1,0:T(8,128)(2,1)S(1)}, u32[]{:S(2)}, u32[]{:S(2)}) collective-permute-start(bf16[80,1152]{1,0:T(8,128)(2,1)S(1)} %get-tuple-element.29), channel_id=1, source_target_pairs={{16,0},{32,16},{48,32},{64,48},{80,64},{96,80},{112,96},{128,112},... | collective-permute-start | bytes 552968 | tf_op jit(solution)/shard_map/ppermute | solution.py:502
  46.1 0.0 copy-done.17
  46.1 4.8 %shard_map.257 = (bf16[256,1152]{1,0:T(8,128)(2,1)}, f32[2,64,1152]{2,1,0:T(8,128)S(1)}, f32[2,64,128]{2,1,0:T(8,128)S(1)}) custom-call(bf16[2,1152,384]{2,1,0:T(8,128)(2,1)S(1)} %get-tuple-element.20.attn_mid, bf16[2,1152,256]{2,1,0:T(8,128)(2,1)S(1)} %get-tuple-element.25.attn_edge, bf16[256,1152]{1,0:T(8,128)(2,1)S(1)} %bitcast.10, ...), custom_call_target="tpu_custom_call" | custom-call | flops 3000000000 | bytes 8000000 | tf_op jit(solution)/shard_map/pallas_call | solution.py:415
  50.9 0.0 collective-permute-done.4.above
  50.9 0.5 %collective-permute-done.5.below = bf16[80,1152]{1,0:T(8,128)(2,1)S(1)} collective-permute-done((bf16[80,1152]{1,0:T(8,128)(2,1)S(1)}, bf16[80,1152]{1,0:T(8,128)(2,1)S(1)}, u32[]{:S(2)}, u32[]{:S(2)}) %collective-permute-start.5) | collective-permute-done | bytes 184352 | tf_op jit(solution)/shard_map/ppermute | solution.py:502
  51.5 0.9 %shard_map.258 = bf16[256,1152]{1,0:T(8,128)(2,1)} custom-call(f32[2,64,1152]{2,1,0:T(8,128)S(1)} %get-tuple-element.26.rest, f32[2,64,128]{2,1,0:T(8,128)S(1)} %get-tuple-element.27.count, bf16[80,1152]{1,0:T(8,128)(2,1)S(1)} %collective-permute-done.4.above, bf16[80,1152]{1,0:T(8,128)(2,1)S(1)} %collective-permute-done.5.below, ...), custom_call_target="tpu_custom_call", output_to_operand_aliasing={{}: (4, {})} | custom-call | flops 200000000 | bytes 3000000 | tf_op jit(solution)/shard_map/pallas_call | solution.py:415
  (15 shorter events, 0.0 us)
Async XLA Ops:
  1.0 13.4 %collective-permute-start = (bf16[64,1152]{1,0:T(8,128)(2,1)S(1)}, bf16[64,1152]{1,0:T(8,128)(2,1)S(1)}, u32[]{:S(2)}, u32[]{:S(2)}) collective-permute-start(bf16[64,1152]{1,0:T(8,128)(2,1)S(1)} %bitcast.23), channel_id=1, source_target_pairs={{0,16},{16,32},{32,48},{48,64},{64,80},{80,96},{96,112},{112,128},... | collective-permute-start | bytes 442376 | tf_op jit(solution)/shard_map/ppermute | solution.py:442
  2.6 11.8 %collective-permute-start.1 = (bf16[64,1152]{1,0:T(8,128)(2,1)S(1)}, bf16[64,1152]{1,0:T(8,128)(2,1)S(1)}, u32[]{:S(2)}, u32[]{:S(2)}) collective-permute-start(bf16[64,1152]{1,0:T(8,128)(2,1)S(1)} %bitcast.22), channel_id=1, source_target_pairs={{16,0},{32,16},{48,32},{64,48},{80,64},{96,80},{112,96},{128,112},... | collective-permute-start | bytes 442376 | tf_op jit(solution)/shard_map/ppermute | solution.py:443
  8.0 6.4 %copy-start.1 = (bf16[2,64,128]{2,1,0:T(8,128)(2,1)S(1)}, bf16[2,64,128]{2,1,0:T(8,128)(2,1)}, u32[]{:S(2)}) copy-start(bf16[2,64,128]{2,1,0:T(8,128)(2,1)} %constant.44.clone.send_rim) | copy-start | bytes 98308
  8.0 11.1 %copy-start = (bf16[8,32,1152]{2,1,0:T(8,128)(2,1)S(1)}, bf16[8,32,1152]{2,1,0:T(8,128)(2,1)}, u32[]{:S(2)}) copy-start(bf16[8,32,1152]{2,1,0:T(8,128)(2,1)} %param.27) | copy-start | bytes 1769476
  8.0 11.1 %copy-start.4 = (f32[2,3,1152]{2,0,1:T(2,128)S(1)}, f32[2,3,1152]{2,0,1:T(2,128)}, u32[]{:S(2)}) copy-start(f32[2,3,1152]{2,0,1:T(2,128)} %param.31) | copy-start | bytes 82948
  8.0 11.1 %copy-start.5 = (s32[1,4,144]{2,1,0:T(4,128)S(1)}, s32[1,4,144]{2,1,0:T(4,128)}, u32[]{:S(2)}) copy-start(s32[1,4,144]{2,1,0:T(4,128)} %param.29) | copy-start | bytes 6916
  8.0 11.1 %copy-start.6 = (s32[16]{0:T(128)S(1)}, s32[16]{0:T(128)}, u32[]{:S(2)}) copy-start(s32[16]{0:T(128)} %radius.3) | copy-start | bytes 196
  8.0 11.0 %copy-start.7 = (bf16[3,2,192,144]{3,2,1,0:T(8,128)(2,1)S(1)}, bf16[3,2,192,144]{3,2,1,0:T(8,128)(2,1)}, u32[]{:S(2)}) copy-start(bf16[3,2,192,144]{3,2,1,0:T(8,128)(2,1)} %constant.47.clone.key) | copy-start | bytes 995332
  8.0 11.0 %copy-start.11 = (bf16[496,384]{1,0:T(8,128)(2,1)S(1)}, bf16[496,384]{1,0:T(8,128)(2,1)}, u32[]{:S(2)}) copy-start(bf16[496,384]{1,0:T(8,128)(2,1)} %constant.45.clone.middle) | copy-start | bytes 1142788
  8.0 11.0 %copy-start.16 = (bf16[3,192,128]{2,1,0:T(8,128)(2,1)S(1)}, bf16[3,192,128]{2,1,0:T(8,128)(2,1)}, u32[]{:S(2)}) copy-start(bf16[3,192,128]{2,1,0:T(8,128)(2,1)} %constant.46.clone.dist) | copy-start | bytes 442372
  8.0 11.0 %copy-start.20 = (f32[3,1,128]{2,1,0:T(1,128)S(1)}, f32[3,1,128]{2,1,0:T(1,128)}, u32[]{:S(2)}) copy-start(f32[3,1,128]{2,1,0:T(1,128)} %constant.48.clone.second) | copy-start | bytes 4612
  14.8 15.6 %collective-permute-start.2 = (bf16[96,1152]{1,0:T(8,128)(2,1)S(1)}, bf16[96,1152]{1,0:T(8,128)(2,1)S(1)}, u32[]{:S(2)}, u32[]{:S(2)}) collective-permute-start(bf16[96,1152]{1,0:T(8,128)(2,1)S(1)} %get-tuple-element.22), channel_id=1, source_target_pairs={{0,1},{1,2},{2,3},{3,4},{4,5},{5,6},{6,7},{7,8},{8,9},{9,10},{10,1... | collective-permute-start | bytes 663560 | tf_op jit(solution)/shard_map/ppermute | solution.py:464
  14.9 15.5 %collective-permute-start.3 = (bf16[96,1152]{1,0:T(8,128)(2,1)S(1)}, bf16[96,1152]{1,0:T(8,128)(2,1)S(1)}, u32[]{:S(2)}, u32[]{:S(2)}) collective-permute-start(bf16[96,1152]{1,0:T(8,128)(2,1)S(1)} %get-tuple-element.23), channel_id=1, source_target_pairs={{1,0},{2,1},{3,2},{4,3},{5,4},{6,5},{7,6},{8,7},{9,8},{10,9},{11,1... | collective-permute-start | bytes 663560 | tf_op jit(solution)/shard_map/ppermute | solution.py:465
  19.1 11.4 %copy-start.2 = (bf16[1152,1152]{1,0:T(8,128)(2,1)S(1)}, bf16[1152,1152]{1,0:T(8,128)(2,1)}, u32[]{:S(2)}) copy-start(bf16[1152,1152]{1,0:T(8,128)(2,1)} %w_out.3) | copy-start | bytes 7962628
  19.1 11.4 %copy-start.3 = (bf16[1,4,144,1152]{3,2,1,0:T(8,128)(2,1)S(1)}, bf16[1,4,144,1152]{3,2,1,0:T(8,128)(2,1)}, u32[]{:S(2)}) copy-start(bf16[1,4,144,1152]{3,2,1,0:T(8,128)(2,1)} %param.28) | copy-start | bytes 3981316
  19.1 11.4 %copy-start.8 = (bf16[448,576]{1,0:T(8,128)(2,1)S(1)}, bf16[448,576]{1,0:T(8,128)(2,1)}, u32[]{:S(2)}) copy-start(bf16[448,576]{1,0:T(8,128)(2,1)} %constant.49.clone.edge) | copy-start | bytes 1548292
  19.1 11.4 %copy-start.10 = (bf16[2,2,192,144]{3,2,1,0:T(8,128)(2,1)S(1)}, bf16[2,2,192,144]{3,2,1,0:T(8,128)(2,1)}, u32[]{:S(2)}) copy-start(bf16[2,2,192,144]{3,2,1,0:T(8,128)(2,1)} %constant.51.clone.key) | copy-start | bytes 663556
  19.1 11.4 %copy-start.12 = (bf16[5,2,144,128]{3,2,1,0:T(8,128)(2,1)S(1)}, bf16[5,2,144,128]{3,2,1,0:T(8,128)(2,1)}, u32[]{:S(2)}) copy-start(bf16[5,2,144,128]{3,2,1,0:T(8,128)(2,1)} %constant.53.clone.slot) | copy-start | bytes 1105924
  19.1 11.4 %copy-start.14 = (bf16[4,128,144]{2,1,0:T(8,128)(2,1)S(1)}, bf16[4,128,144]{2,1,0:T(8,128)(2,1)}, u32[]{:S(2)}) copy-start(bf16[4,128,144]{2,1,0:T(8,128)(2,1)} %constant.55.clone.ctl) | copy-start | bytes 442372
  19.1 11.4 %copy-start.15 = (bf16[5,128,128]{2,1,0:T(8,128)(2,1)S(1)}, bf16[5,128,128]{2,1,0:T(8,128)(2,1)}, u32[]{:S(2)}) copy-start(bf16[5,128,128]{2,1,0:T(8,128)(2,1)} %constant.54.clone.comb) | copy-start | bytes 491524
  19.2 11.4 %copy-start.18 = (bf16[2,192,128]{2,1,0:T(8,128)(2,1)S(1)}, bf16[2,192,128]{2,1,0:T(8,128)(2,1)}, u32[]{:S(2)}) copy-start(bf16[2,192,128]{2,1,0:T(8,128)(2,1)} %constant.50.clone.dist) | copy-start | bytes 294916
  19.2 11.3 %copy-start.19 = (bf16[2,128,32]{2,1,0:T(8,128)(2,1)S(1)}, bf16[2,128,32]{2,1,0:T(8,128)(2,1)}, u32[]{:S(2)}) copy-start(bf16[2,128,32]{2,1,0:T(8,128)(2,1)} %constant.56.clone.put_ctl) | copy-start | bytes 49156
  19.2 11.3 %copy-start.21 = (f32[2,1,128]{2,1,0:T(1,128)S(1)}, f32[2,1,128]{2,1,0:T(1,128)}, u32[]{:S(2)}) copy-start(f32[2,1,128]{2,1,0:T(1,128)} %constant.52.clone.second) | copy-start | bytes 3076
  30.5 15.5 %copy-start.9 = (bf16[4,256,144]{2,1,0:T(8,128)(2,1)S(1)}, bf16[4,256,144]{2,1,0:T(8,128)(2,1)}, u32[]{:S(2)}) copy-start(bf16[4,256,144]{2,1,0:T(8,128)(2,1)} %constant.58.clone.ctl) | copy-start | bytes 884740
  30.5 15.5 %copy-start.13 = (bf16[5,256,128]{2,1,0:T(8,128)(2,1)S(1)}, bf16[5,256,128]{2,1,0:T(8,128)(2,1)}, u32[]{:S(2)}) copy-start(bf16[5,256,128]{2,1,0:T(8,128)(2,1)} %constant.57.clone.comb) | copy-start | bytes 983044
  30.6 15.5 %copy-start.17 = (bf16[2,256,32]{2,1,0:T(8,128)(2,1)S(1)}, bf16[2,256,32]{2,1,0:T(8,128)(2,1)}, u32[]{:S(2)}) copy-start(bf16[2,256,32]{2,1,0:T(8,128)(2,1)} %constant.59.clone.put) | copy-start | bytes 98308
  41.8 9.1 %collective-permute-start.4 = (bf16[80,1152]{1,0:T(8,128)(2,1)S(1)}, bf16[80,1152]{1,0:T(8,128)(2,1)S(1)}, u32[]{:S(2)}, u32[]{:S(2)}) collective-permute-start(bf16[80,1152]{1,0:T(8,128)(2,1)S(1)} %get-tuple-element.28), channel_id=1, source_target_pairs={{0,16},{16,32},{32,48},{48,64},{64,80},{80,96},{96,112},{112,128},... | collective-permute-start | bytes 552968 | tf_op jit(solution)/shard_map/ppermute | solution.py:503
  41.9 9.5 %collective-permute-start.5 = (bf16[80,1152]{1,0:T(8,128)(2,1)S(1)}, bf16[80,1152]{1,0:T(8,128)(2,1)S(1)}, u32[]{:S(2)}, u32[]{:S(2)}) collective-permute-start(bf16[80,1152]{1,0:T(8,128)(2,1)S(1)} %get-tuple-element.29), channel_id=1, source_target_pairs={{16,0},{32,16},{48,32},{64,48},{80,64},{96,80},{112,96},{128,112},... | collective-permute-start | bytes 552968 | tf_op jit(solution)/shard_map/ppermute | solution.py:502

commit v5 on v4

--- a/solution.py
+++ b/solution.py
@@ -47,6 +47,14 @@
     return natural(row, col)
 
 
+def beside(side, row, col):
+    if col < 0 or col >= 32:
+        place = source(row, col)
+        return None if place is None else 192 + place - (384 if side == 0 else 480)
+    line = row if 0 <= row < 8 else row + 10 if row < 0 else row + 2
+    return line * 16 + col - 16 * side
+
+
 def natural(row, col):
     if row < 0:
         return 256 + (row + 2) * 32 + col
@@ -93,10 +101,17 @@
     t["own"] = bf(one_hot([source(*p) for b in range(1, 8) for p in block_tokens(b)[:32]], 256))
     rim = one_hot([source(*p) for b in range(1, 8) for p in block_tokens(b)[32:]], 384)
     queries = [[None if q is None else source(*q[1:]) for q in unit_queries(u)] for u in range(5)]
-    middle = np.concatenate([rim, one_hot(queries[1] + queries[2] + queries[3], 384)])
+    middle = np.concatenate([rim, one_hot(queries[1] + queries[2][:80] + queries[3], 384)])
     t["middle"] = bf(middle)
-    edge = one_hot([source(*p) for b in (-1, 0, 8, 9) for p in block_tokens(b)], 576)
-    t["edge"] = bf(np.concatenate([edge, one_hot(queries[0] + queries[4], 576)]))
+    t["edge"] = bf(
+        np.stack(
+            [
+                one_hot([beside(i, *p) for b in blocks for p in block_tokens(b)], 256).tolist()
+                + one_hot([None if q is None else beside(i, *q[1:]) for q in unit_queries(u)], 256).tolist()
+                for i, (blocks, u) in enumerate((((-1, 0), 0), ((8, 9), 4)))
+            ]
+        )
+    )
     t["dist"] = bf(np.stack([distances(u) for u in range(5)]))
     t["key"] = bf(
         np.stack([[one_hot([tile_token(u + k, *p) for p in unit_keys(u)], TILE_TOK) for k in (-1, 0)] for u in range(5)])
@@ -127,14 +142,20 @@
             put[0, natural(r - 2, k), r * 2 + k] = 1.0
             put[1, natural(r - 2, 30 + k), r * 2 + k] = 1.0
     t["send_own"], t["send_rim"], t["send_ctl"] = bf(send[:, :, :256]), bf(send[:, :, 256:]), bf(send_ctl)
-    t["put_core"], t["put_rim"] = bf(put[:, :256]), bf(put[:, 256:])
+    put = np.concatenate([put[0], put[1]], axis=1)
+    t["put_core"], t["put_rim"] = bf(put[:256]), bf(put[256:])
     t["valid_pad"] = bf(np.eye(TILE_TOK, 256))
     ctl = np.zeros((4, 384, TILE_TOK), np.float32)
     for tile in range(4):
         for r in range(-2, 10):
             for c in range(max(8 * tile - 2, 0), min(8 * tile + 10, 32)):
                 ctl[tile, natural(r, c), tile_token(tile, r, c)] = 1.0
-    t["ctl_core"], t["ctl_rim"] = bf(ctl[:, :256]), bf(ctl[:, 256:])
+    t["ctl_core"] = bf(ctl[:, :256])
+    ends = [np.r_[0:32, 112:144] for _ in range(4)]
+    t["ctl_rim"] = bf(np.concatenate([ctl[i, 256:][:, e] for i, e in enumerate(ends)], axis=1))
+    t["ctl_pick"] = bf(
+        np.stack([np.concatenate([np.eye(TILE_TOK)[:, e] * (i == k) for k, e in enumerate(ends)], axis=1) for i in range(4)])
+    )
     return t
 
 
@@ -275,25 +296,26 @@
     rows = hidden_rows(dot(middle[...], near[...]), mod)
     for g in (0, 1):
         hid[g * 112 : (g + 1) * 112] = rows[g][:112]
-        hid[224 + g * 384 : 224 + (g + 1) * 384] = rows[g][112:]
-    qs[...] = dot(hid[224:], w[:, :D]).astype(BF).reshape(2, 3, 128, D)
+        hid[224 + g * 336 : 224 + (g + 1) * 336] = rows[g][112:]
+    qs[...] = dot(hid[224:], w[:, :D]).astype(BF).reshape(2, 336, D)
+    out = dot(hid[:224], w[:, D:]).astype(BF)
     for c in (0, 1):
-        kv_rim[c] = dot(hid[:224], w[:, (c + 1) * D : (c + 2) * D]).astype(BF).reshape(2, 7, 16, D)
+        kv_rim[c] = out[:, c * D : (c + 1) * D].reshape(2, 7, 16, D)
     val = valid[...].astype(F32)
     for u in range(3):
         fill_bias(bias, u, dist[u], key[u, 0], key[u, 1], second[u], val[u : u + 1], val[u + 1 : u + 2])
 
-    @pl.loop(0, 3)
-    def _(u):
-        first = u + jnp.minimum(u, 1)
+    for u in range(3):
+        first = u + min(u, 1)
+        start = 128 * u - 48 * (u // 2)
         keys = inner_window(kv_own, kv_rim, 0, first, 4)
         values = inner_window(kv_own, kv_rim, 1, first, 4)
 
-        def put(g, rows, o):
-            attn[g, rows, pl.ds(pl.multiple_of(u * 128, 128), 128)] = o
+        def put(g, rows, o, u=u):
+            attn[g, rows, 128 * u : 128 * u + 128] = o
 
         attend(
-            lambda g, lanes: qs[g, u, :, lanes],
+            lambda g, lanes: qs[g, pl.ds(start, 128), lanes],
             lambda g, lanes: jnp.concatenate(keys(g, lanes), axis=0),
             lambda g, lanes: jnp.concatenate(values(g, lanes), axis=0),
             lambda r: bias[u, r],
@@ -313,7 +335,7 @@
     return comb[unit].astype(F32) * weight[:1]
 
 
-def block_sums(attn_mid, attn_edge, rows, x, w_out, mod, control, west, east, slot, comb, ctl, put):
+def block_sums(attn_mid, attn_edge, rows, x, w_out, mod, west, east, slot, comb, ctl, put):
     weights = [gather(u, slot, comb, rows) for u in range(5)]
     number = sum(jnp.sum(w, axis=1, keepdims=True) for w in weights)
     n = number.shape[0]
@@ -322,28 +344,32 @@
     attn = [(dot_nt(inner, attn_mid[g]) + dot_nt(outer, attn_edge[g])).astype(BF) for g in (0, 1)]
     proj = dot(jnp.concatenate(attn, axis=0), w_out[...])
     sums = (GUIDE * mod[2, 0:1]) * proj[:n] + ((1.0 - GUIDE) * mod[2, 1:2]) * proj[n:] + number * x
-    for tile in range(4):
-        sums = sums + dot((ctl[tile].astype(F32) * rows[tile + 1]).astype(BF), control[tile])
-    return sums + dot(put[0], west[64:]) + dot(put[1], east[64:]), number
+    return sums + ctl + dot(put[...], jnp.concatenate([west[64:], east[64:]], axis=0)), number
 
 
 def edge_kernel(
     radius, latent, above, below, west, east, valid, mod, w, kv_own, kv_rim, attn_mid, w_out, control,
-    edge, dist, key, second, slot, comb, ctl, put_ctl,
+    edge, dist, key, second, slot, comb, ctl, ctl_pick, put_ctl,
     up, down, attn, near, hid, qs, kv, bias,
 ):
-    at = 0
-    for ref in (latent, above, below, west, east):
-        near[at : at + ref.shape[0]] = ref[...]
-        at += ref.shape[0]
-    x = dot(edge[...], near[...])
+    parts = []
+    for i, message in ((0, west), (1, east)):
+        at = 0
+        for ref, lines in ((latent, 8), (above, 2), (below, 2)):
+            for line in range(lines):
+                near[i, at : at + 16] = ref[32 * line + 16 * i : 32 * line + 16 * i + 16]
+                at += 16
+        near[i, at:] = message[:64]
+        parts.append(dot(edge[i], near[i]))
+    x = jnp.concatenate([p[:96] for p in parts] + [p[96:] for p in parts], axis=0)
     normed = hidden_rows(x, mod)
     for g in (0, 1):
         hid[g * 192 : (g + 1) * 192] = normed[g][:192]
         hid[384 + g * 256 : 384 + (g + 1) * 256] = normed[g][192:]
     qs[...] = dot(hid[384:], w[:, :D]).astype(BF).reshape(2, 2, 128, D)
+    out = dot(hid[:384], w[:, D:]).astype(BF)
     for c in (0, 1):
-        kv[c] = dot(hid[:384], w[:, (c + 1) * D : (c + 2) * D]).astype(BF).reshape(2, 4, 48, D)
+        kv[c] = out[:, c * D : (c + 1) * D].reshape(2, 4, 48, D)
     rows = valid_rows(valid, west, east)
     for i, u in ((0, 0), (1, 4)):
         fill_bias(bias, i, dist[i], key[i, 0], key[i, 1], second[i], rows[u], rows[u + 1])
@@ -366,7 +392,10 @@
         attend(lambda g, lanes: qs[g, i, :, lanes], window(0), window(1), lambda r: bias[i, r], radius, put)
 
     x = jnp.concatenate([above[...], below[...]], axis=0).astype(F32)
-    sums, number = block_sums(attn_mid, attn, rows, x, w_out, mod, control, west, east, slot, comb, ctl, put_ctl)
+    weight = sum(dot(eight(rows[tile + 1]), ctl_pick[tile]) for tile in range(4))[:1]
+    ends = [control[tile, at : at + 32] for tile in range(4) for at in (0, 112)]
+    extra = dot((ctl[...].astype(F32) * weight).astype(BF), jnp.concatenate(ends, axis=0))
+    sums, number = block_sums(attn_mid, attn, rows, x, w_out, mod, west, east, slot, comb, extra, put_ctl)
     row = lax.broadcasted_iota(jnp.int32, (64, 128), 0)
     lane = lax.broadcasted_iota(jnp.int32, (64, 128), 1)
     for at, out in ((0, up), (64, down)):
@@ -380,9 +409,9 @@
     attn_mid, attn_edge, latent, west, east, valid, mod, w_out, control, slot, comb, ctl, put, out, rest, count, done, sem
 ):
     rows = valid_rows(valid, west, east)
-    sums, number = block_sums(
-        attn_mid, attn_edge, rows, latent[...].astype(F32), w_out, mod, control, west, east, slot, comb, ctl, put
-    )
+    extra = sum(dot((ctl[tile].astype(F32) * rows[tile + 1]).astype(BF), control[tile]) for tile in range(4))
+    x = latent[...].astype(F32)
+    sums, number = block_sums(attn_mid, attn_edge, rows, x, w_out, mod, west, east, slot, comb, extra, put)
     done[...] = (sums[64:192] / number[64:192]).astype(BF)
     copy = pltpu.make_async_copy(done, out.at[pl.ds(64, 128)], sem)
     copy.start()
@@ -475,8 +504,8 @@
         specs={0: smem},
         scratch=[
             pltpu.VMEM((384, D), BF),
-            pltpu.VMEM((992, D), BF),
-            pltpu.VMEM((2, 3, 128, D), BF),
+            pltpu.VMEM((896, D), BF),
+            pltpu.VMEM((2, 336, D), BF),
             pltpu.VMEM((3, 5, KEYS, 128), F32),
         ],
         cost=(8e9, 14e6),
@@ -487,11 +516,11 @@
         [shape(80, D), shape(80, D), shape(2, D, 256)],
         [
             radius, x, above, below, west, east, valid, mod, w, kv_own, kv_rim, attn_mid, w_out, control,
-            t["edge"], t["dist"][ends], t["key"][ends], t["second"][ends], t["slot"], t["comb_rim"], t["ctl_rim"], t["put_rim"],
+            t["edge"], t["dist"][ends], t["key"][ends], t["second"][ends], t["slot"], t["comb_rim"], t["ctl_rim"], t["ctl_pick"], t["put_rim"],
         ],
         specs={0: smem},
         scratch=[
-            pltpu.VMEM((576, D), BF),
+            pltpu.VMEM((2, 256, D), BF),
             pltpu.VMEM((896, D), BF),
             pltpu.VMEM((2, 2, 128, D), BF),
             pltpu.VMEM((2, 2, 4, 48, D), BF),

time: 52.7 us -> 50.2 us (0.953)
  Pallas kernels: 35 us -> 32.6 us
    pallas_call x6, Pallas kernels: 35 us -> 32.6 us  [call(): pl.pallas_call(kernel, out_shape=outs, in_specs=[specs.get(i, vmem) for i...]
  transfers between devices with their start and end apart: 6 -> 6, of which waited for: 1 -> 1; matrix products, arithmetic and copies ran while one was open for 0% -> 0% of each run, Pallas kernels for 43% -> 41%
where the time goes in v5:
time: 50.2 us; the launch traced here: 50.1 us
  Pallas kernels  32.6 us (65%)
  starting transfers between devices  15.4 us (31%)
  local copies, waits for them, and re-layouts  1.15 us (2%)
  between operations  0.57 us (1%)
    pallas_call x6, Pallas kernels, call(): pl.pallas_call(kernel, out_shape=outs, in_specs=[specs.get(i, vmem) for i...  32.6 us
    ppermute x1, starting transfers between devices, local(): below = lax.ppermute(x[:64], 'trow', sooner_r)  5.38 us
    ppermute x1, starting transfers between devices, local(): east = lax.ppermute(to_west, 'tcol', sooner_c)  4.14 us
    ppermute x1, starting transfers between devices, local(): got_below = lax.ppermute(up, 'trow', sooner_r)  4.12 us
    ppermute x1, starting transfers between devices, local(): above = lax.ppermute(x[192:], 'trow', later_r)  1.57 us
    slice x1, local copies, waits for them, and re-layouts, local(): below = lax.ppermute(x[:64], 'trow', sooner_r)  1 us
  transfers between devices with their start and end apart: 6, of which 1 were waited for; matrix products, arithmetic and copies ran while one was open for 0% of the time, Pallas kernels for 41%

profile of v5, /device:TPU:8, one launch (start us, length us, event | category | flops | bytes accessed | tf_op | source)
XLA Modules:
  0.0 50.1 jit_solution(9061996076686851011)
XLA Ops:
  0.0 1.0 %fusion = (bf16[2,32,1152]{2,1,0:T(8,128)(2,1)S(1)}, bf16[2,32,1152]{2,1,0:T(8,128)(2,1)S(1)}) fusion(bf16[8,32,1152]{2,1,0:T(8,128)(2,1)} %param.28), kind=kLoop, calls=%fused_computation | loop fusion | bytes 589824 | tf_op jit(solution)/shard_map/slice | solution.py:472
  1.0 1.6 %collective-permute-start = (bf16[64,1152]{1,0:T(8,128)(2,1)S(1)}, bf16[64,1152]{1,0:T(8,128)(2,1)S(1)}, u32[]{:S(2)}, u32[]{:S(2)}) collective-permute-start(bf16[64,1152]{1,0:T(8,128)(2,1)S(1)} %bitcast.23), channel_id=1, source_target_pairs={{0,16},{16,32},{32,48},{48,64},{64,80},{80,96},{96,112},{112,128},... | collective-permute-start | bytes 442376 | tf_op jit(solution)/shard_map/ppermute | solution.py:471
  2.6 5.4 %collective-permute-start.1 = (bf16[64,1152]{1,0:T(8,128)(2,1)S(1)}, bf16[64,1152]{1,0:T(8,128)(2,1)S(1)}, u32[]{:S(2)}, u32[]{:S(2)}) collective-permute-start(bf16[64,1152]{1,0:T(8,128)(2,1)S(1)} %bitcast.22), channel_id=1, source_target_pairs={{16,0},{32,16},{48,32},{64,48},{80,64},{96,80},{112,96},{128,112},... | collective-permute-start | bytes 442376 | tf_op jit(solution)/shard_map/ppermute | solution.py:472
  8.0 0.0 copy-start.6
  8.0 0.0 copy-start.7
  8.0 0.0 copy-start.11
  8.0 0.0 copy-start.16
  8.0 0.0 copy-start.21
  8.0 6.3 %shard_map.262 = (bf16[2,2,7,32,1152]{4,3,2,1,0:T(8,128)(2,1)S(1)}, bf16[2,96,1152]{2,1,0:T(8,128)(2,1)S(1)}, bf16[1152,3456]{1,0:T(8,128)(2,1)S(1)}) custom-call(bf16[256,1152]{1,0:T(8,128)(2,1)} %bitcast.7, bf16[4,144,1152]{2,1,0:T(8,128)(2,1)} %bitcast.11, s32[4,144]{1,0:T(4,128)} %bitcast.18, f32[3,2,1152]{2,1,0:T(2,128)} %bitcast.14, ...), custom_call_target="tpu_custom_call" | custom-call | flops 3600000000 | bytes 12000000 | tf_op jit(solution)/shard_map/pallas_call | solution.py:444
  14.4 0.0 collective-permute-done.above
  14.4 0.0 collective-permute-done.1.below
  14.4 0.0 copy-done.1
  14.4 0.3 shard_map.264
  14.8 0.1 collective-permute-start.2
  14.9 4.1 %collective-permute-start.3 = (bf16[96,1152]{1,0:T(8,128)(2,1)S(1)}, bf16[96,1152]{1,0:T(8,128)(2,1)S(1)}, u32[]{:S(2)}, u32[]{:S(2)}) collective-permute-start(bf16[96,1152]{1,0:T(8,128)(2,1)S(1)} %get-tuple-element.23), channel_id=1, source_target_pairs={{1,0},{2,1},{3,2},{4,3},{5,4},{6,5},{7,6},{8,7},{9,8},{10,9},{11,1... | collective-permute-start | bytes 663560 | tf_op jit(solution)/shard_map/ppermute | solution.py:494
  19.0 0.0 copy-done
  19.0 0.0 copy-done.4
  19.0 0.0 copy-done.5
  19.0 0.0 copy-done.6
  19.0 0.0 copy-done.7
  19.0 0.0 copy-done.11
  19.0 0.0 copy-done.16
  19.0 0.0 copy-done.21
  19.1 0.0 copy-start.2
  19.1 0.0 copy-start.3
  19.1 0.0 copy-start.9
  19.1 0.0 copy-start.10
  19.1 0.0 copy-start.13
  19.1 0.0 copy-start.14
  19.1 0.0 copy-start.15
  19.1 0.0 copy-start.17
  19.2 0.0 copy-start.19
  19.2 0.0 copy-start.20
  19.2 0.0 copy-start.22
  19.2 9.6 %shard_map.263 = (bf16[2,2,7,16,1152]{4,3,2,1,0:T(8,128)(2,1)S(1)}, bf16[2,1152,384]{2,1,0:T(8,128)(2,1)S(1)}) custom-call(s32[16]{0:T(128)S(1)} %copy-done.6, bf16[256,1152]{1,0:T(8,128)(2,1)S(1)} %bitcast.8, bf16[64,1152]{1,0:T(8,128)(2,1)S(1)} %collective-permute-done.above, bf16[64,1152]{1,0:T(8,128)(2,1)S(1)} %collective-permute-done.1.below, ...), custom_call_target="tpu_custom_call" | custom-call | flops 8000000000 | bytes 14000000 | tf_op jit(solution)/shard_map/pallas_call | solution.py:444
  28.8 0.0 collective-permute-done.2.west
  28.8 0.0 collective-permute-done.3.east
  29.0 0.0 copy-start.8
  29.0 0.0 copy-start.12
  29.0 0.0 copy-start.18
  29.0 10.5 %shard_map.265 = (bf16[80,1152]{1,0:T(8,128)(2,1)S(1)}, bf16[80,1152]{1,0:T(8,128)(2,1)S(1)}, bf16[2,1152,256]{2,1,0:T(8,128)(2,1)S(1)}) custom-call(s32[16]{0:T(128)S(1)} %copy-done.6, bf16[256,1152]{1,0:T(8,128)(2,1)S(1)} %bitcast.9, bf16[64,1152]{1,0:T(8,128)(2,1)S(1)} %collective-permute-done.above, bf16[64,1152]{1,0:T(8,128)(2,1)S(1)} %collective-permute-done.1.below, ...), custom_call_target="tpu_custom_call" | custom-call | flops 10000000000 | bytes 16000000 | tf_op jit(solution)/shard_map/pallas_call | solution.py:444
  39.5 0.1 collective-permute-start.4
  39.6 4.1 %collective-permute-start.5 = (bf16[80,1152]{1,0:T(8,128)(2,1)S(1)}, bf16[80,1152]{1,0:T(8,128)(2,1)S(1)}, u32[]{:S(2)}, u32[]{:S(2)}) collective-permute-start(bf16[80,1152]{1,0:T(8,128)(2,1)S(1)} %get-tuple-element.29), channel_id=1, source_target_pairs={{16,0},{32,16},{48,32},{64,48},{80,64},{96,80},{112,96},{128,112},... | collective-permute-start | bytes 552968 | tf_op jit(solution)/shard_map/ppermute | solution.py:531
  43.7 0.0 copy-done.12
  43.8 4.8 %shard_map.266 = (bf16[256,1152]{1,0:T(8,128)(2,1)}, f32[2,64,1152]{2,1,0:T(8,128)S(1)}, f32[2,64,128]{2,1,0:T(8,128)S(1)}) custom-call(bf16[2,1152,384]{2,1,0:T(8,128)(2,1)S(1)} %get-tuple-element.20.attn_mid, bf16[2,1152,256]{2,1,0:T(8,128)(2,1)S(1)} %get-tuple-element.25.attn_edge, bf16[256,1152]{1,0:T(8,128)(2,1)S(1)} %bitcast.10, ...), custom_call_target="tpu_custom_call" | custom-call | flops 3000000000 | bytes 8000000 | tf_op jit(solution)/shard_map/pallas_call | solution.py:444
  48.6 0.0 collective-permute-done.4.above
  48.6 0.4 collective-permute-done.5.below
  49.0 0.9 %shard_map.267 = bf16[256,1152]{1,0:T(8,128)(2,1)} custom-call(f32[2,64,1152]{2,1,0:T(8,128)S(1)} %get-tuple-element.26.rest, f32[2,64,128]{2,1,0:T(8,128)S(1)} %get-tuple-element.27.count, bf16[80,1152]{1,0:T(8,128)(2,1)S(1)} %collective-permute-done.4.above, bf16[80,1152]{1,0:T(8,128)(2,1)S(1)} %collective-permute-done.5.below, ...), custom_call_target="tpu_custom_call", output_to_operand_aliasing={{}: (4, {})} | custom-call | flops 200000000 | bytes 3000000 | tf_op jit(solution)/shard_map/pallas_call | solution.py:444
  (17 shorter events, 0.0 us)
Async XLA Ops:
  1.0 13.4 %collective-permute-start = (bf16[64,1152]{1,0:T(8,128)(2,1)S(1)}, bf16[64,1152]{1,0:T(8,128)(2,1)S(1)}, u32[]{:S(2)}, u32[]{:S(2)}) collective-permute-start(bf16[64,1152]{1,0:T(8,128)(2,1)S(1)} %bitcast.23), channel_id=1, source_target_pairs={{0,16},{16,32},{32,48},{48,64},{64,80},{80,96},{96,112},{112,128},... | collective-permute-start | bytes 442376 | tf_op jit(solution)/shard_map/ppermute | solution.py:471
  2.6 11.8 %collective-permute-start.1 = (bf16[64,1152]{1,0:T(8,128)(2,1)S(1)}, bf16[64,1152]{1,0:T(8,128)(2,1)S(1)}, u32[]{:S(2)}, u32[]{:S(2)}) collective-permute-start(bf16[64,1152]{1,0:T(8,128)(2,1)S(1)} %bitcast.22), channel_id=1, source_target_pairs={{16,0},{32,16},{48,32},{64,48},{80,64},{96,80},{112,96},{128,112},... | collective-permute-start | bytes 442376 | tf_op jit(solution)/shard_map/ppermute | solution.py:472
  8.0 6.5 %copy-start.1 = (bf16[2,64,128]{2,1,0:T(8,128)(2,1)S(1)}, bf16[2,64,128]{2,1,0:T(8,128)(2,1)}, u32[]{:S(2)}) copy-start(bf16[2,64,128]{2,1,0:T(8,128)(2,1)} %constant.46.clone.send_rim) | copy-start | bytes 98308
  8.0 11.0 %copy-start = (bf16[8,32,1152]{2,1,0:T(8,128)(2,1)S(1)}, bf16[8,32,1152]{2,1,0:T(8,128)(2,1)}, u32[]{:S(2)}) copy-start(bf16[8,32,1152]{2,1,0:T(8,128)(2,1)} %param.28) | copy-start | bytes 1769476
  8.0 11.0 %copy-start.4 = (f32[2,3,1152]{2,0,1:T(2,128)S(1)}, f32[2,3,1152]{2,0,1:T(2,128)}, u32[]{:S(2)}) copy-start(f32[2,3,1152]{2,0,1:T(2,128)} %param.32) | copy-start | bytes 82948
  8.0 11.0 %copy-start.5 = (s32[1,4,144]{2,1,0:T(4,128)S(1)}, s32[1,4,144]{2,1,0:T(4,128)}, u32[]{:S(2)}) copy-start(s32[1,4,144]{2,1,0:T(4,128)} %param.30) | copy-start | bytes 6916
  8.0 11.0 %copy-start.6 = (s32[16]{0:T(128)S(1)}, s32[16]{0:T(128)}, u32[]{:S(2)}) copy-start(s32[16]{0:T(128)} %radius.3) | copy-start | bytes 196
  8.0 11.0 %copy-start.7 = (bf16[3,2,192,144]{3,2,1,0:T(8,128)(2,1)S(1)}, bf16[3,2,192,144]{3,2,1,0:T(8,128)(2,1)}, u32[]{:S(2)}) copy-start(bf16[3,2,192,144]{3,2,1,0:T(8,128)(2,1)} %constant.49.clone.key) | copy-start | bytes 995332
  8.0 11.0 %copy-start.11 = (bf16[448,384]{1,0:T(8,128)(2,1)S(1)}, bf16[448,384]{1,0:T(8,128)(2,1)}, u32[]{:S(2)}) copy-start(bf16[448,384]{1,0:T(8,128)(2,1)} %constant.47.clone.middle) | copy-start | bytes 1032196
  8.0 11.0 %copy-start.16 = (bf16[3,192,128]{2,1,0:T(8,128)(2,1)S(1)}, bf16[3,192,128]{2,1,0:T(8,128)(2,1)}, u32[]{:S(2)}) copy-start(bf16[3,192,128]{2,1,0:T(8,128)(2,1)} %constant.48.clone.dist) | copy-start | bytes 442372
  8.0 11.0 %copy-start.21 = (f32[3,1,128]{2,1,0:T(1,128)S(1)}, f32[3,1,128]{2,1,0:T(1,128)}, u32[]{:S(2)}) copy-start(f32[3,1,128]{2,1,0:T(1,128)} %constant.50.clone.second) | copy-start | bytes 4612
  14.8 14.0 %collective-permute-start.2 = (bf16[96,1152]{1,0:T(8,128)(2,1)S(1)}, bf16[96,1152]{1,0:T(8,128)(2,1)S(1)}, u32[]{:S(2)}, u32[]{:S(2)}) collective-permute-start(bf16[96,1152]{1,0:T(8,128)(2,1)S(1)} %get-tuple-element.22), channel_id=1, source_target_pairs={{0,1},{1,2},{2,3},{3,4},{4,5},{5,6},{6,7},{7,8},{8,9},{9,10},{10,1... | collective-permute-start | bytes 663560 | tf_op jit(solution)/shard_map/ppermute | solution.py:493
  14.9 14.0 %collective-permute-start.3 = (bf16[96,1152]{1,0:T(8,128)(2,1)S(1)}, bf16[96,1152]{1,0:T(8,128)(2,1)S(1)}, u32[]{:S(2)}, u32[]{:S(2)}) collective-permute-start(bf16[96,1152]{1,0:T(8,128)(2,1)S(1)} %get-tuple-element.23), channel_id=1, source_target_pairs={{1,0},{2,1},{3,2},{4,3},{5,4},{6,5},{7,6},{8,7},{9,8},{10,9},{11,1... | collective-permute-start | bytes 663560 | tf_op jit(solution)/shard_map/ppermute | solution.py:494
  19.1 9.8 %copy-start.2 = (bf16[1152,1152]{1,0:T(8,128)(2,1)S(1)}, bf16[1152,1152]{1,0:T(8,128)(2,1)}, u32[]{:S(2)}) copy-start(bf16[1152,1152]{1,0:T(8,128)(2,1)} %w_out.3) | copy-start | bytes 7962628
  19.1 9.8 %copy-start.3 = (bf16[1,4,144,1152]{3,2,1,0:T(8,128)(2,1)S(1)}, bf16[1,4,144,1152]{3,2,1,0:T(8,128)(2,1)}, u32[]{:S(2)}) copy-start(bf16[1,4,144,1152]{3,2,1,0:T(8,128)(2,1)} %param.29) | copy-start | bytes 3981316
  19.1 9.8 %copy-start.9 = (bf16[2,2,192,144]{3,2,1,0:T(8,128)(2,1)S(1)}, bf16[2,2,192,144]{3,2,1,0:T(8,128)(2,1)}, u32[]{:S(2)}) copy-start(bf16[2,2,192,144]{3,2,1,0:T(8,128)(2,1)} %constant.53.clone.key) | copy-start | bytes 663556
  19.1 9.8 %copy-start.10 = (bf16[5,2,144,128]{3,2,1,0:T(8,128)(2,1)S(1)}, bf16[5,2,144,128]{3,2,1,0:T(8,128)(2,1)}, u32[]{:S(2)}) copy-start(bf16[5,2,144,128]{3,2,1,0:T(8,128)(2,1)} %constant.55.clone.slot) | copy-start | bytes 1105924
  19.1 9.8 %copy-start.13 = (bf16[4,144,256]{2,1,0:T(8,128)(2,1)S(1)}, bf16[4,144,256]{2,1,0:T(8,128)(2,1)}, u32[]{:S(2)}) copy-start(bf16[4,144,256]{2,1,0:T(8,128)(2,1)} %constant.58.clone.ctl_pick) | copy-start | bytes 884740
  19.1 9.8 %copy-start.14 = (bf16[2,224,256]{2,1,0:T(8,128)(2,1)S(1)}, bf16[2,224,256]{2,1,0:T(8,128)(2,1)}, u32[]{:S(2)}) copy-start(bf16[2,224,256]{2,1,0:T(8,128)(2,1)} %constant.51.clone.edge) | copy-start | bytes 688132
  19.1 9.8 %copy-start.15 = (bf16[5,128,128]{2,1,0:T(8,128)(2,1)S(1)}, bf16[5,128,128]{2,1,0:T(8,128)(2,1)}, u32[]{:S(2)}) copy-start(bf16[5,128,128]{2,1,0:T(8,128)(2,1)} %constant.56.clone.comb) | copy-start | bytes 491524
  19.1 9.8 %copy-start.17 = (bf16[2,192,128]{2,1,0:T(8,128)(2,1)S(1)}, bf16[2,192,128]{2,1,0:T(8,128)(2,1)}, u32[]{:S(2)}) copy-start(bf16[2,192,128]{2,1,0:T(8,128)(2,1)} %constant.52.clone.dist) | copy-start | bytes 294916
  19.2 9.8 %copy-start.19 = (bf16[128,256]{1,0:T(8,128)(2,1)S(1)}, bf16[128,256]{1,0:T(8,128)(2,1)}, u32[]{:S(2)}) copy-start(bf16[128,256]{1,0:T(8,128)(2,1)} %constant.57.clone.ctl) | copy-start | bytes 196612
  19.2 9.8 %copy-start.20 = (bf16[128,64]{1,0:T(8,128)(2,1)S(1)}, bf16[128,64]{1,0:T(8,128)(2,1)}, u32[]{:S(2)}) copy-start(bf16[128,64]{1,0:T(8,128)(2,1)} %constant.59.clone.put_ctl) | copy-start | bytes 49156
  19.2 9.8 %copy-start.22 = (f32[2,1,128]{2,1,0:T(1,128)S(1)}, f32[2,1,128]{2,1,0:T(1,128)}, u32[]{:S(2)}) copy-start(f32[2,1,128]{2,1,0:T(1,128)} %constant.54.clone.second) | copy-start | bytes 3076
  29.0 14.8 %copy-start.8 = (bf16[4,256,144]{2,1,0:T(8,128)(2,1)S(1)}, bf16[4,256,144]{2,1,0:T(8,128)(2,1)}, u32[]{:S(2)}) copy-start(bf16[4,256,144]{2,1,0:T(8,128)(2,1)} %constant.61.clone.ctl) | copy-start | bytes 884740
  29.0 14.8 %copy-start.12 = (bf16[5,256,128]{2,1,0:T(8,128)(2,1)S(1)}, bf16[5,256,128]{2,1,0:T(8,128)(2,1)}, u32[]{:S(2)}) copy-start(bf16[5,256,128]{2,1,0:T(8,128)(2,1)} %constant.60.clone.comb) | copy-start | bytes 983044
  29.0 14.8 %copy-start.18 = (bf16[256,64]{1,0:T(8,128)(2,1)S(1)}, bf16[256,64]{1,0:T(8,128)(2,1)}, u32[]{:S(2)}) copy-start(bf16[256,64]{1,0:T(8,128)(2,1)} %constant.62.clone.put) | copy-start | bytes 98308
  39.5 9.0 %collective-permute-start.4 = (bf16[80,1152]{1,0:T(8,128)(2,1)S(1)}, bf16[80,1152]{1,0:T(8,128)(2,1)S(1)}, u32[]{:S(2)}, u32[]{:S(2)}) collective-permute-start(bf16[80,1152]{1,0:T(8,128)(2,1)S(1)} %get-tuple-element.28), channel_id=1, source_target_pairs={{0,16},{16,32},{32,48},{48,64},{64,80},{80,96},{96,112},{112,128},... | collective-permute-start | bytes 552968 | tf_op jit(solution)/shard_map/ppermute | solution.py:532
  39.6 9.3 %collective-permute-start.5 = (bf16[80,1152]{1,0:T(8,128)(2,1)S(1)}, bf16[80,1152]{1,0:T(8,128)(2,1)S(1)}, u32[]{:S(2)}, u32[]{:S(2)}) collective-permute-start(bf16[80,1152]{1,0:T(8,128)(2,1)S(1)} %get-tuple-element.29), channel_id=1, source_target_pairs={{16,0},{32,16},{48,32},{64,48},{80,64},{96,80},{112,96},{128,112},... | collective-permute-start | bytes 552968 | tf_op jit(solution)/shard_map/ppermute | solution.py:531

commit v6 on v5

--- a/solution.py
+++ b/solution.py
@@ -25,9 +25,11 @@
 
 JR = np.array([j // 4 if j < 32 else (j - 40) // 4 if j < 40 else 8 + (j - 40) // 4 for j in range(48)])
 JC = np.arange(48) % 4
-FIRST = (-1, 1, 3, 4, 6)
-CUTS = (0, 126, 252, 324, 450, 576)
+FIRST = (-1, 1, 2, 4, 6)
+COUNT = (4, 4, 5, 4, 4)
 KEYS = 192
+LATE_KEYS = 240
+LATE_ROWS = 80
 GROUP = 4
 
 
@@ -72,12 +74,17 @@
     for t in range(4):
         entries += [(t, c) for c in range(max(8 * t - 2, 0), min(8 * t + 10, 32))]
     entries += [(4, 30), (4, 31)]
-    flat = [(t, r, c) for t, c in entries for r in range(-2, 10)][CUTS[unit] : CUTS[unit + 1]]
-    return flat + [None] * (128 - len(flat))
+    flat = [(t, r, c) for t, c in entries for r in range(-2, 10)]
+    left, right = flat[126:288], flat[288:450]
+    rim = [[q for q in half if not 0 <= q[1] < CORE] for half in (left, right)]
+    core = [[q for q in half if 0 <= q[1] < CORE] for half in (left, right)]
+    units = [flat[:126], rim[0] + core[0][:74], core[0][74:] + core[1][:34], rim[1] + core[1][34:], flat[450:]]
+    assert sum(len(u) for u in units) == 576
+    return units[unit] + [None] * (128 - len(units[unit]))
 
 
 def unit_keys(unit):
-    return [p for b in range(FIRST[unit], FIRST[unit] + 4) for p in block_tokens(b)]
+    return [p for b in range(FIRST[unit], FIRST[unit] + COUNT[unit]) for p in block_tokens(b)]
 
 
 def tile_token(tile, row, col):
@@ -86,7 +93,7 @@
 
 
 def distances(unit):
-    dist = np.full((KEYS, 128), FAR, np.float32)
+    dist = np.full((48 * COUNT[unit], 128), FAR, np.float32)
     for i, query in enumerate(unit_queries(unit)):
         for k, key in enumerate(unit_keys(unit)):
             if query is not None and -REACH <= key[1] < 32 + REACH and tile_token(query[0], *key) is not None:
@@ -101,7 +108,7 @@
     t["own"] = bf(one_hot([source(*p) for b in range(1, 8) for p in block_tokens(b)[:32]], 256))
     rim = one_hot([source(*p) for b in range(1, 8) for p in block_tokens(b)[32:]], 384)
     queries = [[None if q is None else source(*q[1:]) for q in unit_queries(u)] for u in range(5)]
-    middle = np.concatenate([rim, one_hot(queries[1] + queries[2][:80] + queries[3], 384)])
+    middle = np.concatenate([rim, one_hot(queries[1] + queries[3], 384)])
     t["middle"] = bf(middle)
     t["edge"] = bf(
         np.stack(
@@ -112,10 +119,12 @@
             ]
         )
     )
-    t["dist"] = bf(np.stack([distances(u) for u in range(5)]))
-    t["key"] = bf(
-        np.stack([[one_hot([tile_token(u + k, *p) for p in unit_keys(u)], TILE_TOK) for k in (-1, 0)] for u in range(5)])
-    )
+    t["late"] = bf(one_hot(queries[2][:LATE_ROWS], 256))
+    for name, members in (("edge", (0, 4)), ("mid", (1, 3)), ("late", (2,))):
+        t["dist_" + name] = bf(np.stack([distances(u) for u in members]))
+        t["key_" + name] = bf(
+            np.stack([[one_hot([tile_token(u + k, *p) for p in unit_keys(u)], TILE_TOK) for k in (-1, 0)] for u in members])
+        )
     slot = np.zeros((5, 2, TILE_TOK, 128), np.float32)
     comb = np.zeros((5, 384, 128), np.float32)
     second = np.zeros((5, 1, 128), np.float32)
@@ -296,29 +305,27 @@
     rows = hidden_rows(dot(middle[...], near[...]), mod)
     for g in (0, 1):
         hid[g * 112 : (g + 1) * 112] = rows[g][:112]
-        hid[224 + g * 336 : 224 + (g + 1) * 336] = rows[g][112:]
-    qs[...] = dot(hid[224:], w[:, :D]).astype(BF).reshape(2, 336, D)
+        hid[224 + g * 256 : 224 + (g + 1) * 256] = rows[g][112:]
+    qs[...] = dot(hid[224:], w[:, :D]).astype(BF).reshape(2, 2, 128, D)
     out = dot(hid[:224], w[:, D:]).astype(BF)
     for c in (0, 1):
         kv_rim[c] = out[:, c * D : (c + 1) * D].reshape(2, 7, 16, D)
     val = valid[...].astype(F32)
-    for u in range(3):
-        fill_bias(bias, u, dist[u], key[u, 0], key[u, 1], second[u], val[u : u + 1], val[u + 1 : u + 2])
-
-    for u in range(3):
-        first = u + min(u, 1)
-        start = 128 * u - 48 * (u // 2)
-        keys = inner_window(kv_own, kv_rim, 0, first, 4)
-        values = inner_window(kv_own, kv_rim, 1, first, 4)
-
-        def put(g, rows, o, u=u):
-            attn[g, rows, 128 * u : 128 * u + 128] = o
+    for i in (0, 1):
+        fill_bias(bias, i, dist[i], key[i, 0], key[i, 1], second[i], val[2 * i : 2 * i + 1], val[2 * i + 1 : 2 * i + 2])
+
+    for i in (0, 1):
+        keys = inner_window(kv_own, kv_rim, 0, 3 * i, 4)
+        values = inner_window(kv_own, kv_rim, 1, 3 * i, 4)
+
+        def put(g, rows, o):
+            attn[g, rows, 128 * i : 128 * i + 128] = o
 
         attend(
-            lambda g, lanes: qs[g, pl.ds(start, 128), lanes],
+            lambda g, lanes: qs[g, i, :, lanes],
             lambda g, lanes: jnp.concatenate(keys(g, lanes), axis=0),
             lambda g, lanes: jnp.concatenate(values(g, lanes), axis=0),
-            lambda r: bias[u, r],
+            lambda r: bias[i, r],
             radius,
             put,
         )
@@ -335,13 +342,15 @@
     return comb[unit].astype(F32) * weight[:1]
 
 
-def block_sums(attn_mid, attn_edge, rows, x, w_out, mod, west, east, slot, comb, ctl, put):
-    weights = [gather(u, slot, comb, rows) for u in range(5)]
-    number = sum(jnp.sum(w, axis=1, keepdims=True) for w in weights)
+def block_sums(parts, rows, x, w_out, mod, west, east, slot, comb, ctl, put):
+    weights = {u: gather(u, slot, comb, rows) for units, _ in parts for u in units}
+    number = sum(jnp.sum(w, axis=1, keepdims=True) for w in weights.values())
     n = number.shape[0]
-    inner = jnp.concatenate(weights[1:4], axis=1).astype(BF)
-    outer = jnp.concatenate([weights[0], weights[4]], axis=1).astype(BF)
-    attn = [(dot_nt(inner, attn_mid[g]) + dot_nt(outer, attn_edge[g])).astype(BF) for g in (0, 1)]
+    attn = [0.0, 0.0]
+    for units, ref in parts:
+        weight = jnp.concatenate([weights[u] for u in units], axis=1).astype(BF)
+        attn = [attn[g] + dot_nt(weight, ref[g]) for g in (0, 1)]
+    attn = [a.astype(BF) for a in attn]
     proj = dot(jnp.concatenate(attn, axis=0), w_out[...])
     sums = (GUIDE * mod[2, 0:1]) * proj[:n] + ((1.0 - GUIDE) * mod[2, 1:2]) * proj[n:] + number * x
     return sums + ctl + dot(put[...], jnp.concatenate([west[64:], east[64:]], axis=0)), number
@@ -395,7 +404,7 @@
     weight = sum(dot(eight(rows[tile + 1]), ctl_pick[tile]) for tile in range(4))[:1]
     ends = [control[tile, at : at + 32] for tile in range(4) for at in (0, 112)]
     extra = dot((ctl[...].astype(F32) * weight).astype(BF), jnp.concatenate(ends, axis=0))
-    sums, number = block_sums(attn_mid, attn, rows, x, w_out, mod, west, east, slot, comb, extra, put_ctl)
+    sums, number = block_sums((((1, 3), attn_mid), ((0, 4), attn)), rows, x, w_out, mod, west, east, slot, comb, extra, put_ctl)
     row = lax.broadcasted_iota(jnp.int32, (64, 128), 0)
     lane = lax.broadcasted_iota(jnp.int32, (64, 128), 1)
     for at, out in ((0, up), (64, down)):
@@ -406,12 +415,38 @@
 
 
 def core_kernel(
-    attn_mid, attn_edge, latent, west, east, valid, mod, w_out, control, slot, comb, ctl, put, out, rest, count, done, sem
+    radius, attn_mid, attn_edge, latent, west, east, valid, mod, w, kv_own, kv_rim, w_out, control,
+    late, dist, key, second, slot, comb, ctl, put,
+    out, rest, count, done, hid, qs, bias, attn, sem,
 ):
     rows = valid_rows(valid, west, east)
+    normed = hidden_rows(dot(late[...], latent[...]), mod)
+    for g in (0, 1):
+        hid[g * LATE_ROWS : (g + 1) * LATE_ROWS] = normed[g]
+    asked = dot(hid[...], w[:, :D]).astype(BF)
+    for g in (0, 1):
+        qs[g, :LATE_ROWS] = asked[g * LATE_ROWS : (g + 1) * LATE_ROWS]
+        qs[g, LATE_ROWS:] = jnp.zeros((128 - LATE_ROWS, D), BF)
+    fill_bias(bias, 0, dist[0], key[0, 0], key[0, 1], second[0], rows[2], rows[3])
+    keys = inner_window(kv_own, kv_rim, 0, 1, 5)
+    values = inner_window(kv_own, kv_rim, 1, 1, 5)
+
+    def keep(g, lines, o):
+        attn[g, lines, :] = o
+
+    attend(
+        lambda g, lanes: qs[g, :, lanes],
+        lambda g, lanes: jnp.concatenate(keys(g, lanes), axis=0),
+        lambda g, lanes: jnp.concatenate(values(g, lanes), axis=0),
+        lambda r: bias[0, r],
+        radius,
+        keep,
+    )
     extra = sum(dot((ctl[tile].astype(F32) * rows[tile + 1]).astype(BF), control[tile]) for tile in range(4))
     x = latent[...].astype(F32)
-    sums, number = block_sums(attn_mid, attn_edge, rows, x, w_out, mod, west, east, slot, comb, extra, put)
+    sums, number = block_sums(
+        (((1, 3), attn_mid), ((0, 4), attn_edge), ((2,), attn)), rows, x, w_out, mod, west, east, slot, comb, extra, put
+    )
     done[...] = (sums[64:192] / number[64:192]).astype(BF)
     copy = pltpu.make_async_copy(done, out.at[pl.ds(64, 128)], sem)
     copy.start()
@@ -493,30 +528,29 @@
     west = lax.ppermute(to_east, "tcol", later_c)
     east = lax.ppermute(to_west, "tcol", sooner_c)
 
-    mid = slice(1, 4)
+    mid, ends, late = slice(1, 4, 2), slice(0, 5, 4), slice(2, 3)
     kv_rim, attn_mid = call(
         middle_kernel,
-        [shape(2, 2, 7, 16, D), shape(2, D, 384)],
+        [shape(2, 2, 7, 16, D), shape(2, D, 256)],
         [
             radius, x, above, below, valid, mod, w, kv_own,
-            t["middle"], t["dist"][mid], t["key"][mid], t["second"][mid],
+            t["middle"], t["dist_mid"], t["key_mid"], t["second"][mid],
         ],
         specs={0: smem},
         scratch=[
             pltpu.VMEM((384, D), BF),
-            pltpu.VMEM((896, D), BF),
-            pltpu.VMEM((2, 336, D), BF),
-            pltpu.VMEM((3, 5, KEYS, 128), F32),
+            pltpu.VMEM((736, D), BF),
+            pltpu.VMEM((2, 2, 128, D), BF),
+            pltpu.VMEM((2, 5, KEYS, 128), F32),
         ],
         cost=(8e9, 14e6),
     )
-    ends = slice(0, 5, 4)
     up, down, attn_edge = call(
         edge_kernel,
         [shape(80, D), shape(80, D), shape(2, D, 256)],
         [
             radius, x, above, below, west, east, valid, mod, w, kv_own, kv_rim, attn_mid, w_out, control,
-            t["edge"], t["dist"][ends], t["key"][ends], t["second"][ends], t["slot"], t["comb_rim"], t["ctl_rim"], t["ctl_pick"], t["put_rim"],
+            t["edge"], t["dist_edge"], t["key_edge"], t["second"][ends], t["slot"], t["comb_rim"], t["ctl_rim"], t["ctl_pick"], t["put_rim"],
         ],
         specs={0: smem},
         scratch=[
@@ -534,12 +568,20 @@
         core_kernel,
         [shape(256, D), shape(2, 64, D, dtype=F32), shape(2, 64, 128, dtype=F32)],
         [
-            attn_mid, attn_edge, x, west, east, valid, mod, w_out, control,
-            t["slot"], t["comb_core"], t["ctl_core"], t["put_core"],
+            radius, attn_mid, attn_edge, x, west, east, valid, mod, w, kv_own, kv_rim, w_out, control,
+            t["late"], t["dist_late"], t["key_late"], t["second"][late], t["slot"], t["comb_core"], t["ctl_core"], t["put_core"],
         ],
+        specs={0: smem},
         out_specs={0: hbm},
-        scratch=[pltpu.VMEM((128, D), BF), pltpu.SemaphoreType.DMA],
-        cost=(3e9, 8e6),
+        scratch=[
+            pltpu.VMEM((128, D), BF),
+            pltpu.VMEM((2 * LATE_ROWS, D), BF),
+            pltpu.VMEM((2, 128, D), BF),
+            pltpu.VMEM((1, 5, LATE_KEYS, 128), F32),
+            pltpu.VMEM((2, D, 128), BF),
+            pltpu.SemaphoreType.DMA,
+        ],
+        cost=(4e9, 8e6),
     )
     (out,) = call(
         final_kernel,

time: 50.2 us -> 50.8 us (1.012)
  Pallas kernels: 32.6 us -> 33.5 us
    pallas_call x6, Pallas kernels: 32.6 us -> 33.5 us  [call(): pl.pallas_call(kernel, out_shape=outs, in_specs=[specs.get(i, vmem) for i...]
  transfers between devices with their start and end apart: 6 -> 6, of which waited for: 1 -> 0; matrix products, arithmetic and copies ran while one was open for 0% -> 0% of each run, Pallas kernels for 41% -> 43%
where the time goes in v6:
time: 50.8 us; the launch traced here: 50.7 us
  Pallas kernels  33.5 us (66%)
  starting transfers between devices  15.4 us (30%)
  local copies, waits for them, and re-layouts  1.17 us (2%)
  between operations  0.62 us (1%)
    pallas_call x6, Pallas kernels, call(): pl.pallas_call(kernel, out_shape=outs, in_specs=[specs.get(i, vmem) for i...  33.5 us
    ppermute x1, starting transfers between devices, local(): below = lax.ppermute(x[:64], 'trow', sooner_r)  5.38 us
    ppermute x1, starting transfers between devices, local(): east = lax.ppermute(to_west, 'tcol', sooner_c)  4.14 us
    ppermute x1, starting transfers between devices, local(): got_below = lax.ppermute(up, 'trow', sooner_r)  4.12 us
    ppermute x1, starting transfers between devices, local(): above = lax.ppermute(x[192:], 'trow', later_r)  1.57 us
  transfers between devices with their start and end apart: 6, of which 0 were waited for; matrix products, arithmetic and copies ran while one was open for 0% of the time, Pallas kernels for 43%

profile of v6, /device:TPU:8, one launch (start us, length us, event | category | flops | bytes accessed | tf_op | source)
XLA Modules:
  0.0 50.7 jit_solution(13163007381516797652)
XLA Ops:
  0.0 1.0 %fusion = (bf16[2,32,1152]{2,1,0:T(8,128)(2,1)S(1)}, bf16[2,32,1152]{2,1,0:T(8,128)(2,1)S(1)}) fusion(bf16[8,32,1152]{2,1,0:T(8,128)(2,1)} %param.32), kind=kLoop, calls=%fused_computation | loop fusion | bytes 589824 | tf_op jit(solution)/shard_map/slice | solution.py:507
  1.0 1.6 %collective-permute-start = (bf16[64,1152]{1,0:T(8,128)(2,1)S(1)}, bf16[64,1152]{1,0:T(8,128)(2,1)S(1)}, u32[]{:S(2)}, u32[]{:S(2)}) collective-permute-start(bf16[64,1152]{1,0:T(8,128)(2,1)S(1)} %bitcast.23), channel_id=1, source_target_pairs={{0,16},{16,32},{32,48},{48,64},{64,80},{80,96},{96,112},{112,128},... | collective-permute-start | bytes 442376 | tf_op jit(solution)/shard_map/ppermute | solution.py:506
  2.6 5.4 %collective-permute-start.1 = (bf16[64,1152]{1,0:T(8,128)(2,1)S(1)}, bf16[64,1152]{1,0:T(8,128)(2,1)S(1)}, u32[]{:S(2)}, u32[]{:S(2)}) collective-permute-start(bf16[64,1152]{1,0:T(8,128)(2,1)S(1)} %bitcast.22), channel_id=1, source_target_pairs={{16,0},{32,16},{48,32},{64,48},{80,64},{96,80},{112,96},{128,112},... | collective-permute-start | bytes 442376 | tf_op jit(solution)/shard_map/ppermute | solution.py:507
  8.0 0.0 copy-start.13
  8.0 0.0 copy-start.15
  8.0 0.0 copy-start.17
  8.0 0.0 copy-start.21
  8.0 0.0 copy-start.25
  8.0 6.3 %shard_map.298 = (bf16[2,2,7,32,1152]{4,3,2,1,0:T(8,128)(2,1)S(1)}, bf16[2,96,1152]{2,1,0:T(8,128)(2,1)S(1)}, bf16[1152,3456]{1,0:T(8,128)(2,1)S(1)}) custom-call(bf16[256,1152]{1,0:T(8,128)(2,1)} %bitcast.10, bf16[4,144,1152]{2,1,0:T(8,128)(2,1)} %bitcast.7, s32[4,144]{1,0:T(4,128)} %bitcast.18, f32[3,2,1152]{2,1,0:T(2,128)} %bitcast.14, ...), custom_call_target="tpu_custom_call" | custom-call | flops 3600000000 | bytes 12000000 | tf_op jit(solution)/shard_map/pallas_call | solution.py:479
  14.4 0.0 collective-permute-done.above
  14.4 0.0 collective-permute-done.1.below
  14.4 0.0 copy-done.10
  14.4 0.4 shard_map.300
  14.8 0.1 collective-permute-start.2
  14.9 4.1 %collective-permute-start.3 = (bf16[96,1152]{1,0:T(8,128)(2,1)S(1)}, bf16[96,1152]{1,0:T(8,128)(2,1)S(1)}, u32[]{:S(2)}, u32[]{:S(2)}) collective-permute-start(bf16[96,1152]{1,0:T(8,128)(2,1)S(1)} %get-tuple-element.23), channel_id=1, source_target_pairs={{1,0},{2,1},{3,2},{4,3},{5,4},{6,5},{7,6},{8,7},{9,8},{10,9},{11,1... | collective-permute-start | bytes 663560 | tf_op jit(solution)/shard_map/ppermute | solution.py:529
  19.0 0.0 copy-done.13
  19.0 0.0 copy-done.15
  19.0 0.0 copy-done.17
  19.0 0.0 copy-done.21
  19.0 0.0 copy-done.25
  19.1 0.0 copy-start
  19.1 0.0 copy-start.1
  19.1 0.0 copy-start.4
  19.1 0.0 copy-start.16
  19.1 0.0 copy-start.18
  19.1 0.0 copy-start.19
  19.1 0.0 copy-start.20
  19.1 0.0 copy-start.22
  19.2 0.0 copy-start.23
  19.2 0.0 copy-start.24
  19.2 7.8 %shard_map.299 = (bf16[2,2,7,16,1152]{4,3,2,1,0:T(8,128)(2,1)S(1)}, bf16[2,1152,256]{2,1,0:T(8,128)(2,1)S(1)}) custom-call(s32[16]{0:T(128)S(1)} %copy-done.13, bf16[256,1152]{1,0:T(8,128)(2,1)S(1)} %bitcast.11, bf16[64,1152]{1,0:T(8,128)(2,1)S(1)} %collective-permute-done.above, bf16[64,1152]{1,0:T(8,128)(2,1)S(1)} %collective-permute-done.1.below, ...), custom_call_target="tpu_custom_call" | custom-call | flops 8000000000 | bytes 14000000 | tf_op jit(solution)/shard_map/pallas_call | solution.py:479
  27.0 0.0 collective-permute-done.2.west
  27.0 0.0 collective-permute-done.3.east
  27.1 0.0 copy-start.3
  27.1 0.0 copy-start.5
  27.1 0.0 copy-start.6
  27.1 0.0 copy-start.7
  27.1 0.0 copy-start.8
  27.1 0.0 copy-start.9
  27.2 0.0 copy-start.14
  27.2 10.3 %shard_map.301 = (bf16[80,1152]{1,0:T(8,128)(2,1)S(1)}, bf16[80,1152]{1,0:T(8,128)(2,1)S(1)}, bf16[2,1152,256]{2,1,0:T(8,128)(2,1)S(1)}) custom-call(s32[16]{0:T(128)S(1)} %copy-done.13, bf16[256,1152]{1,0:T(8,128)(2,1)S(1)} %bitcast.12, bf16[64,1152]{1,0:T(8,128)(2,1)S(1)} %collective-permute-done.above, bf16[64,1152]{1,0:T(8,128)(2,1)S(1)} %collective-permute-done.1.below, ...), custom_call_target="tpu_custom_call" | custom-call | flops 10000000000 | bytes 16000000 | tf_op jit(solution)/shard_map/pallas_call | solution.py:479
  37.5 0.1 collective-permute-start.4
  37.5 4.1 %collective-permute-start.5 = (bf16[80,1152]{1,0:T(8,128)(2,1)S(1)}, bf16[80,1152]{1,0:T(8,128)(2,1)S(1)}, u32[]{:S(2)}, u32[]{:S(2)}) collective-permute-start(bf16[80,1152]{1,0:T(8,128)(2,1)S(1)} %get-tuple-element.29), channel_id=1, source_target_pairs={{16,0},{32,16},{48,32},{64,48},{80,64},{96,80},{112,96},{128,112},... | collective-permute-start | bytes 552968 | tf_op jit(solution)/shard_map/ppermute | solution.py:565
  41.7 0.0 copy-done.3
  41.7 7.8 %shard_map.302 = (bf16[256,1152]{1,0:T(8,128)(2,1)}, f32[2,64,1152]{2,1,0:T(8,128)S(1)}, f32[2,64,128]{2,1,0:T(8,128)S(1)}) custom-call(s32[16]{0:T(128)S(1)} %copy-done.13, bf16[2,1152,256]{2,1,0:T(8,128)(2,1)S(1)} %get-tuple-element.20.attn_mid, bf16[2,1152,256]{2,1,0:T(8,128)(2,1)S(1)} %get-tuple-element.25.attn_edge, bf16[256,1152]{1,0:T(8,128)(2,1)S(1)} %bitcast.13, ...), custom_call_target="tpu_custom_call" | custom-call | flops 4000000000 | bytes 8000000 | tf_op jit(solution)/shard_map/pallas_call | solution.py:479
  49.5 0.0 collective-permute-done.4.above
  49.6 0.0 collective-permute-done.5.below
  49.6 0.9 %shard_map.303 = bf16[256,1152]{1,0:T(8,128)(2,1)} custom-call(f32[2,64,1152]{2,1,0:T(8,128)S(1)} %get-tuple-element.26.rest, f32[2,64,128]{2,1,0:T(8,128)S(1)} %get-tuple-element.27.count, bf16[80,1152]{1,0:T(8,128)(2,1)S(1)} %collective-permute-done.4.above, bf16[80,1152]{1,0:T(8,128)(2,1)S(1)} %collective-permute-done.5.below, ...), custom_call_target="tpu_custom_call", output_to_operand_aliasing={{}: (4, {})} | custom-call | flops 200000000 | bytes 3000000 | tf_op jit(solution)/shard_map/pallas_call | solution.py:479
  (23 shorter events, 0.0 us)
Async XLA Ops:
  1.0 13.4 %collective-permute-start = (bf16[64,1152]{1,0:T(8,128)(2,1)S(1)}, bf16[64,1152]{1,0:T(8,128)(2,1)S(1)}, u32[]{:S(2)}, u32[]{:S(2)}) collective-permute-start(bf16[64,1152]{1,0:T(8,128)(2,1)S(1)} %bitcast.23), channel_id=1, source_target_pairs={{0,16},{16,32},{32,48},{48,64},{64,80},{80,96},{96,112},{112,128},... | collective-permute-start | bytes 442376 | tf_op jit(solution)/shard_map/ppermute | solution.py:506
  2.6 11.8 %collective-permute-start.1 = (bf16[64,1152]{1,0:T(8,128)(2,1)S(1)}, bf16[64,1152]{1,0:T(8,128)(2,1)S(1)}, u32[]{:S(2)}, u32[]{:S(2)}) collective-permute-start(bf16[64,1152]{1,0:T(8,128)(2,1)S(1)} %bitcast.22), channel_id=1, source_target_pairs={{16,0},{32,16},{48,32},{64,48},{80,64},{96,80},{112,96},{128,112},... | collective-permute-start | bytes 442376 | tf_op jit(solution)/shard_map/ppermute | solution.py:507
  8.0 6.4 %copy-start.10 = (bf16[2,64,128]{2,1,0:T(8,128)(2,1)S(1)}, bf16[2,64,128]{2,1,0:T(8,128)(2,1)}, u32[]{:S(2)}) copy-start(bf16[2,64,128]{2,1,0:T(8,128)(2,1)} %constant.52.clone.send_rim) | copy-start | bytes 98308
  8.0 11.0 %copy-start.2 = (bf16[8,32,1152]{2,1,0:T(8,128)(2,1)S(1)}, bf16[8,32,1152]{2,1,0:T(8,128)(2,1)}, u32[]{:S(2)}) copy-start(bf16[8,32,1152]{2,1,0:T(8,128)(2,1)} %param.32) | copy-start | bytes 1769476
  8.0 11.0 %copy-start.11 = (f32[2,3,1152]{2,0,1:T(2,128)S(1)}, f32[2,3,1152]{2,0,1:T(2,128)}, u32[]{:S(2)}) copy-start(f32[2,3,1152]{2,0,1:T(2,128)} %param.36) | copy-start | bytes 82948
  8.0 11.0 %copy-start.12 = (s32[1,4,144]{2,1,0:T(4,128)S(1)}, s32[1,4,144]{2,1,0:T(4,128)}, u32[]{:S(2)}) copy-start(s32[1,4,144]{2,1,0:T(4,128)} %param.34) | copy-start | bytes 6916
  8.0 11.0 %copy-start.13 = (s32[16]{0:T(128)S(1)}, s32[16]{0:T(128)}, u32[]{:S(2)}) copy-start(s32[16]{0:T(128)} %radius.5) | copy-start | bytes 196
  8.0 11.0 %copy-start.15 = (bf16[2,2,192,144]{3,2,1,0:T(8,128)(2,1)S(1)}, bf16[2,2,192,144]{3,2,1,0:T(8,128)(2,1)}, u32[]{:S(2)}) copy-start(bf16[2,2,192,144]{3,2,1,0:T(8,128)(2,1)} %constant.55.clone.key) | copy-start | bytes 663556
  8.0 11.0 %copy-start.17 = (bf16[368,384]{1,0:T(8,128)(2,1)S(1)}, bf16[368,384]{1,0:T(8,128)(2,1)}, u32[]{:S(2)}) copy-start(bf16[368,384]{1,0:T(8,128)(2,1)} %constant.53.clone.middle) | copy-start | bytes 847876
  8.0 11.0 %copy-start.21 = (bf16[2,192,128]{2,1,0:T(8,128)(2,1)S(1)}, bf16[2,192,128]{2,1,0:T(8,128)(2,1)}, u32[]{:S(2)}) copy-start(bf16[2,192,128]{2,1,0:T(8,128)(2,1)} %constant.54.clone.dist) | copy-start | bytes 294916
  8.0 11.0 %copy-start.25 = (f32[2,1,128]{2,1,0:T(1,128)S(1)}, f32[2,1,128]{2,1,0:T(1,128)}, u32[]{:S(2)}) copy-start(f32[2,1,128]{2,1,0:T(1,128)} %constant.56.clone.second) | copy-start | bytes 3076
  14.8 12.2 %collective-permute-start.2 = (bf16[96,1152]{1,0:T(8,128)(2,1)S(1)}, bf16[96,1152]{1,0:T(8,128)(2,1)S(1)}, u32[]{:S(2)}, u32[]{:S(2)}) collective-permute-start(bf16[96,1152]{1,0:T(8,128)(2,1)S(1)} %get-tuple-element.22), channel_id=1, source_target_pairs={{0,1},{1,2},{2,3},{3,4},{4,5},{5,6},{6,7},{7,8},{8,9},{9,10},{10,1... | collective-permute-start | bytes 663560 | tf_op jit(solution)/shard_map/ppermute | solution.py:528
  14.9 12.1 %collective-permute-start.3 = (bf16[96,1152]{1,0:T(8,128)(2,1)S(1)}, bf16[96,1152]{1,0:T(8,128)(2,1)S(1)}, u32[]{:S(2)}, u32[]{:S(2)}) collective-permute-start(bf16[96,1152]{1,0:T(8,128)(2,1)S(1)} %get-tuple-element.23), channel_id=1, source_target_pairs={{1,0},{2,1},{3,2},{4,3},{5,4},{6,5},{7,6},{8,7},{9,8},{10,9},{11,1... | collective-permute-start | bytes 663560 | tf_op jit(solution)/shard_map/ppermute | solution.py:529
  19.1 7.9 %copy-start = (bf16[1152,1152]{1,0:T(8,128)(2,1)S(1)}, bf16[1152,1152]{1,0:T(8,128)(2,1)}, u32[]{:S(2)}) copy-start(bf16[1152,1152]{1,0:T(8,128)(2,1)} %w_out.3) | copy-start | bytes 7962628
  19.1 7.9 %copy-start.1 = (bf16[1,4,144,1152]{3,2,1,0:T(8,128)(2,1)S(1)}, bf16[1,4,144,1152]{3,2,1,0:T(8,128)(2,1)}, u32[]{:S(2)}) copy-start(bf16[1,4,144,1152]{3,2,1,0:T(8,128)(2,1)} %param.33) | copy-start | bytes 3981316
  19.1 7.9 %copy-start.4 = (bf16[5,2,144,128]{3,2,1,0:T(8,128)(2,1)S(1)}, bf16[5,2,144,128]{3,2,1,0:T(8,128)(2,1)}, u32[]{:S(2)}) copy-start(bf16[5,2,144,128]{3,2,1,0:T(8,128)(2,1)} %constant.60.clone.slot) | copy-start | bytes 1105924
  19.1 7.9 %copy-start.16 = (bf16[4,144,256]{2,1,0:T(8,128)(2,1)S(1)}, bf16[4,144,256]{2,1,0:T(8,128)(2,1)}, u32[]{:S(2)}) copy-start(bf16[4,144,256]{2,1,0:T(8,128)(2,1)} %constant.63.clone.ctl_pick) | copy-start | bytes 884740
  19.1 7.9 %copy-start.18 = (bf16[2,224,256]{2,1,0:T(8,128)(2,1)S(1)}, bf16[2,224,256]{2,1,0:T(8,128)(2,1)}, u32[]{:S(2)}) copy-start(bf16[2,224,256]{2,1,0:T(8,128)(2,1)} %constant.57.clone.edge) | copy-start | bytes 688132
  19.1 7.9 %copy-start.19 = (bf16[5,128,128]{2,1,0:T(8,128)(2,1)S(1)}, bf16[5,128,128]{2,1,0:T(8,128)(2,1)}, u32[]{:S(2)}) copy-start(bf16[5,128,128]{2,1,0:T(8,128)(2,1)} %constant.61.clone.comb) | copy-start | bytes 491524
  19.1 7.9 %copy-start.20 = (bf16[2,192,128]{2,1,0:T(8,128)(2,1)S(1)}, bf16[2,192,128]{2,1,0:T(8,128)(2,1)}, u32[]{:S(2)}) copy-start(bf16[2,192,128]{2,1,0:T(8,128)(2,1)} %constant.58.clone.dist) | copy-start | bytes 294916
  19.1 7.9 %copy-start.22 = (bf16[128,256]{1,0:T(8,128)(2,1)S(1)}, bf16[128,256]{1,0:T(8,128)(2,1)}, u32[]{:S(2)}) copy-start(bf16[128,256]{1,0:T(8,128)(2,1)} %constant.62.clone.ctl) | copy-start | bytes 196612
  19.2 7.9 %copy-start.23 = (bf16[128,64]{1,0:T(8,128)(2,1)S(1)}, bf16[128,64]{1,0:T(8,128)(2,1)}, u32[]{:S(2)}) copy-start(bf16[128,64]{1,0:T(8,128)(2,1)} %constant.64.clone.put_ctl) | copy-start | bytes 49156
  19.2 7.9 %copy-start.24 = (f32[2,1,128]{2,1,0:T(1,128)S(1)}, f32[2,1,128]{2,1,0:T(1,128)}, u32[]{:S(2)}) copy-start(f32[2,1,128]{2,1,0:T(1,128)} %constant.59.clone.second) | copy-start | bytes 3076
  27.1 14.6 %copy-start.3 = (bf16[4,256,144]{2,1,0:T(8,128)(2,1)S(1)}, bf16[4,256,144]{2,1,0:T(8,128)(2,1)}, u32[]{:S(2)}) copy-start(bf16[4,256,144]{2,1,0:T(8,128)(2,1)} %constant.70.clone.ctl) | copy-start | bytes 884740
  27.1 14.6 %copy-start.5 = (bf16[5,256,128]{2,1,0:T(8,128)(2,1)S(1)}, bf16[5,256,128]{2,1,0:T(8,128)(2,1)}, u32[]{:S(2)}) copy-start(bf16[5,256,128]{2,1,0:T(8,128)(2,1)} %constant.69.clone.comb) | copy-start | bytes 983044
  27.1 14.6 %copy-start.6 = (bf16[1,2,240,144]{3,2,1,0:T(8,128)(2,1)S(1)}, bf16[1,2,240,144]{3,2,1,0:T(8,128)(2,1)}, u32[]{:S(2)}) copy-start(bf16[1,2,240,144]{3,2,1,0:T(8,128)(2,1)} %constant.67.clone.key) | copy-start | bytes 414724
  27.1 14.6 %copy-start.7 = (bf16[256,64]{1,0:T(8,128)(2,1)S(1)}, bf16[256,64]{1,0:T(8,128)(2,1)}, u32[]{:S(2)}) copy-start(bf16[256,64]{1,0:T(8,128)(2,1)} %constant.71.clone.put) | copy-start | bytes 98308
  27.1 14.6 %copy-start.8 = (bf16[1,240,128]{2,1,0:T(8,128)(2,1)S(1)}, bf16[1,240,128]{2,1,0:T(8,128)(2,1)}, u32[]{:S(2)}) copy-start(bf16[1,240,128]{2,1,0:T(8,128)(2,1)} %constant.66.clone.dist) | copy-start | bytes 184324
  27.1 14.5 %copy-start.9 = (bf16[80,256]{1,0:T(8,128)(2,1)S(1)}, bf16[80,256]{1,0:T(8,128)(2,1)}, u32[]{:S(2)}) copy-start(bf16[80,256]{1,0:T(8,128)(2,1)} %constant.65.clone.late) | copy-start | bytes 122884
  27.2 14.5 %copy-start.14 = (f32[1,1,128]{2,1,0:T(1,128)S(1)}, f32[1,1,128]{2,1,0:T(1,128)}, u32[]{:S(2)}) copy-start(f32[1,1,128]{2,1,0:T(1,128)} %constant.68.clone.second) | copy-start | bytes 1540
  37.5 12.1 %collective-permute-start.4 = (bf16[80,1152]{1,0:T(8,128)(2,1)S(1)}, bf16[80,1152]{1,0:T(8,128)(2,1)S(1)}, u32[]{:S(2)}, u32[]{:S(2)}) collective-permute-start(bf16[80,1152]{1,0:T(8,128)(2,1)S(1)} %get-tuple-element.28), channel_id=1, source_target_pairs={{0,16},{16,32},{32,48},{48,64},{64,80},{80,96},{96,112},{112,128},... | collective-permute-start | bytes 552968 | tf_op jit(solution)/shard_map/ppermute | solution.py:566
  37.5 12.0 %collective-permute-start.5 = (bf16[80,1152]{1,0:T(8,128)(2,1)S(1)}, bf16[80,1152]{1,0:T(8,128)(2,1)S(1)}, u32[]{:S(2)}, u32[]{:S(2)}) collective-permute-start(bf16[80,1152]{1,0:T(8,128)(2,1)S(1)} %get-tuple-element.29), channel_id=1, source_target_pairs={{16,0},{32,16},{48,32},{64,48},{80,64},{96,80},{112,96},{128,112},... | collective-permute-start | bytes 552968 | tf_op jit(solution)/shard_map/ppermute | solution.py:565

commit v7 on v6

--- a/solution.py
+++ b/solution.py
@@ -289,11 +289,22 @@
         msg[i, 64:, :256] = jnp.where(rows == 31, row[0:1], ctl[:, :256]).astype(BF)
 
 
-def pack_kernel(msg, above, below, send_rim, west, east):
-    for i, out in ((0, west), (1, east)):
+def choose(odd, a, b):
+    return jnp.where(odd > 0.5, a.astype(F32), b.astype(F32))
+
+
+def pack_kernel(odd, msg, got_a, got_b, send_rim, out_a, out_b, above, below):
+    row_odd, col_odd = odd[0][:1, :1], odd[1][:1, :1]
+    above[...] = choose(row_odd, got_a[...], got_b[...]).astype(BF)
+    below[...] = choose(row_odd, got_b[...], got_a[...]).astype(BF)
+    messages = []
+    for i in (0, 1):
         rim = dot(send_rim[i, :, :64], above[...]) + dot(send_rim[i, :, 64:], below[...])
-        out[:64] = (msg[i, :64].astype(F32) + rim).astype(BF)
-        out[64:] = msg[i, 64:]
+        messages.append(msg[i, :64].astype(F32) + rim)
+    out_a[:64] = choose(col_odd, messages[0], messages[1]).astype(BF)
+    out_b[:64] = choose(col_odd, messages[1], messages[0]).astype(BF)
+    out_a[64:] = choose(col_odd, msg[0, 64:], msg[1, 64:]).astype(BF)
+    out_b[64:] = choose(col_odd, msg[1, 64:], msg[0, 64:]).astype(BF)
 
 
 def middle_kernel(
@@ -357,10 +368,13 @@
 
 
 def edge_kernel(
-    radius, latent, above, below, west, east, valid, mod, w, kv_own, kv_rim, attn_mid, w_out, control,
+    radius, odd, latent, above, below, got_a, got_b, valid, mod, w, kv_own, kv_rim, attn_mid, w_out, control,
     edge, dist, key, second, slot, comb, ctl, ctl_pick, put_ctl,
-    up, down, attn, near, hid, qs, kv, bias,
+    out_a, out_b, attn, west, east, near, hid, qs, kv, bias,
 ):
+    row_odd, col_odd = odd[0] == 1, odd[1] == 1
+    west[...] = jnp.where(col_odd, got_a[...], got_b[...])
+    east[...] = jnp.where(col_odd, got_b[...], got_a[...])
     parts = []
     for i, message in ((0, west), (1, east)):
         at = 0
@@ -407,10 +421,12 @@
     sums, number = block_sums((((1, 3), attn_mid), ((0, 4), attn)), rows, x, w_out, mod, west, east, slot, comb, extra, put_ctl)
     row = lax.broadcasted_iota(jnp.int32, (64, 128), 0)
     lane = lax.broadcasted_iota(jnp.int32, (64, 128), 1)
-    for at, out in ((0, up), (64, down)):
-        out[:64] = sums[at : at + 64].astype(BF)
-        tail = jnp.sum(jnp.where(row == lane, number[at : at + 64], 0.0), axis=0, keepdims=True)
-        out[64:, :128] = jnp.broadcast_to(tail, (16, 128)).astype(BF)
+    tails = []
+    for at in (0, 64):
+        tails.append(jnp.sum(jnp.where(row == lane, number[at : at + 64], 0.0), axis=0, keepdims=True))
+    for out, upward in ((out_a, row_odd), (out_b, jnp.logical_not(row_odd))):
+        out[:64] = jnp.where(upward, sums[:64], sums[64:]).astype(BF)
+        out[64:, :128] = jnp.broadcast_to(jnp.where(upward, tails[0], tails[1]), (16, 128)).astype(BF)
         out[64:, 128:] = jnp.zeros((16, D - 128), BF)
 
 
@@ -457,19 +473,35 @@
     copy.wait()
 
 
-def final_kernel(rest, count, above, below, whole_out, out, done, sem):
+def final_kernel(odd, rest, count, got_a, got_b, whole_out, out, done, sem):
     del whole_out
     row = lax.broadcasted_iota(jnp.int32, (64, 128), 0)
     lane = lax.broadcasted_iota(jnp.int32, (64, 128), 1)
     copies = []
-    for i, ref in ((0, above), (1, below)):
-        tail = ref[64:80, :128].astype(F32)[:1]
+    for i in (0, 1):
+        first, second = (got_a, got_b) if i == 0 else (got_b, got_a)
+        got = choose(odd[0][:1, :1], first[...], second[...])
+        tail = got[64:65, :128]
         number = jnp.sum(jnp.where(row == lane, tail, 0.0), axis=1, keepdims=True) + count[i][:, :1]
-        done[i] = ((rest[i] + ref[:64].astype(F32)) / number).astype(BF)
+        done[i] = ((rest[i] + got[:64]) / number).astype(BF)
         copies.append(pltpu.make_async_copy(done.at[i], out.at[pl.ds(192 * i, 64)], sem.at[i]))
         copies[i].start()
     for copy in copies:
         copy.wait()
+
+
+def swaps(size_r, size_c, by_row, turn):
+    perm = []
+    for r in range(size_r):
+        for c in range(size_c):
+            here, size = (r, size_r) if by_row else (c, size_c)
+            there = ((here + turn) ^ 1) - turn
+            if 0 <= there < size:
+                to = (there, c) if by_row else (r, there)
+            else:
+                to = (r, min(c ^ 1, size_c - 1)) if by_row else (min(r ^ 1, size_r - 1), c)
+            perm.append((r * size_c + c, to[0] * size_c + to[1]))
+    return perm
 
 
 def call(kernel, outs, args, specs=None, out_specs=None, scratch=(), cost=(1e9, 4e6), aliases=None, limit=VMEM):
@@ -495,16 +527,17 @@
 def local(latent, control, valid, radius, modulation, w_qkv, w_out):
     t = tables()
     size_r, size_c = lax.axis_size("trow"), lax.axis_size("tcol")
-    later_r = [(i, (i + 1) % size_r) for i in range(size_r)]
-    sooner_r = [((i + 1) % size_r, i) for i in range(size_r)]
-    later_c = [(i, (i + 1) % size_c) for i in range(size_c)]
-    sooner_c = [((i + 1) % size_c, i) for i in range(size_c)]
-
     x = latent.reshape(256, D)
     control = control.reshape(4, TILE_TOK, D)
     valid = valid.reshape(4, TILE_TOK)
-    above = lax.ppermute(x[192:], "trow", later_r)
-    below = lax.ppermute(x[:64], "trow", sooner_r)
+    row, col = lax.axis_index("trow") % 2, lax.axis_index("tcol") % 2
+    odd = jnp.stack([row, col]).astype(jnp.int32)
+    mark = jnp.broadcast_to(odd.astype(F32)[:, None, None], (2, 8, 128))
+    axes = ("trow", "tcol")
+    by_row = [swaps(size_r, size_c, True, turn) for turn in (0, 1)]
+    by_col = [swaps(size_r, size_c, False, turn) for turn in (0, 1)]
+    near_a = lax.ppermute(lax.dynamic_slice_in_dim(x, 192 * (1 - row), 64, 0), axes, by_row[0])
+    near_b = lax.ppermute(lax.dynamic_slice_in_dim(x, 192 * row, 64, 0), axes, by_row[1])
     smem = pl.BlockSpec(memory_space=pltpu.SMEM)
     hbm = pl.BlockSpec(memory_space=pl.ANY)
 
@@ -522,11 +555,14 @@
         + [pltpu.VMEM((448, D), BF), pltpu.SemaphoreType.DMA((12,))],
         cost=(3.6e9, 12e6),
     )
-    to_west, to_east = call(
-        pack_kernel, [shape(96, D), shape(96, D)], [msg, above, below, t["send_rim"]], cost=(1e8, 1e6)
-    )
-    west = lax.ppermute(to_east, "tcol", later_c)
-    east = lax.ppermute(to_west, "tcol", sooner_c)
+    side_a, side_b, above, below = call(
+        pack_kernel,
+        [shape(96, D), shape(96, D), shape(64, D), shape(64, D)],
+        [mark, msg, near_a, near_b, t["send_rim"]],
+        cost=(1e8, 1e6),
+    )
+    side_a = lax.ppermute(side_a, axes, by_col[0])
+    side_b = lax.ppermute(side_b, axes, by_col[1])
 
     mid, ends, late = slice(1, 4, 2), slice(0, 5, 4), slice(2, 3)
     kv_rim, attn_mid = call(
@@ -545,14 +581,14 @@
         ],
         cost=(8e9, 14e6),
     )
-    up, down, attn_edge = call(
+    sums_a, sums_b, attn_edge, west, east = call(
         edge_kernel,
-        [shape(80, D), shape(80, D), shape(2, D, 256)],
+        [shape(80, D), shape(80, D), shape(2, D, 256), shape(96, D), shape(96, D)],
         [
-            radius, x, above, below, west, east, valid, mod, w, kv_own, kv_rim, attn_mid, w_out, control,
+            radius, odd, x, above, below, side_a, side_b, valid, mod, w, kv_own, kv_rim, attn_mid, w_out, control,
             t["edge"], t["dist_edge"], t["key_edge"], t["second"][ends], t["slot"], t["comb_rim"], t["ctl_rim"], t["ctl_pick"], t["put_rim"],
         ],
-        specs={0: smem},
+        specs={0: smem, 1: smem},
         scratch=[
             pltpu.VMEM((2, 256, D), BF),
             pltpu.VMEM((896, D), BF),
@@ -562,8 +598,8 @@
         ],
         cost=(1e10, 16e6),
     )
-    got_below = lax.ppermute(up, "trow", sooner_r)
-    got_above = lax.ppermute(down, "trow", later_r)
+    sums_a = lax.ppermute(sums_a, axes, by_row[0])
+    sums_b = lax.ppermute(sums_b, axes, by_row[1])
     out, rest, count = call(
         core_kernel,
         [shape(256, D), shape(2, 64, D, dtype=F32), shape(2, 64, 128, dtype=F32)],
@@ -586,11 +622,11 @@
     (out,) = call(
         final_kernel,
         [shape(256, D)],
-        [rest, count, got_above, got_below, out],
-        specs={4: hbm},
+        [mark, rest, count, sums_a, sums_b, out],
+        specs={5: hbm},
         out_specs={0: hbm},
         scratch=[pltpu.VMEM((2, 64, D), BF), pltpu.SemaphoreType.DMA((2,))],
-        aliases={4: 0},
+        aliases={5: 0},
         cost=(2e8, 3e6),
     )
     return out.reshape(CORE, 32, D)

time: 50.8 us -> 56.3 us (1.11)
  the two profiles are of different devices: /device:TPU:8 before, /device:TPU:112 now
where the time goes in v7:
time: 56.3 us; the launch traced here: 56 us
  Pallas kernels  33.6 us (60%)
  local copies, waits for them, and re-layouts  11.1 us (20%)
  starting transfers between devices  8.17 us (15%)
  waiting for transfers between devices  2.57 us (5%)
    pallas_call x6, Pallas kernels, call(): pl.pallas_call(kernel, out_shape=outs, in_specs=[specs.get(i, vmem) for i...  33.6 us
    unnamed x58, local copies, waits for them, and re-layouts  9.32 us
    ppermute x1, starting transfers between devices, local(): lax.ppermute(lax.dynamic_slice_in_dim(x, 192 * (1 - row), 64, 0), axes, b...  3.55 us
    ppermute x1, starting transfers between devices, local(): side_b = lax.ppermute(side_b, axes, by_col[1])  3.01 us
    ppermute x1, waiting for transfers between devices, local(): sums_a = lax.ppermute(sums_a, axes, by_row[0])  2.55 us
    dynamic_slice x1, local copies, waits for them, and re-layouts, local(): lax.dynamic_slice_in_dim(x, 192 * row, 64, 0)  1.7 us
  transfers between devices with their start and end apart: 6, of which 1 were waited for; matrix products, arithmetic and copies ran while one was open for 0% of the time, Pallas kernels for 39%

profile of v7, /device:TPU:112, one launch (start us, length us, event | category | flops | bytes accessed | tf_op | source)
XLA Modules:
  0.0 56.0 jit_solution(17787125048116958647)
XLA Ops:
  0.0 1.7 %constant_dynamic-slice_fusion = (bf16[64,1152]{1,0:T(8,128)(2,1)}, bf16[64,1152]{1,0:T(8,128)(2,1)}) fusion(bf16[256,1152]{1,0:T(8,128)(2,1)} %bitcast.10, s32[]{:T(128)S(6)} %select_n.20, s32[]{:T(128)S(6)} %select_n.19), kind=kLoop, calls=%fused_computation.1 | loop fusion | bytes 589832 | tf_op jit(solution)/shard_map/dynamic_slice | solution.py:540
  1.7 1.0 %collective-permute-start.1 = (bf16[64,1152]{1,0:T(8,128)(2,1)}, bf16[64,1152]{1,0:T(8,128)(2,1)S(1)}, u32[]{:S(2)}, u32[]{:S(2)}) collective-permute-start(bf16[64,1152]{1,0:T(8,128)(2,1)} %get-tuple-element.41), channel_id=1, source_target_pairs={{0,1},{1,0},{2,3},{3,2},{4,5},{5,4},{6,7},{7,6},{8,9},{9,8},{10,11... | collective-permute-start | bytes 442376 | tf_op jit(solution)/shard_map/ppermute | solution.py:540
  2.7 3.6 %collective-permute-start = (bf16[64,1152]{1,0:T(8,128)(2,1)}, bf16[64,1152]{1,0:T(8,128)(2,1)S(1)}, u32[]{:S(2)}, u32[]{:S(2)}) collective-permute-start(bf16[64,1152]{1,0:T(8,128)(2,1)} %get-tuple-element.42), channel_id=1, source_target_pairs={{0,16},{1,17},{2,18},{3,19},{4,20},{5,21},{6,22},{7,23},{8,24},{9,... | collective-permute-start | bytes 442376 | tf_op jit(solution)/shard_map/ppermute | solution.py:539
  6.3 0.0 copy-start.16
  6.3 0.0 copy-start.28
  6.3 6.3 %shard_map.298 = (bf16[2,2,7,32,1152]{4,3,2,1,0:T(8,128)(2,1)S(1)}, bf16[2,96,1152]{2,1,0:T(8,128)(2,1)S(1)}, bf16[1152,3456]{1,0:T(8,128)(2,1)S(1)}) custom-call(bf16[256,1152]{1,0:T(8,128)(2,1)} %bitcast.11, bf16[4,144,1152]{2,1,0:T(8,128)(2,1)} %bitcast.7, s32[4,144]{1,0:T(4,128)} %bitcast.19, f32[3,2,1152]{2,1,0:T(2,128)} %bitcast.15, ...), custom_call_target="tpu_custom_call" | custom-call | flops 3600000000 | bytes 12000000 | tf_op jit(solution)/shard_map/pallas_call | solution.py:511
  12.6 0.0 copy-start
  12.6 3.1 %copy-done = bf16[1152,3456]{1,0:T(8,128)(2,1)} copy-done((bf16[1152,3456]{1,0:T(8,128)(2,1)}, bf16[1152,3456]{1,0:T(8,128)(2,1)S(1)}, u32[]{:S(2)}) %copy-start) | copy-done | bytes 7962648
  15.7 0.1 fusion
  15.8 0.0 collective-permute-done.1.got_b
  15.8 0.0 collective-permute-done.got_a
  15.8 0.1 broadcast_in_dim.2.odd
  15.8 0.0 copy-done.13
  15.8 0.4 shard_map.299
  16.3 0.1 collective-permute-start.2
  16.4 3.0 %collective-permute-start.3 = (bf16[96,1152]{1,0:T(8,128)(2,1)S(1)}, bf16[96,1152]{1,0:T(8,128)(2,1)S(1)}, u32[]{:S(2)}, u32[]{:S(2)}) collective-permute-start(bf16[96,1152]{1,0:T(8,128)(2,1)S(1)} %get-tuple-element.29), channel_id=1, source_target_pairs={{0,16},{1,2},{2,1},{3,4},{4,3},{5,6},{6,5},{7,8},{8,7},{9,10},{10,... | collective-permute-start | bytes 663560 | tf_op jit(solution)/shard_map/ppermute | solution.py:565
  19.4 0.0 copy-done.14
  19.4 0.0 copy-done.16
  19.4 3.3 %copy-done.1 = bf16[1152,3456]{1,0:T(8,128)(2,1)S(1)} copy-done((bf16[1152,3456]{1,0:T(8,128)(2,1)S(1)}, bf16[1152,3456]{1,0:T(8,128)(2,1)}, u32[]{:S(2)}) %copy-start.1) | copy-done | bytes 7962648
  22.7 1.0 %copy-done.18 = bf16[2,2,192,144]{3,2,1,0:T(8,128)(2,1)S(1)} copy-done((bf16[2,2,192,144]{3,2,1,0:T(8,128)(2,1)S(1)}, bf16[2,2,192,144]{3,2,1,0:T(8,128)(2,1)}, u32[]{:S(2)}) %copy-start.18) | copy-done | bytes 221208
  23.7 1.0 %copy-done.20 = bf16[368,384]{1,0:T(8,128)(2,1)S(1)} copy-done((bf16[368,384]{1,0:T(8,128)(2,1)S(1)}, bf16[368,384]{1,0:T(8,128)(2,1)}, u32[]{:S(2)}) %copy-start.20) | copy-done | bytes 282648
  24.6 0.9 %copy-done.24 = bf16[2,192,128]{2,1,0:T(8,128)(2,1)S(1)} copy-done((bf16[2,192,128]{2,1,0:T(8,128)(2,1)S(1)}, bf16[2,192,128]{2,1,0:T(8,128)(2,1)}, u32[]{:S(2)}) %copy-start.24) | copy-done | bytes 98328
  25.5 0.0 copy-start.19
  25.5 0.0 copy-start.21
  25.5 0.0 copy-start.22
  25.6 0.0 copy-start.23
  25.6 0.0 copy-start.25
  25.6 0.0 copy-start.26
  25.6 0.0 copy-start.27
  25.6 7.7 %shard_map.300 = (bf16[2,2,7,16,1152]{4,3,2,1,0:T(8,128)(2,1)S(1)}, bf16[2,1152,256]{2,1,0:T(8,128)(2,1)S(1)}) custom-call(s32[16]{0:T(128)S(1)} %copy-done.16, bf16[256,1152]{1,0:T(8,128)(2,1)S(1)} %bitcast.12, bf16[64,1152]{1,0:T(8,128)(2,1)S(1)} %get-tuple-element.23.above, bf16[64,1152]{1,0:T(8,128)(2,1)S(1)} %get-tuple-element.24.below, ...), custom_call_target="tpu_custom_call" | custom-call | flops 8000000000 | bytes 14000000 | tf_op jit(solution)/shard_map/pallas_call | solution.py:511
  33.3 0.0 collective-permute-done.2.got_a
  33.3 0.0 collective-permute-done.3.got_b
  33.4 0.0 copy-start.6
  33.4 0.0 copy-start.8
  33.4 0.0 copy-start.9
  33.5 0.0 copy-start.10
  33.5 0.0 copy-start.11
  33.5 0.0 copy-start.12
  33.5 0.0 copy-start.17
  33.5 10.4 %shard_map.301 = (bf16[80,1152]{1,0:T(8,128)(2,1)S(1)}, bf16[80,1152]{1,0:T(8,128)(2,1)S(1)}, bf16[2,1152,256]{2,1,0:T(8,128)(2,1)S(1)}, bf16[96,1152]{1,0:T(8,128)(2,1)S(1)}, bf16[96,1152]{1,0:T(8,128)(2,1)S(1)}) custom-call(s32[16]{0:T(128)S(1)} %copy-done.16, s32[2]{0:T(128)S(1)} %get-tuple-element.40.odd, bf16[256,1152]{1,0:T(8,128)(2,1)S(1)} %bitcast.13, ...), custom_call_target="tpu_custom_call" | custom-call | flops 10000000000 | bytes 16000000 | tf_op jit(solution)/shard_map/pallas_call | solution.py:511
  43.9 0.1 collective-permute-start.4
  44.0 0.4 collective-permute-start.5
  44.4 0.0 copy-done.8
  44.4 0.0 copy-done.10
  44.4 7.9 %shard_map.302 = (bf16[256,1152]{1,0:T(8,128)(2,1)}, f32[2,64,1152]{2,1,0:T(8,128)S(1)}, f32[2,64,128]{2,1,0:T(8,128)S(1)}) custom-call(s32[16]{0:T(128)S(1)} %copy-done.16, bf16[2,1152,256]{2,1,0:T(8,128)(2,1)S(1)} %get-tuple-element.27.attn_mid, bf16[2,1152,256]{2,1,0:T(8,128)(2,1)S(1)} %get-tuple-element.31.attn_edge, bf16[256,1152]{1,0:T(8,128)(2,1)S(1)} %bitcast.14, ...), custom_call_target="tpu_custom_call" | custom-call | flops 4000000000 | bytes 8000000 | tf_op jit(solution)/shard_map/pallas_call | solution.py:511
  52.3 2.6 %collective-permute-done.4.got_a = bf16[80,1152]{1,0:T(8,128)(2,1)S(1)} collective-permute-done((bf16[80,1152]{1,0:T(8,128)(2,1)S(1)}, bf16[80,1152]{1,0:T(8,128)(2,1)S(1)}, u32[]{:S(2)}, u32[]{:S(2)}) %collective-permute-start.4) | collective-permute-done | bytes 184352 | tf_op jit(solution)/shard_map/ppermute | solution.py:601
  54.9 0.0 collective-permute-done.5.got_b
  54.9 1.0 %shard_map.303 = bf16[256,1152]{1,0:T(8,128)(2,1)} custom-call(f32[2,8,128]{2,1,0:T(8,128)S(1)} %broadcast_in_dim.2.odd, f32[2,64,1152]{2,1,0:T(8,128)S(1)} %get-tuple-element.34.rest, f32[2,64,128]{2,1,0:T(8,128)S(1)} %get-tuple-element.35.count, bf16[80,1152]{1,0:T(8,128)(2,1)S(1)} %collective-permute-done.4.got_a, ...), custom_call_target="tpu_custom_call", output_to_operand_aliasing={{}: (5, {})} | custom-call | flops 200000000 | bytes 3000000 | tf_op jit(solution)/shard_map/pallas_call | solution.py:511
  (31 shorter events, 0.1 us)
Async XLA Ops:
  1.7 14.1 %collective-permute-start.1 = (bf16[64,1152]{1,0:T(8,128)(2,1)}, bf16[64,1152]{1,0:T(8,128)(2,1)S(1)}, u32[]{:S(2)}, u32[]{:S(2)}) collective-permute-start(bf16[64,1152]{1,0:T(8,128)(2,1)} %get-tuple-element.41), channel_id=1, source_target_pairs={{0,1},{1,0},{2,3},{3,2},{4,5},{5,4},{6,7},{7,6},{8,9},{9,8},{10,11... | collective-permute-start | bytes 442376 | tf_op jit(solution)/shard_map/ppermute | solution.py:540
  2.7 13.0 %collective-permute-start = (bf16[64,1152]{1,0:T(8,128)(2,1)}, bf16[64,1152]{1,0:T(8,128)(2,1)S(1)}, u32[]{:S(2)}, u32[]{:S(2)}) collective-permute-start(bf16[64,1152]{1,0:T(8,128)(2,1)} %get-tuple-element.42), channel_id=1, source_target_pairs={{0,16},{1,17},{2,18},{3,19},{4,20},{5,21},{6,22},{7,23},{8,24},{9,... | collective-permute-start | bytes 442376 | tf_op jit(solution)/shard_map/ppermute | solution.py:539
  6.3 9.5 %copy-start.13 = (bf16[2,64,128]{2,1,0:T(8,128)(2,1)S(1)}, bf16[2,64,128]{2,1,0:T(8,128)(2,1)}, u32[]{:S(2)}) copy-start(bf16[2,64,128]{2,1,0:T(8,128)(2,1)} %constant.82.clone.send_rim) | copy-start | bytes 98308
  6.3 13.1 %copy-start.5 = (bf16[8,32,1152]{2,1,0:T(8,128)(2,1)S(1)}, bf16[8,32,1152]{2,1,0:T(8,128)(2,1)}, u32[]{:S(2)}) copy-start(bf16[8,32,1152]{2,1,0:T(8,128)(2,1)} %param.32) | copy-start | bytes 1769476
  6.3 13.1 %copy-start.14 = (f32[2,3,1152]{2,0,1:T(2,128)S(1)}, f32[2,3,1152]{2,0,1:T(2,128)}, u32[]{:S(2)}) copy-start(f32[2,3,1152]{2,0,1:T(2,128)} %param.36) | copy-start | bytes 82948
  6.3 13.1 %copy-start.15 = (s32[1,4,144]{2,1,0:T(4,128)S(1)}, s32[1,4,144]{2,1,0:T(4,128)}, u32[]{:S(2)}) copy-start(s32[1,4,144]{2,1,0:T(4,128)} %param.34) | copy-start | bytes 6916
  6.3 13.1 %copy-start.16 = (s32[16]{0:T(128)S(1)}, s32[16]{0:T(128)}, u32[]{:S(2)}) copy-start(s32[16]{0:T(128)} %radius.5) | copy-start | bytes 196
  6.3 13.1 %copy-start.28 = (f32[2,1,128]{2,1,0:T(1,128)S(1)}, f32[2,1,128]{2,1,0:T(1,128)}, u32[]{:S(2)}) copy-start(f32[2,1,128]{2,1,0:T(1,128)} %constant.86.clone.second) | copy-start | bytes 3076
  12.6 3.1 %copy-start = (bf16[1152,3456]{1,0:T(8,128)(2,1)}, bf16[1152,3456]{1,0:T(8,128)(2,1)S(1)}, u32[]{:S(2)}) copy-start(bf16[1152,3456]{1,0:T(8,128)(2,1)S(1)} %get-tuple-element.25.w) | copy-start | bytes 23887876
  16.3 17.0 %collective-permute-start.2 = (bf16[96,1152]{1,0:T(8,128)(2,1)S(1)}, bf16[96,1152]{1,0:T(8,128)(2,1)S(1)}, u32[]{:S(2)}, u32[]{:S(2)}) collective-permute-start(bf16[96,1152]{1,0:T(8,128)(2,1)S(1)} %get-tuple-element.28), channel_id=1, source_target_pairs={{0,1},{1,0},{2,3},{3,2},{4,5},{5,4},{6,7},{7,6},{8,9},{9,8},{10,11... | collective-permute-start | bytes 663560 | tf_op jit(solution)/shard_map/ppermute | solution.py:564
  16.4 16.9 %collective-permute-start.3 = (bf16[96,1152]{1,0:T(8,128)(2,1)S(1)}, bf16[96,1152]{1,0:T(8,128)(2,1)S(1)}, u32[]{:S(2)}, u32[]{:S(2)}) collective-permute-start(bf16[96,1152]{1,0:T(8,128)(2,1)S(1)} %get-tuple-element.29), channel_id=1, source_target_pairs={{0,16},{1,2},{2,1},{3,4},{4,3},{5,6},{6,5},{7,8},{8,7},{9,10},{10,... | collective-permute-start | bytes 663560 | tf_op jit(solution)/shard_map/ppermute | solution.py:565
  19.4 3.3 %copy-start.1 = (bf16[1152,3456]{1,0:T(8,128)(2,1)S(1)}, bf16[1152,3456]{1,0:T(8,128)(2,1)}, u32[]{:S(2)}) copy-start(bf16[1152,3456]{1,0:T(8,128)(2,1)} %copy-done) | copy-start | bytes 23887876
  22.7 1.0 %copy-start.18 = (bf16[2,2,192,144]{3,2,1,0:T(8,128)(2,1)S(1)}, bf16[2,2,192,144]{3,2,1,0:T(8,128)(2,1)}, u32[]{:S(2)}) copy-start(bf16[2,2,192,144]{3,2,1,0:T(8,128)(2,1)} %constant.85.clone.key) | copy-start | bytes 663556
  23.7 1.0 %copy-start.20 = (bf16[368,384]{1,0:T(8,128)(2,1)S(1)}, bf16[368,384]{1,0:T(8,128)(2,1)}, u32[]{:S(2)}) copy-start(bf16[368,384]{1,0:T(8,128)(2,1)} %constant.83.clone.middle) | copy-start | bytes 847876
  24.6 0.9 %copy-start.24 = (bf16[2,192,128]{2,1,0:T(8,128)(2,1)S(1)}, bf16[2,192,128]{2,1,0:T(8,128)(2,1)}, u32[]{:S(2)}) copy-start(bf16[2,192,128]{2,1,0:T(8,128)(2,1)} %constant.84.clone.dist) | copy-start | bytes 294916
  25.5 7.8 %copy-start.2 = (bf16[1152,3456]{1,0:T(8,128)(2,1)S(1)}, bf16[1152,3456]{1,0:T(8,128)(2,1)}, u32[]{:S(2)}) copy-start(bf16[1152,3456]{1,0:T(8,128)(2,1)} %copy-done) | copy-start | bytes 23887876
  25.5 7.8 %copy-start.3 = (bf16[1152,1152]{1,0:T(8,128)(2,1)S(1)}, bf16[1152,1152]{1,0:T(8,128)(2,1)}, u32[]{:S(2)}) copy-start(bf16[1152,1152]{1,0:T(8,128)(2,1)} %w_out.3) | copy-start | bytes 7962628
  25.5 7.8 %copy-start.4 = (bf16[1,4,144,1152]{3,2,1,0:T(8,128)(2,1)S(1)}, bf16[1,4,144,1152]{3,2,1,0:T(8,128)(2,1)}, u32[]{:S(2)}) copy-start(bf16[1,4,144,1152]{3,2,1,0:T(8,128)(2,1)} %param.33) | copy-start | bytes 3981316
  25.5 7.8 %copy-start.7 = (bf16[5,2,144,128]{3,2,1,0:T(8,128)(2,1)S(1)}, bf16[5,2,144,128]{3,2,1,0:T(8,128)(2,1)}, u32[]{:S(2)}) copy-start(bf16[5,2,144,128]{3,2,1,0:T(8,128)(2,1)} %constant.90.clone.slot) | copy-start | bytes 1105924
  25.5 7.8 %copy-start.19 = (bf16[4,144,256]{2,1,0:T(8,128)(2,1)S(1)}, bf16[4,144,256]{2,1,0:T(8,128)(2,1)}, u32[]{:S(2)}) copy-start(bf16[4,144,256]{2,1,0:T(8,128)(2,1)} %constant.93.clone.ctl_pick) | copy-start | bytes 884740
  25.5 7.8 %copy-start.21 = (bf16[2,224,256]{2,1,0:T(8,128)(2,1)S(1)}, bf16[2,224,256]{2,1,0:T(8,128)(2,1)}, u32[]{:S(2)}) copy-start(bf16[2,224,256]{2,1,0:T(8,128)(2,1)} %constant.87.clone.edge) | copy-start | bytes 688132
  25.5 7.8 %copy-start.22 = (bf16[5,128,128]{2,1,0:T(8,128)(2,1)S(1)}, bf16[5,128,128]{2,1,0:T(8,128)(2,1)}, u32[]{:S(2)}) copy-start(bf16[5,128,128]{2,1,0:T(8,128)(2,1)} %constant.91.clone.comb) | copy-start | bytes 491524
  25.6 7.8 %copy-start.23 = (bf16[2,192,128]{2,1,0:T(8,128)(2,1)S(1)}, bf16[2,192,128]{2,1,0:T(8,128)(2,1)}, u32[]{:S(2)}) copy-start(bf16[2,192,128]{2,1,0:T(8,128)(2,1)} %constant.88.clone.dist) | copy-start | bytes 294916
  25.6 7.8 %copy-start.25 = (bf16[128,256]{1,0:T(8,128)(2,1)S(1)}, bf16[128,256]{1,0:T(8,128)(2,1)}, u32[]{:S(2)}) copy-start(bf16[128,256]{1,0:T(8,128)(2,1)} %constant.92.clone.ctl) | copy-start | bytes 196612
  25.6 7.8 %copy-start.26 = (bf16[128,64]{1,0:T(8,128)(2,1)S(1)}, bf16[128,64]{1,0:T(8,128)(2,1)}, u32[]{:S(2)}) copy-start(bf16[128,64]{1,0:T(8,128)(2,1)} %constant.94.clone.put_ctl) | copy-start | bytes 49156
  25.6 7.8 %copy-start.27 = (f32[2,1,128]{2,1,0:T(1,128)S(1)}, f32[2,1,128]{2,1,0:T(1,128)}, u32[]{:S(2)}) copy-start(f32[2,1,128]{2,1,0:T(1,128)} %constant.89.clone.second) | copy-start | bytes 3076
  33.4 10.9 %copy-start.6 = (bf16[4,256,144]{2,1,0:T(8,128)(2,1)S(1)}, bf16[4,256,144]{2,1,0:T(8,128)(2,1)}, u32[]{:S(2)}) copy-start(bf16[4,256,144]{2,1,0:T(8,128)(2,1)} %constant.100.clone.ctl) | copy-start | bytes 884740
  33.4 10.9 %copy-start.8 = (bf16[5,256,128]{2,1,0:T(8,128)(2,1)S(1)}, bf16[5,256,128]{2,1,0:T(8,128)(2,1)}, u32[]{:S(2)}) copy-start(bf16[5,256,128]{2,1,0:T(8,128)(2,1)} %constant.99.clone.comb) | copy-start | bytes 983044
  33.4 10.9 %copy-start.9 = (bf16[1,2,240,144]{3,2,1,0:T(8,128)(2,1)S(1)}, bf16[1,2,240,144]{3,2,1,0:T(8,128)(2,1)}, u32[]{:S(2)}) copy-start(bf16[1,2,240,144]{3,2,1,0:T(8,128)(2,1)} %constant.97.clone.key) | copy-start | bytes 414724
  33.5 10.9 %copy-start.10 = (bf16[256,64]{1,0:T(8,128)(2,1)S(1)}, bf16[256,64]{1,0:T(8,128)(2,1)}, u32[]{:S(2)}) copy-start(bf16[256,64]{1,0:T(8,128)(2,1)} %constant.101.clone.put) | copy-start | bytes 98308
  33.5 10.9 %copy-start.11 = (bf16[1,240,128]{2,1,0:T(8,128)(2,1)S(1)}, bf16[1,240,128]{2,1,0:T(8,128)(2,1)}, u32[]{:S(2)}) copy-start(bf16[1,240,128]{2,1,0:T(8,128)(2,1)} %constant.96.clone.dist) | copy-start | bytes 184324
  33.5 10.9 %copy-start.12 = (bf16[80,256]{1,0:T(8,128)(2,1)S(1)}, bf16[80,256]{1,0:T(8,128)(2,1)}, u32[]{:S(2)}) copy-start(bf16[80,256]{1,0:T(8,128)(2,1)} %constant.95.clone.late) | copy-start | bytes 122884
  33.5 10.9 %copy-start.17 = (f32[1,1,128]{2,1,0:T(1,128)S(1)}, f32[1,1,128]{2,1,0:T(1,128)}, u32[]{:S(2)}) copy-start(f32[1,1,128]{2,1,0:T(1,128)} %constant.98.clone.second) | copy-start | bytes 1540
  43.9 11.0 %collective-permute-start.4 = (bf16[80,1152]{1,0:T(8,128)(2,1)S(1)}, bf16[80,1152]{1,0:T(8,128)(2,1)S(1)}, u32[]{:S(2)}, u32[]{:S(2)}) collective-permute-start(bf16[80,1152]{1,0:T(8,128)(2,1)S(1)} %get-tuple-element.36), channel_id=1, source_target_pairs={{0,16},{1,17},{2,18},{3,19},{4,20},{5,21},{6,22},{7,23},{8,24},{9,... | collective-permute-start | bytes 552968 | tf_op jit(solution)/shard_map/ppermute | solution.py:601
  44.0 10.9 %collective-permute-start.5 = (bf16[80,1152]{1,0:T(8,128)(2,1)S(1)}, bf16[80,1152]{1,0:T(8,128)(2,1)S(1)}, u32[]{:S(2)}, u32[]{:S(2)}) collective-permute-start(bf16[80,1152]{1,0:T(8,128)(2,1)S(1)} %get-tuple-element.37), channel_id=1, source_target_pairs={{0,1},{1,0},{2,3},{3,2},{4,5},{5,4},{6,7},{7,6},{8,9},{9,8},{10,11... | collective-permute-start | bytes 552968 | tf_op jit(solution)/shard_map/ppermute | solution.py:602

commit v8 on v7

--- a/solution.py
+++ b/solution.py
@@ -247,9 +247,10 @@
 
 
 def own_kernel(
-    latent_h, control_h, valid_h, mod_h, w_h, own_h, send_own_h, send_ctl_h, valid_pad_h,
-    kv, msg, w, latent, control, valid, mod, own, send_own, send_ctl, valid_pad, hid, sem,
+    latent_h, control_h, valid_h, mod_h, w_h, own_h, send_own_h, send_ctl_h, valid_pad_h, mark,
+    kv, msg, w, odd, latent, control, valid, mod, own, send_own, send_ctl, valid_pad, hid, sem,
 ):
+    odd[...] = mark[...]
     pairs = [
         (latent_h, latent),
         (own_h, own),
@@ -372,9 +373,9 @@
     edge, dist, key, second, slot, comb, ctl, ctl_pick, put_ctl,
     out_a, out_b, attn, west, east, near, hid, qs, kv, bias,
 ):
-    row_odd, col_odd = odd[0] == 1, odd[1] == 1
-    west[...] = jnp.where(col_odd, got_a[...], got_b[...])
-    east[...] = jnp.where(col_odd, got_b[...], got_a[...])
+    row_odd, col_odd = odd[0][:1, :1], odd[1][:1, :1]
+    west[...] = choose(col_odd, got_a[...], got_b[...]).astype(BF)
+    east[...] = choose(col_odd, got_b[...], got_a[...]).astype(BF)
     parts = []
     for i, message in ((0, west), (1, east)):
         at = 0
@@ -424,9 +425,9 @@
     tails = []
     for at in (0, 64):
         tails.append(jnp.sum(jnp.where(row == lane, number[at : at + 64], 0.0), axis=0, keepdims=True))
-    for out, upward in ((out_a, row_odd), (out_b, jnp.logical_not(row_odd))):
-        out[:64] = jnp.where(upward, sums[:64], sums[64:]).astype(BF)
-        out[64:, :128] = jnp.broadcast_to(jnp.where(upward, tails[0], tails[1]), (16, 128)).astype(BF)
+    for out, upward in ((out_a, row_odd), (out_b, 1.0 - row_odd)):
+        out[:64] = choose(upward, sums[:64], sums[64:]).astype(BF)
+        out[64:, :128] = jnp.broadcast_to(choose(upward, tails[0], tails[1]), (16, 128)).astype(BF)
         out[64:, 128:] = jnp.zeros((16, D - 128), BF)
 
 
@@ -531,8 +532,7 @@
     control = control.reshape(4, TILE_TOK, D)
     valid = valid.reshape(4, TILE_TOK)
     row, col = lax.axis_index("trow") % 2, lax.axis_index("tcol") % 2
-    odd = jnp.stack([row, col]).astype(jnp.int32)
-    mark = jnp.broadcast_to(odd.astype(F32)[:, None, None], (2, 8, 128))
+    mark = jnp.broadcast_to(jnp.stack([row, col]).astype(F32)[:, None, None], (2, 8, 128))
     axes = ("trow", "tcol")
     by_row = [swaps(size_r, size_c, True, turn) for turn in (0, 1)]
     by_col = [swaps(size_r, size_c, False, turn) for turn in (0, 1)]
@@ -546,10 +546,10 @@
     first = [x, control, valid, mod, w_qkv, t["own"], t["send_own"], t["send_ctl"], t["valid_pad"]]
     staged = [(256, D, BF), (2, TILE_TOK, D, BF), (4, TILE_TOK, jnp.int32), (3, 2, D, F32)]
     staged += [t[k].shape + (BF,) for k in ("own", "send_own", "send_ctl", "valid_pad")]
-    kv_own, msg, w = call(
+    kv_own, msg, w, mark = call(
         own_kernel,
-        [shape(2, 2, 7, 32, D), shape(2, 96, D), shape(D, 3 * D)],
-        [far(a) for a in first],
+        [shape(2, 2, 7, 32, D), shape(2, 96, D), shape(D, 3 * D), shape(2, 8, 128, dtype=F32)],
+        [far(a) for a in first] + [mark],
         specs={i: hbm for i in range(len(first))},
         scratch=[pltpu.VMEM(s[:-1], s[-1]) for s in staged]
         + [pltpu.VMEM((448, D), BF), pltpu.SemaphoreType.DMA((12,))],
@@ -585,10 +585,10 @@
         edge_kernel,
         [shape(80, D), shape(80, D), shape(2, D, 256), shape(96, D), shape(96, D)],
         [
-            radius, odd, x, above, below, side_a, side_b, valid, mod, w, kv_own, kv_rim, attn_mid, w_out, control,
+            radius, mark, x, above, below, side_a, side_b, valid, mod, w, kv_own, kv_rim, attn_mid, w_out, control,
             t["edge"], t["dist_edge"], t["key_edge"], t["second"][ends], t["slot"], t["comb_rim"], t["ctl_rim"], t["ctl_pick"], t["put_rim"],
         ],
-        specs={0: smem, 1: smem},
+        specs={0: smem},
         scratch=[
             pltpu.VMEM((2, 256, D), BF),
             pltpu.VMEM((896, D), BF),

time: 56.3 us -> 46.4 us (0.82)
  local copies, waits for them, and re-layouts: 11.1 us -> 1.24 us
    unnamed x58 -> x52, local copies, waits for them, and re-layouts: 9.32 us -> 0.16 us
    dynamic_slice x1, local copies, waits for them, and re-layouts: 1.7 us -> 1 us  [local(): lax.dynamic_slice_in_dim(x, 192 * row, 64, 0)]
  transfers between devices with their start and end apart: 6 -> 6, of which waited for: 1 -> 1; matrix products, arithmetic and copies ran while one was open for 0% -> 0% of each run, Pallas kernels for 39% -> 47%
where the time goes in v8:
time: 46.4 us; the launch traced here: 46.3 us
  Pallas kernels  33.5 us (72%)
  starting transfers between devices  8.26 us (18%)
  waiting for transfers between devices  2.65 us (6%)
  local copies, waits for them, and re-layouts  1.24 us (3%)
  between operations  0.6 us (1%)
    pallas_call x6, Pallas kernels, call(): pl.pallas_call(kernel, out_shape=outs, in_specs=[specs.get(i, vmem) for i...  33.5 us
    ppermute x1, starting transfers between devices, local(): lax.ppermute(lax.dynamic_slice_in_dim(x, 192 * (1 - row), 64, 0), axes, b...  3.56 us
    ppermute x1, starting transfers between devices, local(): side_b = lax.ppermute(side_b, axes, by_col[1])  3.02 us
    ppermute x1, waiting for transfers between devices, local(): sums_a = lax.ppermute(sums_a, axes, by_row[0])  2.64 us
    ppermute x1, starting transfers between devices, local(): lax.ppermute(lax.dynamic_slice_in_dim(x, 192 * row, 64, 0), axes, by_row[1])  1.12 us
    dynamic_slice x1, local copies, waits for them, and re-layouts, local(): lax.dynamic_slice_in_dim(x, 192 * row, 64, 0)  1 us
  transfers between devices with their start and end apart: 6, of which 1 were waited for; matrix products, arithmetic and copies ran while one was open for 0% of the time, Pallas kernels for 47%

profile of v8, /device:TPU:112, one launch (start us, length us, event | category | flops | bytes accessed | tf_op | source)
XLA Modules:
  0.0 46.3 jit_solution(8166067554510677478)
XLA Ops:
  0.0 1.0 %constant_dynamic-slice_fusion = (bf16[64,1152]{1,0:T(8,128)(2,1)S(1)}, bf16[64,1152]{1,0:T(8,128)(2,1)S(1)}) fusion(bf16[256,1152]{1,0:T(8,128)(2,1)} %bitcast.10, s32[]{:T(128)S(6)} %select_n.20, s32[]{:T(128)S(6)} %select_n.19), kind=kLoop, calls=%fused_computation.1 | loop fusion | bytes 589832 | tf_op jit(solution)/shard_map/dynamic_slice | solution.py:540
  1.0 1.1 %collective-permute-start.1 = (bf16[64,1152]{1,0:T(8,128)(2,1)S(1)}, bf16[64,1152]{1,0:T(8,128)(2,1)S(1)}, u32[]{:S(2)}, u32[]{:S(2)}) collective-permute-start(bf16[64,1152]{1,0:T(8,128)(2,1)S(1)} %get-tuple-element.41), channel_id=1, source_target_pairs={{0,1},{1,0},{2,3},{3,2},{4,5},{5,4},{6,7},{7,6},{8,9},{9,8},{10,11... | collective-permute-start | bytes 442376 | tf_op jit(solution)/shard_map/ppermute | solution.py:540
  2.1 3.6 %collective-permute-start = (bf16[64,1152]{1,0:T(8,128)(2,1)S(1)}, bf16[64,1152]{1,0:T(8,128)(2,1)S(1)}, u32[]{:S(2)}, u32[]{:S(2)}) collective-permute-start(bf16[64,1152]{1,0:T(8,128)(2,1)S(1)} %get-tuple-element.42), channel_id=1, source_target_pairs={{0,16},{1,17},{2,18},{3,19},{4,20},{5,21},{6,22},{7,23},{8,24},{9,... | collective-permute-start | bytes 442376 | tf_op jit(solution)/shard_map/ppermute | solution.py:539
  5.7 0.1 add_convert_fusion
  5.8 0.1 broadcast_in_dim.2.mark
  5.8 0.0 copy-start.13
  5.9 0.0 copy-start.15
  5.9 0.0 copy-start.17
  5.9 0.0 copy-start.21
  5.9 0.0 copy-start.25
  5.9 6.3 %shard_map.298 = (bf16[2,2,7,32,1152]{4,3,2,1,0:T(8,128)(2,1)S(1)}, bf16[2,96,1152]{2,1,0:T(8,128)(2,1)S(1)}, bf16[1152,3456]{1,0:T(8,128)(2,1)S(1)}, f32[2,8,128]{2,1,0:T(8,128)S(1)}) custom-call(bf16[256,1152]{1,0:T(8,128)(2,1)} %bitcast.11, bf16[4,144,1152]{2,1,0:T(8,128)(2,1)} %bitcast.7, s32[4,144]{1,0:T(4,128)} %bitcast.19, f32[3,2,1152]{2,1,0:T(2,128)} %bitcast.15, ...), custom_call_target="tpu_custom_call" | custom-call | flops 3600000000 | bytes 12000000 | tf_op jit(solution)/shard_map/pallas_call | solution.py:512
  12.2 0.0 collective-permute-done.1.got_b
  12.2 0.0 collective-permute-done.got_a
  12.2 0.0 copy-done.10
  12.2 0.4 shard_map.299
  12.7 0.1 collective-permute-start.2
  12.8 3.0 %collective-permute-start.3 = (bf16[96,1152]{1,0:T(8,128)(2,1)S(1)}, bf16[96,1152]{1,0:T(8,128)(2,1)S(1)}, u32[]{:S(2)}, u32[]{:S(2)}) collective-permute-start(bf16[96,1152]{1,0:T(8,128)(2,1)S(1)} %get-tuple-element.31), channel_id=1, source_target_pairs={{0,16},{1,2},{2,1},{3,4},{4,3},{5,6},{6,5},{7,8},{8,7},{9,10},{10,... | collective-permute-start | bytes 663560 | tf_op jit(solution)/shard_map/ppermute | solution.py:565
  15.8 0.0 copy-done.2
  15.8 0.0 copy-done.11
  15.8 0.0 copy-done.12
  15.8 0.0 copy-start
  15.8 0.0 copy-start.1
  15.9 0.0 copy-start.4
  15.9 0.0 copy-start.16
  15.9 0.0 copy-start.18
  15.9 0.0 copy-start.19
  15.9 0.0 copy-start.20
  15.9 0.0 copy-start.22
  15.9 0.0 copy-start.23
  15.9 0.0 copy-start.24
  16.0 7.7 %shard_map.300 = (bf16[2,2,7,16,1152]{4,3,2,1,0:T(8,128)(2,1)S(1)}, bf16[2,1152,256]{2,1,0:T(8,128)(2,1)S(1)}) custom-call(s32[16]{0:T(128)S(1)} %copy-done.13, bf16[256,1152]{1,0:T(8,128)(2,1)S(1)} %bitcast.12, bf16[64,1152]{1,0:T(8,128)(2,1)S(1)} %get-tuple-element.25.above, bf16[64,1152]{1,0:T(8,128)(2,1)S(1)} %get-tuple-element.26.below, ...), custom_call_target="tpu_custom_call" | custom-call | flops 8000000000 | bytes 14000000 | tf_op jit(solution)/shard_map/pallas_call | solution.py:512
  23.6 0.0 collective-permute-done.2.got_a
  23.6 0.0 collective-permute-done.3.got_b
  23.7 0.0 copy-start.3
  23.7 0.0 copy-start.5
  23.8 0.0 copy-start.6
  23.8 0.0 copy-start.7
  23.8 0.0 copy-start.8
  23.8 0.0 copy-start.9
  23.8 0.0 copy-start.14
  23.8 10.3 %shard_map.301 = (bf16[80,1152]{1,0:T(8,128)(2,1)S(1)}, bf16[80,1152]{1,0:T(8,128)(2,1)S(1)}, bf16[2,1152,256]{2,1,0:T(8,128)(2,1)S(1)}, bf16[96,1152]{1,0:T(8,128)(2,1)S(1)}, bf16[96,1152]{1,0:T(8,128)(2,1)S(1)}) custom-call(s32[16]{0:T(128)S(1)} %copy-done.13, f32[2,8,128]{2,1,0:T(8,128)S(1)} %get-tuple-element.23.odd, bf16[256,1152]{1,0:T(8,128)(2,1)S(1)} %bitcast.13, ...), custom_call_target="tpu_custom_call" | custom-call | flops 10000000000 | bytes 16000000 | tf_op jit(solution)/shard_map/pallas_call | solution.py:512
  34.1 0.4 collective-permute-start.4
  34.5 0.1 collective-permute-start.5
  34.6 0.0 copy-done.6
  34.6 7.9 %shard_map.302 = (bf16[256,1152]{1,0:T(8,128)(2,1)}, f32[2,64,1152]{2,1,0:T(8,128)S(1)}, f32[2,64,128]{2,1,0:T(8,128)S(1)}) custom-call(s32[16]{0:T(128)S(1)} %copy-done.13, bf16[2,1152,256]{2,1,0:T(8,128)(2,1)S(1)} %get-tuple-element.29.attn_mid, bf16[2,1152,256]{2,1,0:T(8,128)(2,1)S(1)} %get-tuple-element.33.attn_edge, bf16[256,1152]{1,0:T(8,128)(2,1)S(1)} %bitcast.14, ...), custom_call_target="tpu_custom_call" | custom-call | flops 4000000000 | bytes 8000000 | tf_op jit(solution)/shard_map/pallas_call | solution.py:512
  42.5 2.6 %collective-permute-done.4.got_a = bf16[80,1152]{1,0:T(8,128)(2,1)S(1)} collective-permute-done((bf16[80,1152]{1,0:T(8,128)(2,1)S(1)}, bf16[80,1152]{1,0:T(8,128)(2,1)S(1)}, u32[]{:S(2)}, u32[]{:S(2)}) %collective-permute-start.4) | collective-permute-done | bytes 184352 | tf_op jit(solution)/shard_map/ppermute | solution.py:601
  45.1 0.0 collective-permute-done.5.got_b
  45.1 1.0 %shard_map.303 = bf16[256,1152]{1,0:T(8,128)(2,1)} custom-call(f32[2,8,128]{2,1,0:T(8,128)S(1)} %get-tuple-element.23.odd, f32[2,64,1152]{2,1,0:T(8,128)S(1)} %get-tuple-element.36.rest, f32[2,64,128]{2,1,0:T(8,128)S(1)} %get-tuple-element.37.count, bf16[80,1152]{1,0:T(8,128)(2,1)S(1)} %collective-permute-done.4.got_a, ...), custom_call_target="tpu_custom_call", output_to_operand_aliasing={{}: (5, {})} | custom-call | flops 200000000 | bytes 3000000 | tf_op jit(solution)/shard_map/pallas_call | solution.py:512
  (25 shorter events, 0.1 us)
Async XLA Ops:
  1.0 11.2 %collective-permute-start.1 = (bf16[64,1152]{1,0:T(8,128)(2,1)S(1)}, bf16[64,1152]{1,0:T(8,128)(2,1)S(1)}, u32[]{:S(2)}, u32[]{:S(2)}) collective-permute-start(bf16[64,1152]{1,0:T(8,128)(2,1)S(1)} %get-tuple-element.41), channel_id=1, source_target_pairs={{0,1},{1,0},{2,3},{3,2},{4,5},{5,4},{6,7},{7,6},{8,9},{9,8},{10,11... | collective-permute-start | bytes 442376 | tf_op jit(solution)/shard_map/ppermute | solution.py:540
  2.1 10.1 %collective-permute-start = (bf16[64,1152]{1,0:T(8,128)(2,1)S(1)}, bf16[64,1152]{1,0:T(8,128)(2,1)S(1)}, u32[]{:S(2)}, u32[]{:S(2)}) collective-permute-start(bf16[64,1152]{1,0:T(8,128)(2,1)S(1)} %get-tuple-element.42), channel_id=1, source_target_pairs={{0,16},{1,17},{2,18},{3,19},{4,20},{5,21},{6,22},{7,23},{8,24},{9,... | collective-permute-start | bytes 442376 | tf_op jit(solution)/shard_map/ppermute | solution.py:539
  5.8 6.4 %copy-start.10 = (bf16[2,64,128]{2,1,0:T(8,128)(2,1)S(1)}, bf16[2,64,128]{2,1,0:T(8,128)(2,1)}, u32[]{:S(2)}) copy-start(bf16[2,64,128]{2,1,0:T(8,128)(2,1)} %constant.82.clone.send_rim) | copy-start | bytes 98308
  5.8 9.9 %copy-start.2 = (bf16[8,32,1152]{2,1,0:T(8,128)(2,1)S(1)}, bf16[8,32,1152]{2,1,0:T(8,128)(2,1)}, u32[]{:S(2)}) copy-start(bf16[8,32,1152]{2,1,0:T(8,128)(2,1)} %param.32) | copy-start | bytes 1769476
  5.8 9.9 %copy-start.11 = (f32[2,3,1152]{2,0,1:T(2,128)S(1)}, f32[2,3,1152]{2,0,1:T(2,128)}, u32[]{:S(2)}) copy-start(f32[2,3,1152]{2,0,1:T(2,128)} %param.36) | copy-start | bytes 82948
  5.8 9.9 %copy-start.12 = (s32[1,4,144]{2,1,0:T(4,128)S(1)}, s32[1,4,144]{2,1,0:T(4,128)}, u32[]{:S(2)}) copy-start(s32[1,4,144]{2,1,0:T(4,128)} %param.34) | copy-start | bytes 6916
  5.8 9.9 %copy-start.13 = (s32[16]{0:T(128)S(1)}, s32[16]{0:T(128)}, u32[]{:S(2)}) copy-start(s32[16]{0:T(128)} %radius.5) | copy-start | bytes 196
  5.9 9.9 %copy-start.15 = (bf16[2,2,192,144]{3,2,1,0:T(8,128)(2,1)S(1)}, bf16[2,2,192,144]{3,2,1,0:T(8,128)(2,1)}, u32[]{:S(2)}) copy-start(bf16[2,2,192,144]{3,2,1,0:T(8,128)(2,1)} %constant.85.clone.key) | copy-start | bytes 663556
  5.9 9.9 %copy-start.17 = (bf16[368,384]{1,0:T(8,128)(2,1)S(1)}, bf16[368,384]{1,0:T(8,128)(2,1)}, u32[]{:S(2)}) copy-start(bf16[368,384]{1,0:T(8,128)(2,1)} %constant.83.clone.middle) | copy-start | bytes 847876
  5.9 9.9 %copy-start.21 = (bf16[2,192,128]{2,1,0:T(8,128)(2,1)S(1)}, bf16[2,192,128]{2,1,0:T(8,128)(2,1)}, u32[]{:S(2)}) copy-start(bf16[2,192,128]{2,1,0:T(8,128)(2,1)} %constant.84.clone.dist) | copy-start | bytes 294916
  5.9 9.9 %copy-start.25 = (f32[2,1,128]{2,1,0:T(1,128)S(1)}, f32[2,1,128]{2,1,0:T(1,128)}, u32[]{:S(2)}) copy-start(f32[2,1,128]{2,1,0:T(1,128)} %constant.86.clone.second) | copy-start | bytes 3076
  12.7 11.0 %collective-permute-start.2 = (bf16[96,1152]{1,0:T(8,128)(2,1)S(1)}, bf16[96,1152]{1,0:T(8,128)(2,1)S(1)}, u32[]{:S(2)}, u32[]{:S(2)}) collective-permute-start(bf16[96,1152]{1,0:T(8,128)(2,1)S(1)} %get-tuple-element.30), channel_id=1, source_target_pairs={{0,1},{1,0},{2,3},{3,2},{4,5},{5,4},{6,7},{7,6},{8,9},{9,8},{10,11... | collective-permute-start | bytes 663560 | tf_op jit(solution)/shard_map/ppermute | solution.py:564
  12.8 10.9 %collective-permute-start.3 = (bf16[96,1152]{1,0:T(8,128)(2,1)S(1)}, bf16[96,1152]{1,0:T(8,128)(2,1)S(1)}, u32[]{:S(2)}, u32[]{:S(2)}) collective-permute-start(bf16[96,1152]{1,0:T(8,128)(2,1)S(1)} %get-tuple-element.31), channel_id=1, source_target_pairs={{0,16},{1,2},{2,1},{3,4},{4,3},{5,6},{6,5},{7,8},{8,7},{9,10},{10,... | collective-permute-start | bytes 663560 | tf_op jit(solution)/shard_map/ppermute | solution.py:565
  15.8 7.8 %copy-start = (bf16[1152,1152]{1,0:T(8,128)(2,1)S(1)}, bf16[1152,1152]{1,0:T(8,128)(2,1)}, u32[]{:S(2)}) copy-start(bf16[1152,1152]{1,0:T(8,128)(2,1)} %w_out.3) | copy-start | bytes 7962628
  15.8 7.8 %copy-start.1 = (bf16[1,4,144,1152]{3,2,1,0:T(8,128)(2,1)S(1)}, bf16[1,4,144,1152]{3,2,1,0:T(8,128)(2,1)}, u32[]{:S(2)}) copy-start(bf16[1,4,144,1152]{3,2,1,0:T(8,128)(2,1)} %param.33) | copy-start | bytes 3981316
  15.9 7.8 %copy-start.4 = (bf16[5,2,144,128]{3,2,1,0:T(8,128)(2,1)S(1)}, bf16[5,2,144,128]{3,2,1,0:T(8,128)(2,1)}, u32[]{:S(2)}) copy-start(bf16[5,2,144,128]{3,2,1,0:T(8,128)(2,1)} %constant.90.clone.slot) | copy-start | bytes 1105924
  15.9 7.8 %copy-start.16 = (bf16[4,144,256]{2,1,0:T(8,128)(2,1)S(1)}, bf16[4,144,256]{2,1,0:T(8,128)(2,1)}, u32[]{:S(2)}) copy-start(bf16[4,144,256]{2,1,0:T(8,128)(2,1)} %constant.93.clone.ctl_pick) | copy-start | bytes 884740
  15.9 7.8 %copy-start.18 = (bf16[2,224,256]{2,1,0:T(8,128)(2,1)S(1)}, bf16[2,224,256]{2,1,0:T(8,128)(2,1)}, u32[]{:S(2)}) copy-start(bf16[2,224,256]{2,1,0:T(8,128)(2,1)} %constant.87.clone.edge) | copy-start | bytes 688132
  15.9 7.8 %copy-start.19 = (bf16[5,128,128]{2,1,0:T(8,128)(2,1)S(1)}, bf16[5,128,128]{2,1,0:T(8,128)(2,1)}, u32[]{:S(2)}) copy-start(bf16[5,128,128]{2,1,0:T(8,128)(2,1)} %constant.91.clone.comb) | copy-start | bytes 491524
  15.9 7.8 %copy-start.20 = (bf16[2,192,128]{2,1,0:T(8,128)(2,1)S(1)}, bf16[2,192,128]{2,1,0:T(8,128)(2,1)}, u32[]{:S(2)}) copy-start(bf16[2,192,128]{2,1,0:T(8,128)(2,1)} %constant.88.clone.dist) | copy-start | bytes 294916
  15.9 7.8 %copy-start.22 = (bf16[128,256]{1,0:T(8,128)(2,1)S(1)}, bf16[128,256]{1,0:T(8,128)(2,1)}, u32[]{:S(2)}) copy-start(bf16[128,256]{1,0:T(8,128)(2,1)} %constant.92.clone.ctl) | copy-start | bytes 196612
  15.9 7.8 %copy-start.23 = (bf16[128,64]{1,0:T(8,128)(2,1)S(1)}, bf16[128,64]{1,0:T(8,128)(2,1)}, u32[]{:S(2)}) copy-start(bf16[128,64]{1,0:T(8,128)(2,1)} %constant.94.clone.put_ctl) | copy-start | bytes 49156
  15.9 7.8 %copy-start.24 = (f32[2,1,128]{2,1,0:T(1,128)S(1)}, f32[2,1,128]{2,1,0:T(1,128)}, u32[]{:S(2)}) copy-start(f32[2,1,128]{2,1,0:T(1,128)} %constant.89.clone.second) | copy-start | bytes 3076
  23.7 10.9 %copy-start.3 = (bf16[4,256,144]{2,1,0:T(8,128)(2,1)S(1)}, bf16[4,256,144]{2,1,0:T(8,128)(2,1)}, u32[]{:S(2)}) copy-start(bf16[4,256,144]{2,1,0:T(8,128)(2,1)} %constant.100.clone.ctl) | copy-start | bytes 884740
  23.7 10.8 %copy-start.5 = (bf16[5,256,128]{2,1,0:T(8,128)(2,1)S(1)}, bf16[5,256,128]{2,1,0:T(8,128)(2,1)}, u32[]{:S(2)}) copy-start(bf16[5,256,128]{2,1,0:T(8,128)(2,1)} %constant.99.clone.comb) | copy-start | bytes 983044
  23.8 10.8 %copy-start.6 = (bf16[1,2,240,144]{3,2,1,0:T(8,128)(2,1)S(1)}, bf16[1,2,240,144]{3,2,1,0:T(8,128)(2,1)}, u32[]{:S(2)}) copy-start(bf16[1,2,240,144]{3,2,1,0:T(8,128)(2,1)} %constant.97.clone.key) | copy-start | bytes 414724
  23.8 10.8 %copy-start.7 = (bf16[256,64]{1,0:T(8,128)(2,1)S(1)}, bf16[256,64]{1,0:T(8,128)(2,1)}, u32[]{:S(2)}) copy-start(bf16[256,64]{1,0:T(8,128)(2,1)} %constant.101.clone.put) | copy-start | bytes 98308
  23.8 10.8 %copy-start.8 = (bf16[1,240,128]{2,1,0:T(8,128)(2,1)S(1)}, bf16[1,240,128]{2,1,0:T(8,128)(2,1)}, u32[]{:S(2)}) copy-start(bf16[1,240,128]{2,1,0:T(8,128)(2,1)} %constant.96.clone.dist) | copy-start | bytes 184324
  23.8 10.8 %copy-start.9 = (bf16[80,256]{1,0:T(8,128)(2,1)S(1)}, bf16[80,256]{1,0:T(8,128)(2,1)}, u32[]{:S(2)}) copy-start(bf16[80,256]{1,0:T(8,128)(2,1)} %constant.95.clone.late) | copy-start | bytes 122884
  23.8 10.8 %copy-start.14 = (f32[1,1,128]{2,1,0:T(1,128)S(1)}, f32[1,1,128]{2,1,0:T(1,128)}, u32[]{:S(2)}) copy-start(f32[1,1,128]{2,1,0:T(1,128)} %constant.98.clone.second) | copy-start | bytes 1540
  34.1 11.0 %collective-permute-start.4 = (bf16[80,1152]{1,0:T(8,128)(2,1)S(1)}, bf16[80,1152]{1,0:T(8,128)(2,1)S(1)}, u32[]{:S(2)}, u32[]{:S(2)}) collective-permute-start(bf16[80,1152]{1,0:T(8,128)(2,1)S(1)} %get-tuple-element.38), channel_id=1, source_target_pairs={{0,16},{1,17},{2,18},{3,19},{4,20},{5,21},{6,22},{7,23},{8,24},{9,... | collective-permute-start | bytes 552968 | tf_op jit(solution)/shard_map/ppermute | solution.py:601
  34.5 10.6 %collective-permute-start.5 = (bf16[80,1152]{1,0:T(8,128)(2,1)S(1)}, bf16[80,1152]{1,0:T(8,128)(2,1)S(1)}, u32[]{:S(2)}, u32[]{:S(2)}) collective-permute-start(bf16[80,1152]{1,0:T(8,128)(2,1)S(1)} %get-tuple-element.39), channel_id=1, source_target_pairs={{0,1},{1,0},{2,3},{3,2},{4,5},{5,4},{6,7},{7,6},{8,9},{9,8},{10,11... | collective-permute-start | bytes 552968 | tf_op jit(solution)/shard_map/ppermute | solution.py:602
